TPU v7x, 128 devices: a whole 4x4x4 slice. The times are simulated.
128 devices in a mesh: rows: 32 (over y, x_lo, z), protos: 4 (over x_hi, core).
Axes of the slice: x: 4 (x_hi: 2, x_lo: 2; x = x_hi * 2 + x_lo), y: 4, z: 4, core: 2. Of those that a mesh axis runs over, the one named last changes fastest.
Arguments:
- student: bfloat16 [16384, 256], P('rows'), may hold values from -256 to 256
- teacher: bfloat16 [16384, 256], P('rows'), may hold values from -256 to 256
- prototypes: bfloat16 [65536, 256], P('protos'), may hold values from -1 to 1
- masked: int32 [16384], P('rows'), may hold values from 0 to 1, as said below
Outputs:
- feature_grad: bfloat16 [16384, 256], P(('rows', 'protos'))
- proto_grad: bfloat16 [65536, 256], P(('protos', 'rows'))
Inputs may be any that keep to these rules, and one draw needn't show every extreme that they name: Rows whose index is a multiple of 16 are masked.
All inputs are finite; a program needn't handle non-finite values.
Results may differ from a plain program's by a relative error of at most 0.02.
Values may be sent and summed in bfloat16 or wider, within the bound.
No kernel may reach another device: no remote copies, remote signals or barrier semaphores. Data moves between devices by JAX's collectives and lax.ppermute only.
A program may use at most 256 MiB of HBM per device.

v0:
```python
import functools
import math

import jax
import jax.numpy as jnp
from jax import lax
from jax.experimental import pallas as pl
from jax.experimental.pallas import tpu as pltpu
from jax.sharding import Mesh
from jax.sharding import PartitionSpec as P

ITERS = 3
student_temp = 0.1
teacher_temp = 0.05

F32 = jnp.float32
BF16 = jnp.bfloat16
TILE = 512
LANES = 128
ALIGN = 16
FAR = 1e30
INFO = 16
BLOCKS = 8
END, TILES = 2 * BLOCKS, 2 * BLOCKS + 1
MIB = 2**20

NT = (((1,), (1,)), ((), ()))


def params(mib):
    return pltpu.CompilerParams(vmem_limit_bytes=mib * MIB)


def vmem():
    return pl.BlockSpec(memory_space=pltpu.VMEM)


def smem():
    return pl.BlockSpec(memory_space=pltpu.SMEM)


def hbm():
    return pl.BlockSpec(memory_space=pltpu.HBM)


def pinned(value):
    return pltpu.with_memory_space_constraint(value, pltpu.VMEM)


def streamed(value):
    return pltpu.with_memory_space_constraint(value, pltpu.HBM)


def own_protos(place, proto_ref, own_ref, sem):
    count = own_ref.shape[0]
    start = pl.multiple_of(place[3] * count, count)
    return pltpu.make_async_copy(proto_ref.at[pl.ds(start, count)], own_ref, sem)


def turn(own_ref):
    chunk = 512
    return jnp.concatenate(
        [jnp.transpose(own_ref[k : k + chunk]) for k in range(0, own_ref.shape[0], chunk)], axis=1
    )


def split(value):
    high = value.astype(BF16)
    low = (value - high.astype(F32)).astype(BF16)
    return high, low


def as_row(block):
    pieces = []
    for start in range(0, block.shape[0], LANES):
        part = block[start : start + LANES]
        total = part[:, :LANES]
        for lane in range(LANES, block.shape[1], LANES):
            total = total + part[:, lane : lane + LANES]
        pieces.append(jnp.sum(jnp.transpose(total), axis=0, keepdims=True))
    return jnp.concatenate(pieces, axis=1)


def compact_kernel(mask_ref, teach_ref, stud_ref, teach_out, stud_out):
    rows, width = teach_ref.shape
    mask = mask_ref[...]
    down = lax.broadcasted_iota(jnp.int32, (rows, rows), 0)
    along = lax.broadcasted_iota(jnp.int32, (rows, rows), 1)
    upper = jnp.where(down <= along, 1.0, 0.0).astype(BF16)
    many = jnp.broadcast_to(mask, (16, rows)).astype(BF16)
    rank = jnp.dot(many, upper, preferred_element_type=F32)[:1]
    place = jnp.where(mask > 0, rank - 1.0, -1.0)
    onehot = jnp.where(down.astype(F32) == place, 1.0, 0.0).astype(BF16)
    teach_out[:rows] = jnp.dot(onehot, teach_ref[...], preferred_element_type=F32).astype(BF16)
    stud_out[:rows] = jnp.dot(onehot, stud_ref[...], preferred_element_type=F32).astype(BF16)
    which = lax.broadcasted_iota(jnp.int32, (INFO, width), 0)
    info = jnp.zeros((INFO, width), F32)
    for piece in range(rows // width):
        info = jnp.where(which == piece, mask[:, piece * width : (piece + 1) * width], info)
    teach_out[rows:] = info.astype(BF16)
    stud_out[rows:] = info.astype(BF16)


def compact(mask_row, teacher, student):
    rows, width = teacher.shape
    return pl.pallas_call(
        compact_kernel,
        out_shape=(jax.ShapeDtypeStruct((rows + INFO, width), BF16),) * 2,
        in_specs=[vmem()] * 3,
        out_specs=(vmem(), vmem()),
        compiler_params=params(12),
        name="compact",
    )(mask_row, teacher, student)


def max_kernel(teach_ref, proto_ref, out_ref, turned_ref):
    rows = out_ref.shape[1]
    chunk = 512

    @pl.when(pl.program_id(0) == 0)
    def _():
        out_ref[...] = jnp.full_like(out_ref, -FAR)
        turned_ref[...] = jnp.transpose(teach_ref[:rows])

    best = out_ref[...]
    for start in range(0, proto_ref.shape[0], chunk):
        logit = jnp.dot(proto_ref[start : start + chunk], turned_ref[...], preferred_element_type=F32)
        best = jnp.maximum(best, jnp.max(logit, axis=0, keepdims=True))
    out_ref[...] = best


def row_max(feats, protos, rows, part, parts):
    count, width = protos.shape
    block = 2048
    steps = count // block // parts
    return pl.pallas_call(
        max_kernel,
        grid=(steps,),
        out_shape=jax.ShapeDtypeStruct((1, rows), F32),
        in_specs=[
            pl.BlockSpec(feats.shape, lambda i: (0, 0)),
            pl.BlockSpec((block, width), lambda i: (i + part * steps, 0)),
        ],
        out_specs=pl.BlockSpec((1, rows), lambda i: (0, 0)),
        scratch_shapes=[pltpu.VMEM((width, rows), BF16)],
        compiler_params=params(14),
        cost_estimate=cost(2 * count * width * rows // parts),
        name="row_max",
    )(feats, protos)


def soft_kernel(feat_ref, proto_ref, top_ref, sum_ref, turned_ref):
    chunk = 512

    @pl.when(pl.program_id(0) == 0)
    def _():
        top_ref[...] = jnp.full_like(top_ref, -FAR)
        sum_ref[...] = jnp.zeros_like(sum_ref)
        turned_ref[...] = jnp.transpose(feat_ref[: turned_ref.shape[1]])

    top = top_ref[...]
    total = sum_ref[...]
    for start in range(0, proto_ref.shape[0], chunk):
        logit = jnp.dot(proto_ref[start : start + chunk], turned_ref[...], preferred_element_type=F32)
        higher = jnp.maximum(top, jnp.max(logit, axis=0, keepdims=True))
        total = total * jnp.exp((top - higher) * (1 / student_temp)) + jnp.sum(
            jnp.exp((logit - higher) * (1 / student_temp)), axis=0, keepdims=True
        )
        top = higher
    top_ref[...] = top
    sum_ref[...] = total


def row_soft(feats, protos, rows, part, parts):
    count, width = protos.shape
    block = 2048
    steps = count // block // parts
    row = pl.BlockSpec((1, rows), lambda i: (0, 0))
    return pl.pallas_call(
        soft_kernel,
        grid=(steps,),
        out_shape=(jax.ShapeDtypeStruct((1, rows), F32),) * 2,
        in_specs=[
            pl.BlockSpec(feats.shape, lambda i: (0, 0)),
            pl.BlockSpec((block, width), lambda i: (i + part * steps, 0)),
        ],
        out_specs=(row, row),
        scratch_shapes=[pltpu.VMEM((width, rows), BF16)],
        compiler_params=params(14),
        cost_estimate=cost(3 * count * width * rows // parts),
        name="row_soft",
    )(feats, protos)


def cost(flops):
    return pl.CostEstimate(flops=flops, bytes_accessed=2**20, transcendentals=0)


def joined(place, refs, block, rows):
    piece, side = block // 2, block % 2
    mine = refs[piece][side, :rows]
    other = refs[4 + piece][side, :rows]
    first = place[1] == 0
    return jnp.where(first, mine, other), jnp.where(first, other, mine)


def true_block(place, block):
    return (place[0] ^ (block // 2)) * 2 + block % 2


def load_rows(place, meta, refs, rows_ref, rows):
    for true in range(BLOCKS):

        def fill(block, true=true):
            @pl.when(place[0] == (true // 2) ^ (block // 2))
            def _():
                offset = pl.multiple_of(meta[true], ALIGN)
                low, high = joined(place, refs, block, rows)
                rows_ref[pl.ds(offset, rows), :LANES] = low
                rows_ref[pl.ds(offset, rows), LANES:] = high

        for piece in range(4):
            fill(piece * 2 + true % 2)
    tail = pl.multiple_of(meta[END], ALIGN)
    rows_ref[pl.ds(tail, TILE), :] = jnp.zeros((TILE, rows_ref.shape[1]), BF16)


def load_line(meta, lines, out_ref, fill):
    rows = lines[0].shape[1]
    out_ref[...] = jnp.full_like(out_ref, fill)
    lane = lax.broadcasted_iota(jnp.int32, (1, rows + LANES), 1)
    for block in range(BLOCKS):
        offset = meta[block]
        shift = lax.rem(offset, LANES)
        base = pl.multiple_of(offset - shift, LANES)
        wide = jnp.concatenate([lines[block], jnp.zeros((1, LANES), F32)], axis=1)
        wide = pltpu.roll(jnp.broadcast_to(wide, (8, rows + LANES)), shift, axis=1)[:1]
        there = (lane >= shift) & (lane < shift + meta[BLOCKS + block])
        out_ref[:, pl.ds(base, rows + LANES)] = jnp.where(
            there, wide, out_ref[:, pl.ds(base, rows + LANES)]
        )


def place_blocks(place, meta, refs, rows):
    for block in range(BLOCKS):
        piece, side = block // 2, block % 2
        info = refs[piece][side, rows:].astype(F32) + refs[4 + piece][side, rows:].astype(F32)
        meta[BLOCKS + true_block(place, block)] = jnp.sum(info).astype(jnp.int32)
    end = jnp.int32(0)
    for block in range(BLOCKS):
        meta[block] = end
        end = end + (meta[BLOCKS + block] + (ALIGN - 1)) // ALIGN * ALIGN
    meta[END] = end
    meta[TILES] = (end + (TILE - 1)) // TILE


def expo_kernel(place, *refs):
    pieces, tops, proto_ref, refs = refs[:8], refs[8:12], refs[12], refs[13:]
    expo_ref, col_ref, valid_ref, meta, rows_ref, line_ref, acc_ref, own_ref, sem = refs
    rows = tops[0].shape[2]
    protos = own_protos(place, proto_ref, own_ref, sem)
    protos.start()
    place_blocks(place, meta, pieces, rows)
    load_rows(place, meta, pieces, rows_ref, rows)
    lines = []
    for block in range(BLOCKS):
        line = tops[0][block % 2]
        for piece in range(1, 4):
            line = jnp.where((place[0] ^ piece) == block // 2, tops[piece][block % 2], line)
        lines.append(line)
    load_line(meta, lines, line_ref, FAR)
    valid_ref[...] = jnp.where(line_ref[:, : valid_ref.shape[1]] < 0.5 * FAR, 1.0, 0.0)
    acc_ref[...] = jnp.zeros_like(acc_ref)
    protos.wait()
    chunk = 512
    count = own_ref.shape[0]

    @pl.loop(0, meta[TILES])
    def _(tile):
        start = pl.multiple_of(tile * TILE, TILE)
        feats = jnp.transpose(rows_ref[pl.ds(start, TILE), :])
        top = line_ref[:, pl.ds(start, TILE)]
        for k in range(0, count, chunk):
            logit = jnp.dot(own_ref[k : k + chunk], feats, preferred_element_type=F32)
            expo = jnp.exp((logit - top) * (1 / teacher_temp))
            expo_ref[tile, k : k + chunk] = expo.astype(BF16)
            acc_ref[k : k + chunk] += fold(expo)

    col_ref[:, :count] = as_row(acc_ref[...])
    col_ref[:, count:] = jnp.zeros((1, LANES), F32) + jnp.sum(valid_ref[...])


def fold(block):
    total = block[:, :LANES]
    for lane in range(LANES, block.shape[1], LANES):
        total = total + block[:, lane : lane + LANES]
    return total


def expo_step(place, pieces, tops, protos):
    rows = tops[0].shape[2]
    width = protos.shape[1]
    count = protos.shape[0] // BLOCKS
    total = BLOCKS * rows
    return pl.pallas_call(
        expo_kernel,
        out_shape=(
            pltpu.VMEM((total // TILE, count, TILE), BF16),
            jax.ShapeDtypeStruct((1, count + LANES), F32),
            jax.ShapeDtypeStruct((1, total), F32),
            jax.ShapeDtypeStruct((24,), jnp.int32),
        ),
        in_specs=[smem()] + [vmem()] * 12 + [hbm()],
        out_specs=(vmem(), vmem(), vmem(), smem()),
        scratch_shapes=[
            pltpu.VMEM((total + TILE, width), BF16),
            pltpu.VMEM((1, total + LANES), F32),
            pltpu.VMEM((count, LANES), F32),
            pltpu.VMEM((count, width), BF16),
            pltpu.SemaphoreType.DMA,
        ],
        compiler_params=params(26),
        cost_estimate=cost(count * total * width * 2),
        name="expo",
    )(place, *pieces, *tops, streamed(protos))


def col_scale_of(total_ref, count, proto_total):
    return 1.0 / (proto_total * total_ref[:, :count])


def two_rows(value):
    high, low = split(value)
    which = lax.broadcasted_iota(jnp.int32, (16, value.shape[1]), 0)
    return jnp.where(which == 0, high.astype(F32), jnp.where(which == 1, low.astype(F32), 0.0)).astype(BF16)


def row_kernel(proto_total, with_lse, place, meta, total_ref, expo_ref, *refs):
    out_ref = refs[-1]
    lhs = two_rows(col_scale_of(total_ref, expo_ref.shape[1], proto_total))
    out_ref[...] = jnp.zeros_like(out_ref)
    if with_lse:
        lse_ref = refs[0]
        rows = lse_ref.shape[1]
        start = pl.multiple_of(rows * BLOCKS + place[3] * rows, rows)
        out_ref[:, pl.ds(start, rows)] = lse_ref[...] * 0.25

    @pl.loop(0, meta[TILES])
    def _(tile):
        start = pl.multiple_of(tile * TILE, TILE)
        both = jnp.dot(lhs, expo_ref[tile], preferred_element_type=F32)
        out_ref[:, pl.ds(start, TILE)] = both[:1] + both[1:2]


def row_step(place, meta, total, expo, proto_total, lse=None):
    tiles, count, _ = expo.shape
    more = () if lse is None else (lse,)
    return pl.pallas_call(
        functools.partial(row_kernel, proto_total, lse is not None),
        out_shape=jax.ShapeDtypeStruct((1, (1 + len(more)) * tiles * TILE), F32),
        in_specs=[smem()] * 2 + [vmem()] * (2 + len(more)),
        out_specs=vmem(),
        compiler_params=params(10),
        cost_estimate=cost(count * tiles * TILE * 400),
        name="row_step",
    )(place, meta, total, pinned(expo), *more)


def weights_of(total_ref, valid_ref):
    valid = valid_ref[...]
    return valid / jnp.where(valid > 0, total_ref[:, : valid.shape[1]], 1.0)


def col_kernel(meta, total_ref, valid_ref, expo_ref, out_ref, line_ref, acc_ref):
    line_ref[...] = weights_of(total_ref, valid_ref)
    acc_ref[...] = jnp.zeros_like(acc_ref)
    chunk = 64

    @pl.loop(0, meta[TILES])
    def _(tile):
        start = pl.multiple_of(tile * TILE, TILE)
        weight = line_ref[:, pl.ds(start, TILE)]
        for k in range(0, acc_ref.shape[0], chunk):
            acc_ref[k : k + chunk] += fold(expo_ref[tile, k : k + chunk].astype(F32) * weight)

    out_ref[...] = as_row(acc_ref[...])


def col_step(meta, total, valid, expo):
    tiles, count, _ = expo.shape
    return pl.pallas_call(
        col_kernel,
        out_shape=jax.ShapeDtypeStruct((1, count), F32),
        in_specs=[smem()] + [vmem()] * 3,
        out_specs=vmem(),
        scratch_shapes=[pltpu.VMEM((1, tiles * TILE), F32), pltpu.VMEM((count, LANES), F32)],
        compiler_params=params(10),
        cost_estimate=cost(count * tiles * TILE * 400),
        name="col_step",
    )(meta, total, valid, pinned(expo))


def load_kernel(place, meta, *refs):
    pieces, proto_ref, refs = refs[:8], refs[8], refs[9:]
    out_ref, rank_ref, own_out, turned_ref, rows_ref, own_ref, sem = refs
    protos = own_protos(place, proto_ref, own_ref, sem)
    protos.start()
    rows = pieces[0].shape[1] - INFO
    load_rows(place, meta, pieces, rows_ref, rows)
    out_ref[...] = rows_ref[...]
    masks = [jnp.zeros((1, rows), F32)] * BLOCKS
    for block in range(BLOCKS):
        low, high = joined(place, pieces, block, rows + INFO)
        low, high = low[rows:].astype(F32), high[rows:].astype(F32)
        line = []
        for index in range(rows // (2 * LANES)):
            line += [low[index : index + 1], high[index : index + 1]]
        line = jnp.concatenate(line, axis=1)
        for true in range(block % 2, BLOCKS, 2):
            masks[true] = jnp.where(true_block(place, block) == true, line, masks[true])
    masks = jnp.concatenate(masks, axis=0)
    down = lax.broadcasted_iota(jnp.int32, (rows, rows), 0)
    along = lax.broadcasted_iota(jnp.int32, (rows, rows), 1)
    upper = jnp.where(down <= along, 1.0, 0.0).astype(BF16)
    many = jnp.concatenate([masks, masks], axis=0).astype(BF16)
    rank = jnp.dot(many, upper, preferred_element_type=F32)[:BLOCKS]
    rank_ref[...] = jnp.where(masks > 0, rank - 1.0, -1.0)
    protos.wait()
    own_out[...] = own_ref[...]
    turned_ref[...] = turn(own_ref)


def load_step(place, meta, pieces, protos):
    rows = pieces[0].shape[1] - INFO
    width = protos.shape[1]
    count = protos.shape[0] // BLOCKS
    total = BLOCKS * rows
    return pl.pallas_call(
        load_kernel,
        out_shape=(
            jax.ShapeDtypeStruct((total + TILE, width), BF16),
            jax.ShapeDtypeStruct((BLOCKS, rows), F32),
            jax.ShapeDtypeStruct((count, width), BF16),
            jax.ShapeDtypeStruct((width, count), BF16),
        ),
        in_specs=[smem()] * 2 + [vmem()] * 8 + [hbm()],
        out_specs=(vmem(),) * 4,
        scratch_shapes=[
            pltpu.VMEM((total + TILE, width), BF16),
            pltpu.VMEM((count, width), BF16),
            pltpu.SemaphoreType.DMA,
        ],
        compiler_params=params(18),
        cost_estimate=cost(2**31),
        name="load_student",
    )(place, meta, *pieces, streamed(protos))


def student_kernel(part, place, meta, rows_ref, all_ref, own_ref, turned_ref, *refs):
    if part == 1:
        sums_in, refs = refs[0], refs[1:]
    grads, (sums_out, acc_ref, line_ref) = refs[:2], refs[2:]
    total = sums_out.shape[0]
    rows = total // BLOCKS
    load_line(
        meta, [all_ref[:, total + block * rows : total + (block + 1) * rows] for block in range(BLOCKS)], line_ref, FAR
    )
    acc_ref[...] = jnp.zeros_like(acc_ref)
    sums_out[...] = jnp.zeros_like(sums_out)
    chunk = grads[0].shape[0]

    @pl.loop(0, meta[TILES])
    def _(tile):
        start = pl.multiple_of(tile * TILE, TILE)
        feats = rows_ref[pl.ds(start, TILE), :]
        across = jnp.transpose(feats)
        lse = line_ref[:, pl.ds(start, TILE)]
        turned = jnp.zeros((turned_ref.shape[0], TILE), F32)
        for piece in range(2):
            k = pl.multiple_of((place[2] ^ (2 * part + piece)) * chunk, chunk)
            logit = jnp.dot(own_ref[pl.ds(k, chunk), :], across, preferred_element_type=F32)
            probs = jnp.exp(logit * (1 / student_temp) - lse).astype(BF16)
            acc_ref[piece] += jnp.dot(probs, feats, preferred_element_type=F32)
            turned += jnp.dot(turned_ref[:, pl.ds(k, chunk)], probs, preferred_element_type=F32)
        sums = jnp.transpose(turned)
        if part == 1:
            sums = sums + sums_in[pl.ds(start, TILE), :].astype(F32)
        sums_out[pl.ds(start, TILE), :] = sums.astype(BF16)

    for piece in range(2):
        grads[piece][...] = acc_ref[piece].astype(BF16)


def student_step(part, place, meta, rows, line, own, turned, *sums):
    width, count = turned.shape
    total = line.shape[1] // 2
    outs = (jax.ShapeDtypeStruct((count // 4, width), BF16),) * 2 + (jax.ShapeDtypeStruct((total, width), BF16),)
    return pl.pallas_call(
        functools.partial(student_kernel, part),
        out_shape=outs,
        in_specs=[smem()] * 2 + [vmem()] * (4 + len(sums)),
        out_specs=(vmem(),) * len(outs),
        scratch_shapes=[pltpu.VMEM((2, count // 4, width), F32), pltpu.VMEM((1, total + LANES), F32)],
        compiler_params=params(20),
        cost_estimate=cost(count * total * width * 3),
        name="student",
    )(place, meta, rows, line, own, turned, *sums)


def scaled_rows(feats, factor):
    parts = []
    for start in range(0, feats.shape[0], LANES):
        column = jnp.transpose(jnp.broadcast_to(factor[:, start : start + LANES], (LANES, LANES)))
        part = feats[start : start + LANES].astype(F32)
        parts.append(
            jnp.concatenate([part[:, d : d + LANES] * column for d in range(0, part.shape[1], LANES)], axis=1)
        )
    return jnp.concatenate(parts, axis=0)


def feature_kernel(proto_total, meta, total_ref, expo_ref, turned_ref, sums_ref):
    scale = col_scale_of(total_ref, expo_ref.shape[1], proto_total)
    sums_ref[...] = jnp.zeros_like(sums_ref)
    scaled = (turned_ref[...].astype(F32) * scale).astype(BF16)

    @pl.loop(0, meta[TILES])
    def _(tile):
        start = pl.multiple_of(tile * TILE, TILE)
        turned = jnp.dot(scaled, expo_ref[tile], preferred_element_type=F32)
        sums_ref[pl.ds(start, TILE), :] = jnp.transpose(turned).astype(BF16)


def feature_step(meta, total, expo, turned, proto_total):
    tiles, count, _ = expo.shape
    width = turned.shape[0]
    return pl.pallas_call(
        functools.partial(feature_kernel, proto_total),
        out_shape=jax.ShapeDtypeStruct((tiles * TILE, width), BF16),
        in_specs=[smem()] + [vmem()] * 3,
        out_specs=vmem(),
        compiler_params=params(14),
        cost_estimate=cost(count * tiles * TILE * width * 2),
        name="feature_step",
    )(meta, total, pinned(expo), turned)


def join_kernel(place, meta, total_ref, valid_ref, rank_ref, stud_ref, plan_ref, keep_ref, give_ref, weight_ref, sums_ref):
    weight_ref[...] = weights_of(total_ref, valid_ref)

    @pl.loop(0, meta[TILES])
    def _(tile):
        start = pl.multiple_of(tile * TILE, TILE)
        plan = scaled_rows(plan_ref[pl.ds(start, TILE), :], weight_ref[:, pl.ds(start, TILE)])
        sums_ref[pl.ds(start, TILE), :] = (stud_ref[pl.ds(start, TILE), :].astype(F32) - plan).astype(BF16)

    tail = pl.multiple_of(meta[TILES] * TILE, TILE)
    rows = rank_ref.shape[1]
    sums_ref[pl.ds(tail, rows), :] = jnp.zeros((rows, sums_ref.shape[1]), BF16)
    along = lax.broadcasted_iota(jnp.int32, (LANES, rows), 1).astype(F32)
    first = place[1] == 0
    for block in range(BLOCKS):
        offset = pl.multiple_of(meta[block], ALIGN)
        sums = sums_ref[pl.ds(offset, rows), :]
        pieces = []
        for start in range(0, rows, LANES):
            column = jnp.transpose(jnp.broadcast_to(rank_ref[block : block + 1, start : start + LANES], (LANES, LANES)))
            column = jnp.concatenate([column] * (rows // LANES), axis=1)
            onehot = jnp.where(column == along, 1.0, 0.0).astype(BF16)
            pieces.append(jnp.dot(onehot, sums, preferred_element_type=F32).astype(BF16))
        for half in range(2):
            low, high = pieces[2 * half], pieces[2 * half + 1]
            keep_ref[2 * block + half] = jnp.where(first, low, high)
            give_ref[2 * block + half] = jnp.where(first, high, low)


def join_step(place, meta, total, valid, rank, stud, plan):
    all_rows, width = stud.shape
    out = jax.ShapeDtypeStruct((2 * BLOCKS, LANES, width), BF16)
    return pl.pallas_call(
        join_kernel,
        out_shape=(out, out),
        in_specs=[smem()] * 2 + [vmem()] * 5,
        out_specs=(vmem(),) * 2,
        scratch_shapes=[
            pltpu.VMEM((1, all_rows), F32),
            pltpu.VMEM((all_rows + rank.shape[1], width), BF16),
        ],
        compiler_params=params(14),
        cost_estimate=cost(2**31),
        name="join_step",
    )(place, meta, total, valid, rank, stud, plan)


def grad_kernel(proto_total, place, meta, total_ref, valid_ref, rows_ref, expo_ref, col_ref, *refs):
    studs, grads, (weight_ref, acc_ref) = refs[:4], refs[4:8], refs[8:]
    weight_ref[...] = weights_of(total_ref, valid_ref)
    acc_ref[...] = jnp.zeros_like(acc_ref)
    chunk = 512

    @pl.loop(0, meta[TILES])
    def _(tile):
        start = pl.multiple_of(tile * TILE, TILE)
        scaled = scaled_rows(rows_ref[pl.ds(start, TILE), :], weight_ref[:, pl.ds(start, TILE)]).astype(BF16)
        for k in range(0, acc_ref.shape[0], chunk):
            acc_ref[k : k + chunk] += jnp.dot(
                expo_ref[tile, k : k + chunk], scaled, preferred_element_type=F32
            )

    rows = grads[0].shape[0]
    for piece in range(len(grads)):
        start = pl.multiple_of((place[2] ^ piece) * rows, rows)
        scale = 1.0 / (proto_total * col_ref[:, pl.ds(start, rows)])
        plan = scaled_rows(acc_ref[pl.ds(start, rows), :], scale)
        grads[piece][...] = (studs[piece][...].astype(F32) - plan).astype(BF16)


def grad_step(place, meta, total, valid, rows, expo, col, studs, proto_total):
    tiles, count, _ = expo.shape
    width = rows.shape[1]
    return pl.pallas_call(
        functools.partial(grad_kernel, proto_total),
        out_shape=(jax.ShapeDtypeStruct((count // 4, width), BF16),) * 4,
        in_specs=[smem()] * 2 + [vmem()] * 9,
        out_specs=(vmem(),) * 4,
        scratch_shapes=[pltpu.VMEM((1, tiles * TILE), F32), pltpu.VMEM((count, width), F32)],
        compiler_params=params(18),
        cost_estimate=cost(count * tiles * TILE * width * 2),
        name="grad_step",
    )(place, meta, total, valid, rows, pinned(expo), col, *studs)


def swap(value, axis):
    return lax.ppermute(value, axis, [(0, 1), (1, 0)])


def from_xor(value, axis, mask):
    return lax.ppermute(value, axis, [(i, i ^ mask) for i in range(4)])


def exchange(many, axes):
    return lax.all_to_all(many, axes, 0, 0, tiled=True)


def spread(value, axes, size):
    return exchange(jnp.broadcast_to(value[None], (size,) + value.shape), axes)


def tie(*values):
    return lax.optimization_barrier(values)


def pair_of(half, low):
    return jnp.stack(choose(low, half, swap(half, "xl")))


def gather_along(pair):
    return [pair] + [from_xor(pair, "y", mask) for mask in (1, 3, 2)]


def ordered(pieces):
    own, one, three, two = pieces
    return [own, one, two, three]


def scatter_protos(pieces):
    return [pieces[0]] + [from_xor(pieces[mask], "z", mask) for mask in (1, 3, 2)]


def choose(first, one, two):
    return jnp.where(first, one, two), jnp.where(first, two, one)


RINGS = {"x": (("xl", "xh"), (1, 2, 3)), "y": ("y", (2, 1, 3)), "z": ("z", (2, 1, 3))}


def ring(value, name):
    axes, masks = RINGS[name]
    return [lax.ppermute(value, axes, [(i, i ^ mask) for i in range(4)]) for mask in masks]


def total_of(value, got):
    return value + got[0] + got[1] + got[2]


def merged(one, two):
    high = jnp.maximum(one[0], two[0])
    return high, one[1] * jnp.exp((one[0] - high) / student_temp) + two[1] * jnp.exp(
        (two[0] - high) / student_temp
    )


def local(student, teacher, prototypes, masked):
    rows, width = student.shape
    y, xl, z = lax.axis_index("y"), lax.axis_index("xl"), lax.axis_index("z")
    core = lax.axis_index("c")
    block_id = y * 2 + xl
    count = prototypes.shape[0] // BLOCKS
    proto_total = prototypes.shape[0] * 4
    place = jnp.stack([y, core, z, block_id]).astype(jnp.int32)
    low_x, low_c = xl == 0, core == 0
    table = streamed(prototypes)

    teach, stud = compact(masked.astype(F32)[None], streamed(teacher), streamed(student))
    t_half, _ = choose(low_c, teach[:, :LANES], teach[:, LANES:])
    s_half, _ = choose(low_c, stud[:, :LANES], stud[:, LANES:])
    t_half, s_half, teach, stud = tie(t_half, s_half, teach, stud)
    t_beside, s_beside = swap(t_half, "xl"), swap(s_half, "xl")
    top = row_max(teach, table, rows, 0, 1)
    t_beside, s_beside, top, stud = tie(t_beside, s_beside, top, stud)
    t_pair = jnp.stack(choose(low_x, t_half, t_beside))
    s_pair = jnp.stack(choose(low_x, s_half, s_beside))
    top = jnp.maximum(top, swap(top, "c"))

    t_pair, s_pair, top, stud = tie(t_pair, s_pair, top, stud)
    mine = gather_along(t_pair)
    far = swap(top, "xh")
    soft = row_soft(stud, table, rows, 0, 2)
    mine, far, soft, top, stud, s_pair = tie(mine, far, soft, top, stud, s_pair)

    top = jnp.maximum(top, far)
    other = [swap(piece, "c") for piece in mine]
    beside = swap(top, "xl")
    mine, other, top, beside, soft, stud, s_pair = tie(mine, other, top, beside, soft, stud, s_pair)

    tops = gather_along(jnp.stack(choose(low_x, top, beside)))
    soft_two = row_soft(stud, table, rows, 1, 2)
    mine, other, tops, soft, soft_two, s_pair, place = tie(mine, other, tops, soft, soft_two, s_pair, place)

    s_mine = gather_along(s_pair)
    soft = jnp.stack(merged(soft, soft_two))
    soft = jnp.stack(merged(soft, swap(soft, "c")))
    soft_far = swap(soft, "xh")
    expo, col, valid, meta = expo_step(place, ordered(mine) + ordered(other), ordered(tops), prototypes)
    s_mine, col, soft, soft_far = tie(s_mine, col, soft, soft_far)

    got = ring(col, "z")
    soft = merged(soft, soft_far)
    got, s_mine, col, soft = tie(got, s_mine, col, soft)
    col = total_of(col, got)
    mask_total = col[0, count]
    row = row_step(place, meta, col, expo, proto_total, soft[0] / student_temp + jnp.log(soft[1]))
    row = row + swap(row, "c")
    row, s_mine = tie(row, s_mine)
    got = ring(row, "x")
    s_other = [swap(piece, "c") for piece in s_mine]
    row, got, s_mine, s_other = tie(row, got, s_mine, s_other)
    row = total_of(row, got)
    got = ring(row, "y")
    loaded = load_step(place, meta, ordered(s_mine) + ordered(s_other), prototypes)
    row, got, loaded = tie(row, got, loaded)
    stud_rows, rank, protos, turned = loaded
    row = total_of(row, got)
    col = col_step(meta, row, valid, expo)

    col, stud_rows, line = tie(col, stud_rows, row)
    got = ring(col, "z")
    one = student_step(0, place, meta, stud_rows, line, protos, turned)
    col, got, one = tie(col, got, one)
    row = row_step(place, meta, total_of(col, got), expo, proto_total)
    row = row + swap(row, "c")
    row, one = tie(row, one)
    got = ring(row, "x")
    two = student_step(1, place, meta, stud_rows, line, protos, turned, one[2])
    row, got, two = tie(row, got, two)
    row = total_of(row, got)
    got = ring(row, "y")
    row, got = tie(row, got)
    col = col_step(meta, total_of(row, got), valid, expo)

    got = ring(col, "z")
    col, got = tie(col, got)
    col = total_of(col, got)
    row = row_step(place, meta, col, expo, proto_total)
    row = row + swap(row, "c")
    row, turned = tie(row, turned)
    got = ring(row, "x")
    plan_sums = feature_step(meta, col, expo, turned, proto_total)
    row, got, plan_sums = tie(row, got, plan_sums)
    row = total_of(row, got)
    got = ring(row, "y")
    row, got = tie(row, got)
    row = total_of(row, got)

    keep, give = join_step(place, meta, row, valid, rank, two[2], plan_sums)
    keep, give, row = tie(keep, give, row)
    got = swap(give, "c")
    grads = grad_step(
        place, meta, row, valid, stud_rows, expo, col, tuple(one[:2]) + tuple(two[:2]), proto_total
    )
    keep, got, grads = tie(keep, got, grads)
    keep = (keep.astype(F32) + got.astype(F32)).astype(BF16)
    parts = exchange(keep, ("y", "xl", "xh"))
    pieces = scatter_protos(grads)
    parts, pieces = tie(parts, pieces)
    feature_grad = (
        jnp.sum(parts.astype(F32), axis=0) * (math.sqrt(proto_total) / student_temp)
    ).astype(BF16)
    proto_grad = (
        sum(piece.astype(F32) for piece in pieces) * (proto_total / jnp.sqrt(mask_total))
    ).astype(BF16)
    return feature_grad, proto_grad


def solution(mesh):
    fine = Mesh(mesh.devices.reshape(4, 2, 4, 2, 2), ("y", "xl", "z", "xh", "c"))
    rows, protos = ("y", "xl", "z"), ("xh", "c")
    in_specs = (P(rows, None), P(rows, None), P(protos, None), P(rows))
    out_specs = (P(rows + protos, None), P(protos + rows, None))
    return jax.shard_map(local, mesh=fine, in_specs=in_specs, out_specs=out_specs, check_vma=False)
```

profile of v0, /device:TPU:0, one launch (start us, length us, event | category | flops | bytes accessed | tf_op | source)
XLA Modules:
  0.0 203.7 jit_solution(10356059512850189731)
XLA Ops:
  5.1 8.9 %row_max.1 = f32[1,512]{1,0:T(1,128)S(1)} custom-call(bf16[528,256]{1,0:T(8,128)(2,1)S(1)} %get-tuple-element.182.teach_ref, bf16[16384,256]{1,0:T(8,128)(2,1)} %refs_8_.1), custom_call_target="tpu_custom_call" | custom-call | flops 4294967296 | bytes 1048576 | tf_op jit(solution)/shard_map/row_max/pallas_call | solution.py:136
  15.3 3.3 %collective-permute-start.5 = (bf16[2,528,128]{2,1,0:T(8,128)(2,1)S(1)}, bf16[2,528,128]{2,1,0:T(8,128)(2,1)S(1)}, u32[]{:S(2)}, u32[]{:S(2)}) collective-permute-start(bf16[2,528,128]{2,1,0:T(8,128)(2,1)S(1)} %pad_maximum_fusion.refs_0_), channel_id=1, source_target_pairs={{0,64},{32,96},{64,0},{96,32},{1,65},{33,97},{65,1},{97,33},{2,66}... | collective-permute-start | bytes 811016 | tf_op jit(solution)/shard_map/ppermute | solution.py:637
  19.7 3.0 %collective-permute-start.6 = (f32[1,512]{1,0:T(1,128)S(1)}, f32[1,512]{1,0:T(1,128)S(1)}, u32[]{:S(2)}, u32[]{:S(2)}) collective-permute-start(f32[1,512]{1,0:T(1,128)S(1)} %max.27), channel_id=1, source_target_pairs={{0,2},{2,0},{1,3},{3,1},{4,6},{6,4},{5,7},{7,5},{8,10},{10,8},{9,1... | collective-permute-start | bytes 6152 | tf_op jit(solution)/shard_map/ppermute | solution.py:633
  22.7 7.6 %row_soft.2 = (f32[1,512]{1,0:T(1,128)S(1)}, f32[1,512]{1,0:T(1,128)S(1)}) custom-call(bf16[528,256]{1,0:T(8,128)(2,1)S(1)} %get-tuple-element.216.feat_ref, bf16[16384,256]{1,0:T(8,128)(2,1)} %refs_8_.1), custom_call_target="tpu_custom_call" | custom-call | flops 3221225472 | bytes 1048576 | tf_op jit(solution)/shard_map/row_soft/pallas_call | solution.py:179
  36.3 2.5 %collective-permute-start.14 = (f32[2,1,512]{2,1,0:T(1,128)S(1)}, f32[2,1,512]{2,1,0:T(1,128)S(1)}, u32[]{:S(2)}, u32[]{:S(2)}) collective-permute-start(f32[2,1,512]{2,1,0:T(1,128)S(1)} %pad_maximum_fusion.2.refs_8_), channel_id=1, source_target_pairs={{0,64},{32,96},{64,0},{96,32},{1,65},{33,97},{65,1},{97,33},{2,66}... | collective-permute-start | bytes 12296 | tf_op jit(solution)/shard_map/ppermute | solution.py:637
  40.4 7.6 %row_soft.3 = (f32[1,512]{1,0:T(1,128)S(1)}, f32[1,512]{1,0:T(1,128)S(1)}) custom-call(bf16[528,256]{1,0:T(8,128)(2,1)S(1)} %get-tuple-element.216.feat_ref, bf16[16384,256]{1,0:T(8,128)(2,1)} %refs_8_.1), custom_call_target="tpu_custom_call" | custom-call | flops 3221225472 | bytes 1048576 | tf_op jit(solution)/shard_map/row_soft/pallas_call | solution.py:179
  48.2 3.1 %collective-permute-start.17 = (bf16[2,528,128]{2,1,0:T(8,128)(2,1)S(1)}, bf16[2,528,128]{2,1,0:T(8,128)(2,1)S(1)}, u32[]{:S(2)}, u32[]{:S(2)}) collective-permute-start(bf16[2,528,128]{2,1,0:T(8,128)(2,1)S(1)} %pad_maximum_fusion.1.refs_0_), channel_id=1, source_target_pairs={{0,64},{32,96},{64,0},{96,32},{1,65},{33,97},{65,1},{97,33},{2,66}... | collective-permute-start | bytes 811016 | tf_op jit(solution)/shard_map/ppermute | solution.py:637
  53.0 3.1 %collective-permute-start.19 = (f32[2,1,512]{2,1,0:T(1,128)S(1)}, f32[2,1,512]{2,1,0:T(1,128)S(1)}, u32[]{:S(2)}, u32[]{:S(2)}) collective-permute-start(f32[2,1,512]{2,1,0:T(1,128)S(1)} %pad_maximum_fusion.4), channel_id=1, source_target_pairs={{0,2},{2,0},{1,3},{3,1},{4,6},{6,4},{5,7},{7,5},{8,10},{10,8},{9,1... | collective-permute-start | bytes 12296 | tf_op jit(solution)/shard_map/ppermute | solution.py:633
  56.1 7.4 %expo.1 = (bf16[8,2048,512]{2,1,0:T(8,128)(2,1)S(1)}, f32[1,2176]{1,0:T(1,128)S(1)}, f32[1,4096]{1,0:T(1,128)S(1)}, s32[24]{0:T(128)S(1)}) custom-call(s32[4]{0:T(128)S(1)} %pad_add_fusion.place, bf16[2,528,128]{2,1,0:T(8,128)(2,1)S(1)} %pad_maximum_fusion.refs_0_, bf16[2,528,128]{2,1,0:T(8,128)(2,1)S(1)} %collective-permute-done.3.refs_1_, ...), custom_call_target="tpu_custom_call" | custom-call | flops 4294967296 | bytes 1048576 | tf_op jit(solution)/shard_map/expo/pallas_call | solution.py:305
  64.4 4.0 %collective-permute-start.22 = (f32[1,2176]{1,0:T(1,128)S(1)}, f32[1,2176]{1,0:T(1,128)S(1)}, u32[]{:S(2)}, u32[]{:S(2)}) collective-permute-start(f32[1,2176]{1,0:T(1,128)S(1)} %get-tuple-element.247), channel_id=1, source_target_pairs={{0,12},{4,8},{8,4},{12,0},{1,13},{5,9},{9,5},{13,1},{2,14},{6,10},... | collective-permute-start | bytes 26120 | tf_op jit(solution)/shard_map/ppermute | solution.py:678
  73.6 2.5 %row_step.3 = f32[1,8192]{1,0:T(1,128)S(1)} custom-call(s32[4]{0:T(128)S(1)} %pad_add_fusion.place, s32[24]{0:T(128)S(1)} %get-tuple-element.233.meta, f32[1,2176]{1,0:T(1,128)S(1)} %add_add_fusion.6.total_ref, bf16[8,2048,512]{2,1,0:T(8,128)(2,1)S(1)} %get-tuple-element.251.expo_ref, f32[1,512]{1,0:T(1,128)S(1)} %log_add_fusion.refs_0_), custom_call_target="tpu_custom_call" | custom-call | flops 3355443200 | bytes 1048576 | tf_op jit(solution)/shard_map/row_step/pallas_call | solution.py:358
  78.5 2.8 %collective-permute-start.26 = (f32[1,8192]{1,0:T(1,128)S(1)}, f32[1,8192]{1,0:T(1,128)S(1)}, u32[]{:S(2)}, u32[]{:S(2)}) collective-permute-start(f32[1,8192]{1,0:T(1,128)S(1)} %add.133), channel_id=1, source_target_pairs={{0,18},{2,16},{16,2},{18,0},{1,19},{3,17},{17,3},{19,1},{4,22},{6,... | collective-permute-start | bytes 98312 | tf_op jit(solution)/shard_map/ppermute | solution.py:678
  81.3 2.3 %collective-permute-done.26 = f32[1,8192]{1,0:T(1,128)S(1)} collective-permute-done((f32[1,8192]{1,0:T(1,128)S(1)}, f32[1,8192]{1,0:T(1,128)S(1)}, u32[]{:S(2)}, u32[]{:S(2)}) %collective-permute-start.26) | collective-permute-done | bytes 32800 | tf_op jit(solution)/shard_map/ppermute | solution.py:678
  83.9 3.6 %collective-permute-done.25 = f32[1,8192]{1,0:T(1,128)S(1)} collective-permute-done((f32[1,8192]{1,0:T(1,128)S(1)}, f32[1,8192]{1,0:T(1,128)S(1)}, u32[]{:S(2)}, u32[]{:S(2)}) %collective-permute-start.25) | collective-permute-done | bytes 32800 | tf_op jit(solution)/shard_map/ppermute | solution.py:678
  89.8 3.2 %collective-permute-done.24 = f32[1,8192]{1,0:T(1,128)S(1)} collective-permute-done((f32[1,8192]{1,0:T(1,128)S(1)}, f32[1,8192]{1,0:T(1,128)S(1)}, u32[]{:S(2)}, u32[]{:S(2)}) %collective-permute-start.24) | collective-permute-done | bytes 32800 | tf_op jit(solution)/shard_map/ppermute | solution.py:678
  101.3 3.2 %col_step.2 = f32[1,2048]{1,0:T(1,128)S(1)} custom-call(s32[24]{0:T(128)S(1)} %get-tuple-element.233.meta, f32[1,8192]{1,0:T(1,128)S(1)} %add_add_fusion.total_ref.all_ref, f32[1,4096]{1,0:T(1,128)S(1)} %get-tuple-element.283.valid_ref, bf16[8,2048,512]{2,1,0:T(8,128)(2,1)S(1)} %get-tuple-element.251.expo_ref), custom_call_target="tpu_custom_call" | custom-call | flops 3355443200 | bytes 1048576 | tf_op jit(solution)/shard_map/col_step/pallas_call | solution.py:391
  106.6 2.6 %collective-permute-start.34 = (f32[1,2048]{1,0:T(1,128)S(1)}, f32[1,2048]{1,0:T(1,128)S(1)}, u32[]{:S(2)}, u32[]{:S(2)}) collective-permute-start(f32[1,2048]{1,0:T(1,128)S(1)} %col_step.2), channel_id=1, source_target_pairs={{0,8},{4,12},{8,0},{12,4},{1,9},{5,13},{9,1},{13,5},{2,10},{6,14},... | collective-permute-start | bytes 24584 | tf_op jit(solution)/shard_map/ppermute | solution.py:678
  109.2 6.5 %student.2 = (bf16[512,256]{1,0:T(8,128)(2,1)S(1)}, bf16[512,256]{1,0:T(8,128)(2,1)S(1)}, bf16[4096,256]{1,0:T(8,128)(2,1)S(1)}) custom-call(s32[4]{0:T(128)S(1)} %pad_add_fusion.place, s32[24]{0:T(128)S(1)} %get-tuple-element.233.meta, bf16[4608,256]{1,0:T(8,128)(2,1)S(1)} %get-tuple-element.286.rows_ref, f32[1,8192]{1,0:T(1,128)S(1)} %add_add_fusion.total_ref.all_ref, ...), custom_call_target="tpu_custom_call" | custom-call | flops 6442450944 | bytes 1048576 | tf_op jit(solution)/shard_map/student/pallas_call | solution.py:498
  115.8 2.5 %row_step.4 = f32[1,4096]{1,0:T(1,128)S(1)} custom-call(s32[4]{0:T(128)S(1)} %pad_add_fusion.place, s32[24]{0:T(128)S(1)} %get-tuple-element.233.meta, f32[1,2048]{1,0:T(1,128)S(1)} %add_add_fusion.8.total_ref, bf16[8,2048,512]{2,1,0:T(8,128)(2,1)S(1)} %get-tuple-element.251.expo_ref), custom_call_target="tpu_custom_call" | custom-call | flops 3355443200 | bytes 1048576 | tf_op jit(solution)/shard_map/row_step/pallas_call | solution.py:358
  119.5 3.1 %collective-permute-start.40 = (f32[1,4096]{1,0:T(1,128)S(1)}, f32[1,4096]{1,0:T(1,128)S(1)}, u32[]{:S(2)}, u32[]{:S(2)}) collective-permute-start(f32[1,4096]{1,0:T(1,128)S(1)} %add.143), channel_id=1, source_target_pairs={{0,18},{2,16},{16,2},{18,0},{1,19},{3,17},{17,3},{19,1},{4,22},{6,... | collective-permute-start | bytes 49160 | tf_op jit(solution)/shard_map/ppermute | solution.py:678
  124.3 6.5 %student.3 = (bf16[512,256]{1,0:T(8,128)(2,1)S(1)}, bf16[512,256]{1,0:T(8,128)(2,1)S(1)}, bf16[4096,256]{1,0:T(8,128)(2,1)S(1)}) custom-call(s32[4]{0:T(128)S(1)} %pad_add_fusion.place, s32[24]{0:T(128)S(1)} %get-tuple-element.233.meta, bf16[4608,256]{1,0:T(8,128)(2,1)S(1)} %get-tuple-element.286.rows_ref, f32[1,8192]{1,0:T(1,128)S(1)} %add_add_fusion.total_ref.all_ref, ...), custom_call_target="tpu_custom_call" | custom-call | flops 6442450944 | bytes 1048576 | tf_op jit(solution)/shard_map/student/pallas_call | solution.py:498
  133.0 2.7 %collective-permute-start.41 = (f32[1,4096]{1,0:T(1,128)S(1)}, f32[1,4096]{1,0:T(1,128)S(1)}, u32[]{:S(2)}, u32[]{:S(2)}) collective-permute-start(f32[1,4096]{1,0:T(1,128)S(1)} %add_add_fusion.5), channel_id=1, source_target_pairs={{0,64},{32,96},{64,0},{96,32},{1,65},{33,97},{65,1},{97,33},{2,66}... | collective-permute-start | bytes 49160 | tf_op jit(solution)/shard_map/ppermute | solution.py:678
  138.2 3.2 %col_step.3 = f32[1,2048]{1,0:T(1,128)S(1)} custom-call(s32[24]{0:T(128)S(1)} %get-tuple-element.233.meta, f32[1,4096]{1,0:T(1,128)S(1)} %add_add_fusion.4.total_ref, f32[1,4096]{1,0:T(1,128)S(1)} %get-tuple-element.283.valid_ref, bf16[8,2048,512]{2,1,0:T(8,128)(2,1)S(1)} %get-tuple-element.251.expo_ref), custom_call_target="tpu_custom_call" | custom-call | flops 3355443200 | bytes 1048576 | tf_op jit(solution)/shard_map/col_step/pallas_call | solution.py:391
  142.8 3.4 %collective-permute-start.44 = (f32[1,2048]{1,0:T(1,128)S(1)}, f32[1,2048]{1,0:T(1,128)S(1)}, u32[]{:S(2)}, u32[]{:S(2)}) collective-permute-start(f32[1,2048]{1,0:T(1,128)S(1)} %col_step.3), channel_id=1, source_target_pairs={{0,8},{4,12},{8,0},{12,4},{1,9},{5,13},{9,1},{13,5},{2,10},{6,14},... | collective-permute-start | bytes 24584 | tf_op jit(solution)/shard_map/ppermute | solution.py:678
  148.0 2.5 %row_step.5 = f32[1,4096]{1,0:T(1,128)S(1)} custom-call(s32[4]{0:T(128)S(1)} %pad_add_fusion.place, s32[24]{0:T(128)S(1)} %get-tuple-element.233.meta, f32[1,2048]{1,0:T(1,128)S(1)} %add_add_fusion.7.total_ref.col_ref, bf16[8,2048,512]{2,1,0:T(8,128)(2,1)S(1)} %get-tuple-element.251.expo_ref), custom_call_target="tpu_custom_call" | custom-call | flops 3355443200 | bytes 1048576 | tf_op jit(solution)/shard_map/row_step/pallas_call | solution.py:358
  151.7 3.1 %collective-permute-start.50 = (f32[1,4096]{1,0:T(1,128)S(1)}, f32[1,4096]{1,0:T(1,128)S(1)}, u32[]{:S(2)}, u32[]{:S(2)}) collective-permute-start(f32[1,4096]{1,0:T(1,128)S(1)} %add.153), channel_id=1, source_target_pairs={{0,18},{2,16},{16,2},{18,0},{1,19},{3,17},{17,3},{19,1},{4,22},{6,... | collective-permute-start | bytes 49160 | tf_op jit(solution)/shard_map/ppermute | solution.py:678
  156.5 5.1 %feature_step.1.plan_ref = bf16[4096,256]{1,0:T(8,128)(2,1)S(1)} custom-call(s32[24]{0:T(128)S(1)} %get-tuple-element.233.meta, f32[1,2048]{1,0:T(1,128)S(1)} %add_add_fusion.7.total_ref.col_ref, bf16[8,2048,512]{2,1,0:T(8,128)(2,1)S(1)} %get-tuple-element.251.expo_ref, bf16[256,2048]{1,0:T(8,128)(2,1)S(1)} %get-tuple-element.318.turned_ref), custom_call_target="tpu_custom_call" | custom-call | flops 4294967296 | bytes 1048576 | tf_op jit(solution)/shard_map/feature_step/pallas_call | solution.py:536
  169.7 2.6 %join_step.1 = (bf16[16,128,256]{2,1,0:T(8,128)(2,1)S(1)}, bf16[16,128,256]{2,1,0:T(8,128)(2,1)S(1)}) custom-call(s32[4]{0:T(128)S(1)} %pad_add_fusion.place, s32[24]{0:T(128)S(1)} %get-tuple-element.233.meta, f32[1,4096]{1,0:T(1,128)S(1)} %add_add_fusion.2.total_ref, f32[1,4096]{1,0:T(1,128)S(1)} %get-tuple-element.283.valid_ref, ...), custom_call_target="tpu_custom_call" | custom-call | flops 2147483648 | bytes 1048576 | tf_op jit(solution)/shard_map/join_step/pallas_call | solution.py:579
  172.4 5.3 %grad_step.1 = (bf16[512,256]{1,0:T(8,128)(2,1)S(1)}, bf16[512,256]{1,0:T(8,128)(2,1)S(1)}, bf16[512,256]{1,0:T(8,128)(2,1)S(1)}, bf16[512,256]{1,0:T(8,128)(2,1)S(1)}) custom-call(s32[4]{0:T(128)S(1)} %pad_add_fusion.place, s32[24]{0:T(128)S(1)} %get-tuple-element.233.meta, f32[1,4096]{1,0:T(1,128)S(1)} %add_add_fusion.2.total_ref, ...), custom_call_target="tpu_custom_call" | custom-call | flops 4294967296 | bytes 1048576 | tf_op jit(solution)/shard_map/grad_step/pallas_call | solution.py:620
  179.1 5.9 %all-to-all-start = ((bf16[16,128,256]{2,1,0:T(8,128)(2,1)}), bf16[16,128,256]{2,1,0:T(8,128)(2,1)S(1)}, u32[]{:S(2)}, u32[]{:S(2)}) async-start(bf16[16,128,256]{2,1,0:T(8,128)(2,1)} %add_convert_fusion), calls=%async_computation | async-start | bytes 2097152 | tf_op jit(solution)/shard_map/all_to_all | solution.py:641
  190.5 3.7 %collective-permute-done.55 = bf16[512,256]{1,0:T(8,128)(2,1)S(1)} collective-permute-done((bf16[512,256]{1,0:T(8,128)(2,1)S(1)}, bf16[512,256]{1,0:T(8,128)(2,1)S(1)}, u32[]{:S(2)}, u32[]{:S(2)}) %collective-permute-start.55) | collective-permute-done | bytes 262176 | tf_op jit(solution)/shard_map/ppermute | solution.py:637
  194.2 7.9 %collective-permute-done.56 = bf16[512,256]{1,0:T(8,128)(2,1)S(1)} collective-permute-done((bf16[512,256]{1,0:T(8,128)(2,1)S(1)}, bf16[512,256]{1,0:T(8,128)(2,1)S(1)}, u32[]{:S(2)}, u32[]{:S(2)}) %collective-permute-start.56) | collective-permute-done | bytes 262176 | tf_op jit(solution)/shard_map/ppermute | solution.py:637
  (136 shorter events, 67.0 us)
Async XLA Ops:
  3.0 11.0 %collective-permute-start = (bf16[528,128]{1,0:T(8,128)(2,1)S(1)}, bf16[528,128]{1,0:T(8,128)(2,1)S(1)}, u32[]{:S(2)}, u32[]{:S(2)}) collective-permute-start(bf16[528,128]{1,0:T(8,128)(2,1)S(1)} %get-tuple-element.180), channel_id=1, source_target_pairs={{0,16},{16,0},{1,17},{17,1},{2,18},{18,2},{3,19},{19,3},{4,20},{20... | collective-permute-start | bytes 405512 | tf_op jit(solution)/shard_map/ppermute | solution.py:633
  4.7 9.4 %collective-permute-start.1 = (bf16[528,128]{1,0:T(8,128)(2,1)S(1)}, bf16[528,128]{1,0:T(8,128)(2,1)S(1)}, u32[]{:S(2)}, u32[]{:S(2)}) collective-permute-start(bf16[528,128]{1,0:T(8,128)(2,1)S(1)} %get-tuple-element.181), channel_id=1, source_target_pairs={{0,16},{16,0},{1,17},{17,1},{2,18},{18,2},{3,19},{19,3},{4,20},{20... | collective-permute-start | bytes 405512 | tf_op jit(solution)/shard_map/ppermute | solution.py:633
  15.3 15.0 %collective-permute-start.5 = (bf16[2,528,128]{2,1,0:T(8,128)(2,1)S(1)}, bf16[2,528,128]{2,1,0:T(8,128)(2,1)S(1)}, u32[]{:S(2)}, u32[]{:S(2)}) collective-permute-start(bf16[2,528,128]{2,1,0:T(8,128)(2,1)S(1)} %pad_maximum_fusion.refs_0_), channel_id=1, source_target_pairs={{0,64},{32,96},{64,0},{96,32},{1,65},{33,97},{65,1},{97,33},{2,66}... | collective-permute-start | bytes 811016 | tf_op jit(solution)/shard_map/ppermute | solution.py:637
  18.6 12.6 %collective-permute-start.4 = (bf16[2,528,128]{2,1,0:T(8,128)(2,1)S(1)}, bf16[2,528,128]{2,1,0:T(8,128)(2,1)S(1)}, u32[]{:S(2)}, u32[]{:S(2)}) collective-permute-start(bf16[2,528,128]{2,1,0:T(8,128)(2,1)S(1)} %pad_maximum_fusion.refs_0_), channel_id=1, source_target_pairs={{0,96},{32,64},{64,32},{96,0},{1,97},{33,65},{65,33},{97,1},{2,98}... | collective-permute-start | bytes 811016 | tf_op jit(solution)/shard_map/ppermute | solution.py:637
  19.7 12.0 %collective-permute-start.3 = (bf16[2,528,128]{2,1,0:T(8,128)(2,1)S(1)}, bf16[2,528,128]{2,1,0:T(8,128)(2,1)S(1)}, u32[]{:S(2)}, u32[]{:S(2)}) collective-permute-start(bf16[2,528,128]{2,1,0:T(8,128)(2,1)S(1)} %pad_maximum_fusion.refs_0_), channel_id=1, source_target_pairs={{0,32},{32,0},{64,96},{96,64},{1,33},{33,1},{65,97},{97,65},{2,34}... | collective-permute-start | bytes 811016 | tf_op jit(solution)/shard_map/ppermute | solution.py:637
  19.7 10.6 %collective-permute-start.6 = (f32[1,512]{1,0:T(1,128)S(1)}, f32[1,512]{1,0:T(1,128)S(1)}, u32[]{:S(2)}, u32[]{:S(2)}) collective-permute-start(f32[1,512]{1,0:T(1,128)S(1)} %max.27), channel_id=1, source_target_pairs={{0,2},{2,0},{1,3},{3,1},{4,6},{6,4},{5,7},{7,5},{8,10},{10,8},{9,1... | collective-permute-start | bytes 6152 | tf_op jit(solution)/shard_map/ppermute | solution.py:633
  36.3 11.7 %collective-permute-start.14 = (f32[2,1,512]{2,1,0:T(1,128)S(1)}, f32[2,1,512]{2,1,0:T(1,128)S(1)}, u32[]{:S(2)}, u32[]{:S(2)}) collective-permute-start(f32[2,1,512]{2,1,0:T(1,128)S(1)} %pad_maximum_fusion.2.refs_8_), channel_id=1, source_target_pairs={{0,64},{32,96},{64,0},{96,32},{1,65},{33,97},{65,1},{97,33},{2,66}... | collective-permute-start | bytes 12296 | tf_op jit(solution)/shard_map/ppermute | solution.py:637
  38.8 9.2 %collective-permute-start.13 = (f32[2,1,512]{2,1,0:T(1,128)S(1)}, f32[2,1,512]{2,1,0:T(1,128)S(1)}, u32[]{:S(2)}, u32[]{:S(2)}) collective-permute-start(f32[2,1,512]{2,1,0:T(1,128)S(1)} %pad_maximum_fusion.2.refs_8_), channel_id=1, source_target_pairs={{0,96},{32,64},{64,32},{96,0},{1,97},{33,65},{65,33},{97,1},{2,98}... | collective-permute-start | bytes 12296 | tf_op jit(solution)/shard_map/ppermute | solution.py:637
  40.4 7.6 %collective-permute-start.12 = (f32[2,1,512]{2,1,0:T(1,128)S(1)}, f32[2,1,512]{2,1,0:T(1,128)S(1)}, u32[]{:S(2)}, u32[]{:S(2)}) collective-permute-start(f32[2,1,512]{2,1,0:T(1,128)S(1)} %pad_maximum_fusion.2.refs_8_), channel_id=1, source_target_pairs={{0,32},{32,0},{64,96},{96,64},{1,33},{33,1},{65,97},{97,65},{2,34}... | collective-permute-start | bytes 12296 | tf_op jit(solution)/shard_map/ppermute | solution.py:637
  48.2 15.3 %collective-permute-start.17 = (bf16[2,528,128]{2,1,0:T(8,128)(2,1)S(1)}, bf16[2,528,128]{2,1,0:T(8,128)(2,1)S(1)}, u32[]{:S(2)}, u32[]{:S(2)}) collective-permute-start(bf16[2,528,128]{2,1,0:T(8,128)(2,1)S(1)} %pad_maximum_fusion.1.refs_0_), channel_id=1, source_target_pairs={{0,64},{32,96},{64,0},{96,32},{1,65},{33,97},{65,1},{97,33},{2,66}... | collective-permute-start | bytes 811016 | tf_op jit(solution)/shard_map/ppermute | solution.py:637
  51.3 13.1 %collective-permute-start.16 = (bf16[2,528,128]{2,1,0:T(8,128)(2,1)S(1)}, bf16[2,528,128]{2,1,0:T(8,128)(2,1)S(1)}, u32[]{:S(2)}, u32[]{:S(2)}) collective-permute-start(bf16[2,528,128]{2,1,0:T(8,128)(2,1)S(1)} %pad_maximum_fusion.1.refs_0_), channel_id=1, source_target_pairs={{0,96},{32,64},{64,32},{96,0},{1,97},{33,65},{65,33},{97,1},{2,98}... | collective-permute-start | bytes 811016 | tf_op jit(solution)/shard_map/ppermute | solution.py:637
  53.0 11.4 %collective-permute-start.15 = (bf16[2,528,128]{2,1,0:T(8,128)(2,1)S(1)}, bf16[2,528,128]{2,1,0:T(8,128)(2,1)S(1)}, u32[]{:S(2)}, u32[]{:S(2)}) collective-permute-start(bf16[2,528,128]{2,1,0:T(8,128)(2,1)S(1)} %pad_maximum_fusion.1.refs_0_), channel_id=1, source_target_pairs={{0,32},{32,0},{64,96},{96,64},{1,33},{33,1},{65,97},{97,65},{2,34}... | collective-permute-start | bytes 811016 | tf_op jit(solution)/shard_map/ppermute | solution.py:637
  53.0 10.5 %collective-permute-start.19 = (f32[2,1,512]{2,1,0:T(1,128)S(1)}, f32[2,1,512]{2,1,0:T(1,128)S(1)}, u32[]{:S(2)}, u32[]{:S(2)}) collective-permute-start(f32[2,1,512]{2,1,0:T(1,128)S(1)} %pad_maximum_fusion.4), channel_id=1, source_target_pairs={{0,2},{2,0},{1,3},{3,1},{4,6},{6,4},{5,7},{7,5},{8,10},{10,8},{9,1... | collective-permute-start | bytes 12296 | tf_op jit(solution)/shard_map/ppermute | solution.py:633
  64.4 5.7 %collective-permute-start.22 = (f32[1,2176]{1,0:T(1,128)S(1)}, f32[1,2176]{1,0:T(1,128)S(1)}, u32[]{:S(2)}, u32[]{:S(2)}) collective-permute-start(f32[1,2176]{1,0:T(1,128)S(1)} %get-tuple-element.247), channel_id=1, source_target_pairs={{0,12},{4,8},{8,4},{12,0},{1,13},{5,9},{9,5},{13,1},{2,14},{6,10},... | collective-permute-start | bytes 26120 | tf_op jit(solution)/shard_map/ppermute | solution.py:678
  77.4 15.6 %collective-permute-start.27 = (bf16[2,528,128]{2,1,0:T(8,128)(2,1)S(1)}, bf16[2,528,128]{2,1,0:T(8,128)(2,1)S(1)}, u32[]{:S(2)}, u32[]{:S(2)}) collective-permute-start(bf16[2,528,128]{2,1,0:T(8,128)(2,1)S(1)} %pad_maximum_fusion.1.refs_0_), channel_id=1, source_target_pairs={{0,1},{1,0},{2,3},{3,2},{4,5},{5,4},{6,7},{7,6},{8,9},{9,8},{10,11... | collective-permute-start | bytes 811016 | tf_op jit(solution)/shard_map/ppermute | solution.py:633
  77.7 15.3 %collective-permute-start.28 = (bf16[2,528,128]{2,1,0:T(8,128)(2,1)S(1)}, bf16[2,528,128]{2,1,0:T(8,128)(2,1)S(1)}, u32[]{:S(2)}, u32[]{:S(2)}) collective-permute-start(bf16[2,528,128]{2,1,0:T(8,128)(2,1)S(1)} %collective-permute-done.15.refs_1_), channel_id=1, source_target_pairs={{0,1},{1,0},{2,3},{3,2},{4,5},{5,4},{6,7},{7,6},{8,9},{9,8},{10,11... | collective-permute-start | bytes 811016 | tf_op jit(solution)/shard_map/ppermute | solution.py:633
  78.0 15.0 %collective-permute-start.29 = (bf16[2,528,128]{2,1,0:T(8,128)(2,1)S(1)}, bf16[2,528,128]{2,1,0:T(8,128)(2,1)S(1)}, u32[]{:S(2)}, u32[]{:S(2)}) collective-permute-start(bf16[2,528,128]{2,1,0:T(8,128)(2,1)S(1)} %collective-permute-done.16.refs_3_), channel_id=1, source_target_pairs={{0,1},{1,0},{2,3},{3,2},{4,5},{5,4},{6,7},{7,6},{8,9},{9,8},{10,11... | collective-permute-start | bytes 811016 | tf_op jit(solution)/shard_map/ppermute | solution.py:633
  78.2 14.8 %collective-permute-start.30 = (bf16[2,528,128]{2,1,0:T(8,128)(2,1)S(1)}, bf16[2,528,128]{2,1,0:T(8,128)(2,1)S(1)}, u32[]{:S(2)}, u32[]{:S(2)}) collective-permute-start(bf16[2,528,128]{2,1,0:T(8,128)(2,1)S(1)} %collective-permute-done.17.refs_2_), channel_id=1, source_target_pairs={{0,1},{1,0},{2,3},{3,2},{4,5},{5,4},{6,7},{7,6},{8,9},{9,8},{10,11... | collective-permute-start | bytes 811016 | tf_op jit(solution)/shard_map/ppermute | solution.py:633
  93.1 7.0 %collective-permute-start.33 = (f32[1,8192]{1,0:T(1,128)S(1)}, f32[1,8192]{1,0:T(1,128)S(1)}, u32[]{:S(2)}, u32[]{:S(2)}) collective-permute-start(f32[1,8192]{1,0:T(1,128)S(1)} %add_add_fusion.1), channel_id=1, source_target_pairs={{0,96},{32,64},{64,32},{96,0},{1,97},{33,65},{65,33},{97,1},{2,98}... | collective-permute-start | bytes 98312 | tf_op jit(solution)/shard_map/ppermute | solution.py:678
  104.4 11.3 %collective-permute-start.36 = (f32[1,2048]{1,0:T(1,128)S(1)}, f32[1,2048]{1,0:T(1,128)S(1)}, u32[]{:S(2)}, u32[]{:S(2)}) collective-permute-start(f32[1,2048]{1,0:T(1,128)S(1)} %col_step.2), channel_id=1, source_target_pairs={{0,12},{4,8},{8,4},{12,0},{1,13},{5,9},{9,5},{13,1},{2,14},{6,10},... | collective-permute-start | bytes 24584 | tf_op jit(solution)/shard_map/ppermute | solution.py:678
  105.8 10.0 %collective-permute-start.35 = (f32[1,2048]{1,0:T(1,128)S(1)}, f32[1,2048]{1,0:T(1,128)S(1)}, u32[]{:S(2)}, u32[]{:S(2)}) collective-permute-start(f32[1,2048]{1,0:T(1,128)S(1)} %col_step.2), channel_id=1, source_target_pairs={{0,4},{4,0},{8,12},{12,8},{1,5},{5,1},{9,13},{13,9},{2,6},{6,2},{1... | collective-permute-start | bytes 24584 | tf_op jit(solution)/shard_map/ppermute | solution.py:678
  106.6 9.1 %collective-permute-start.34 = (f32[1,2048]{1,0:T(1,128)S(1)}, f32[1,2048]{1,0:T(1,128)S(1)}, u32[]{:S(2)}, u32[]{:S(2)}) collective-permute-start(f32[1,2048]{1,0:T(1,128)S(1)} %col_step.2), channel_id=1, source_target_pairs={{0,8},{4,12},{8,0},{12,4},{1,9},{5,13},{9,1},{13,5},{2,10},{6,14},... | collective-permute-start | bytes 24584 | tf_op jit(solution)/shard_map/ppermute | solution.py:678
  119.5 11.3 %collective-permute-start.40 = (f32[1,4096]{1,0:T(1,128)S(1)}, f32[1,4096]{1,0:T(1,128)S(1)}, u32[]{:S(2)}, u32[]{:S(2)}) collective-permute-start(f32[1,4096]{1,0:T(1,128)S(1)} %add.143), channel_id=1, source_target_pairs={{0,18},{2,16},{16,2},{18,0},{1,19},{3,17},{17,3},{19,1},{4,22},{6,... | collective-permute-start | bytes 49160 | tf_op jit(solution)/shard_map/ppermute | solution.py:678
  122.7 8.1 %collective-permute-start.39 = (f32[1,4096]{1,0:T(1,128)S(1)}, f32[1,4096]{1,0:T(1,128)S(1)}, u32[]{:S(2)}, u32[]{:S(2)}) collective-permute-start(f32[1,4096]{1,0:T(1,128)S(1)} %add.143), channel_id=1, source_target_pairs={{0,16},{2,18},{16,0},{18,2},{1,17},{3,19},{17,1},{19,3},{4,20},{6,... | collective-permute-start | bytes 49160 | tf_op jit(solution)/shard_map/ppermute | solution.py:678
  122.7 8.2 %collective-permute-start.38 = (f32[1,4096]{1,0:T(1,128)S(1)}, f32[1,4096]{1,0:T(1,128)S(1)}, u32[]{:S(2)}, u32[]{:S(2)}) collective-permute-start(f32[1,4096]{1,0:T(1,128)S(1)} %add.143), channel_id=1, source_target_pairs={{0,2},{2,0},{16,18},{18,16},{1,3},{3,1},{17,19},{19,17},{4,6},{6,4... | collective-permute-start | bytes 49160 | tf_op jit(solution)/shard_map/ppermute | solution.py:678
  151.7 9.9 %collective-permute-start.50 = (f32[1,4096]{1,0:T(1,128)S(1)}, f32[1,4096]{1,0:T(1,128)S(1)}, u32[]{:S(2)}, u32[]{:S(2)}) collective-permute-start(f32[1,4096]{1,0:T(1,128)S(1)} %add.153), channel_id=1, source_target_pairs={{0,18},{2,16},{16,2},{18,0},{1,19},{3,17},{17,3},{19,1},{4,22},{6,... | collective-permute-start | bytes 49160 | tf_op jit(solution)/shard_map/ppermute | solution.py:678
  154.9 6.8 %collective-permute-start.49 = (f32[1,4096]{1,0:T(1,128)S(1)}, f32[1,4096]{1,0:T(1,128)S(1)}, u32[]{:S(2)}, u32[]{:S(2)}) collective-permute-start(f32[1,4096]{1,0:T(1,128)S(1)} %add.153), channel_id=1, source_target_pairs={{0,16},{2,18},{16,0},{18,2},{1,17},{3,19},{17,1},{19,3},{4,20},{6,... | collective-permute-start | bytes 49160 | tf_op jit(solution)/shard_map/ppermute | solution.py:678
  154.9 6.8 %collective-permute-start.48 = (f32[1,4096]{1,0:T(1,128)S(1)}, f32[1,4096]{1,0:T(1,128)S(1)}, u32[]{:S(2)}, u32[]{:S(2)}) collective-permute-start(f32[1,4096]{1,0:T(1,128)S(1)} %add.153), channel_id=1, source_target_pairs={{0,2},{2,0},{16,18},{18,16},{1,3},{3,1},{17,19},{19,17},{4,6},{6,4... | collective-permute-start | bytes 49160 | tf_op jit(solution)/shard_map/ppermute | solution.py:678
  179.1 23.0 %all-to-all-start = ((bf16[16,128,256]{2,1,0:T(8,128)(2,1)}), bf16[16,128,256]{2,1,0:T(8,128)(2,1)S(1)}, u32[]{:S(2)}, u32[]{:S(2)}) async-start(bf16[16,128,256]{2,1,0:T(8,128)(2,1)} %add_convert_fusion), calls=%async_computation | async-start | bytes 2097152 | tf_op jit(solution)/shard_map/all_to_all | solution.py:641
  185.0 9.2 %collective-permute-start.55 = (bf16[512,256]{1,0:T(8,128)(2,1)S(1)}, bf16[512,256]{1,0:T(8,128)(2,1)S(1)}, u32[]{:S(2)}, u32[]{:S(2)}) collective-permute-start(bf16[512,256]{1,0:T(8,128)(2,1)S(1)} %get-tuple-element.346), channel_id=1, source_target_pairs={{0,4},{4,0},{8,12},{12,8},{1,5},{5,1},{9,13},{13,9},{2,6},{6,2},{1... | collective-permute-start | bytes 786440 | tf_op jit(solution)/shard_map/ppermute | solution.py:637
  187.1 15.0 %collective-permute-start.56 = (bf16[512,256]{1,0:T(8,128)(2,1)S(1)}, bf16[512,256]{1,0:T(8,128)(2,1)S(1)}, u32[]{:S(2)}, u32[]{:S(2)}) collective-permute-start(bf16[512,256]{1,0:T(8,128)(2,1)S(1)} %get-tuple-element.347), channel_id=1, source_target_pairs={{0,12},{4,8},{8,4},{12,0},{1,13},{5,9},{9,5},{13,1},{2,14},{6,10},... | collective-permute-start | bytes 786440 | tf_op jit(solution)/shard_map/ppermute | solution.py:637
  189.1 13.0 %collective-permute-start.57 = (bf16[512,256]{1,0:T(8,128)(2,1)S(1)}, bf16[512,256]{1,0:T(8,128)(2,1)S(1)}, u32[]{:S(2)}, u32[]{:S(2)}) collective-permute-start(bf16[512,256]{1,0:T(8,128)(2,1)S(1)} %get-tuple-element.348), channel_id=1, source_target_pairs={{0,8},{4,12},{8,0},{12,4},{1,9},{5,13},{9,1},{13,5},{2,10},{6,14},... | collective-permute-start | bytes 786440 | tf_op jit(solution)/shard_map/ppermute | solution.py:637
  (27 other events, 111.4 us)
where the time goes:
time: 204 us
  starting transfers between devices  79.8 us (39%)
  Pallas kernels  75.2 us (37%)
  waiting for transfers between devices  42 us (21%)
  other arithmetic  4.39 us (2%)
    ppermute x27, starting transfers between devices, ring(): lax.ppermute(value, axes, [(i, i ^ mask) for i in range(4)])  44.2 us
    ppermute x27, waiting for transfers between devices, ring(): lax.ppermute(value, axes, [(i, i ^ mask) for i in range(4)])  21.5 us
    ppermute x12, starting transfers between devices, from_xor(): return lax.ppermute(value, axis, [(i, i ^ mask) for i in range(4)])  17.5 us
    pallas_call x2, Pallas kernels, row_soft(): pl.pallas_call(soft_kernel, grid=(steps,), out_shape=(jax.ShapeDtypeStruc...  15.2 us
    ppermute x12, waiting for transfers between devices, from_xor(): return lax.ppermute(value, axis, [(i, i ^ mask) for i in range(4)])  13.8 us
    pallas_call x2, Pallas kernels, student_step(): pl.pallas_call(functools.partial(student_kernel, part), out_shape=outs, i...  13 us
    ppermute x19, starting transfers between devices, swap(): return lax.ppermute(value, axis, [(0, 1), (1, 0)])  12.1 us
    pallas_call x1, Pallas kernels, row_max(): pl.pallas_call(max_kernel, grid=(steps,), out_shape=jax.ShapeDtypeStruct(...  8.93 us
  transfers between devices with their start and end apart: 59, of which 26 were waited for; matrix products, arithmetic and copies ran while one was open for 0% of the time, Pallas kernels for 28%

commit v1 on v0

--- a/solution.py
+++ b/solution.py
@@ -20,11 +20,12 @@
 ALIGN = 16
 FAR = 1e30
 INFO = 16
+SPAN = 3
 BLOCKS = 8
 END, TILES = 2 * BLOCKS, 2 * BLOCKS + 1
 MIB = 2**20
 
-NT = (((1,), (1,)), ((), ()))
+LOG2E = math.log2(math.e)
 
 
 def params(mib):
@@ -83,7 +84,7 @@
 
 def compact_kernel(mask_ref, teach_ref, stud_ref, teach_out, stud_out):
     rows, width = teach_ref.shape
-    mask = mask_ref[...]
+    mask = mask_ref[...].reshape(1, rows).astype(F32)
     down = lax.broadcasted_iota(jnp.int32, (rows, rows), 0)
     along = lax.broadcasted_iota(jnp.int32, (rows, rows), 1)
     upper = jnp.where(down <= along, 1.0, 0.0).astype(BF16)
@@ -101,7 +102,7 @@
     stud_out[rows:] = info.astype(BF16)
 
 
-def compact(mask_row, teacher, student):
+def compact(masked, teacher, student):
     rows, width = teacher.shape
     return pl.pallas_call(
         compact_kernel,
@@ -110,7 +111,7 @@
         out_specs=(vmem(), vmem()),
         compiler_params=params(12),
         name="compact",
-    )(mask_row, teacher, student)
+    )(masked, teacher, student)
 
 
 def max_kernel(teach_ref, proto_ref, out_ref, turned_ref):
@@ -164,7 +165,7 @@
         logit = jnp.dot(proto_ref[start : start + chunk], turned_ref[...], preferred_element_type=F32)
         higher = jnp.maximum(top, jnp.max(logit, axis=0, keepdims=True))
         total = total * jnp.exp((top - higher) * (1 / student_temp)) + jnp.sum(
-            jnp.exp((logit - higher) * (1 / student_temp)), axis=0, keepdims=True
+            jnp.exp2((logit - higher) * (LOG2E / student_temp)), axis=0, keepdims=True
         )
         top = higher
     top_ref[...] = top
@@ -282,7 +283,7 @@
         top = line_ref[:, pl.ds(start, TILE)]
         for k in range(0, count, chunk):
             logit = jnp.dot(own_ref[k : k + chunk], feats, preferred_element_type=F32)
-            expo = jnp.exp((logit - top) * (1 / teacher_temp))
+            expo = jnp.exp2((logit - top) * (LOG2E / teacher_temp))
             expo_ref[tile, k : k + chunk] = expo.astype(BF16)
             acc_ref[k : k + chunk] += fold(expo)
 
@@ -479,7 +480,7 @@
         for piece in range(2):
             k = pl.multiple_of((place[2] ^ (2 * part + piece)) * chunk, chunk)
             logit = jnp.dot(own_ref[pl.ds(k, chunk), :], across, preferred_element_type=F32)
-            probs = jnp.exp(logit * (1 / student_temp) - lse).astype(BF16)
+            probs = jnp.exp2((logit - lse) * (LOG2E / student_temp)).astype(BF16)
             acc_ref[piece] += jnp.dot(probs, feats, preferred_element_type=F32)
             turned += jnp.dot(turned_ref[:, pl.ds(k, chunk)], probs, preferred_element_type=F32)
         sums = jnp.transpose(turned)
@@ -518,30 +519,36 @@
     return jnp.concatenate(parts, axis=0)
 
 
-def feature_kernel(proto_total, meta, total_ref, expo_ref, turned_ref, sums_ref):
+def feature_kernel(proto_total, first, meta, total_ref, expo_ref, turned_ref, *refs):
+    sums_ref = refs[-1]
     scale = col_scale_of(total_ref, expo_ref.shape[1], proto_total)
-    sums_ref[...] = jnp.zeros_like(sums_ref)
     scaled = (turned_ref[...].astype(F32) * scale).astype(BF16)
-
-    @pl.loop(0, meta[TILES])
+    if first == 0:
+        sums_ref[...] = jnp.zeros_like(sums_ref)
+        span = (0, jnp.minimum(meta[TILES], SPAN))
+    else:
+        span = (SPAN, meta[TILES])
+
+    @pl.loop(*span)
     def _(tile):
         start = pl.multiple_of(tile * TILE, TILE)
         turned = jnp.dot(scaled, expo_ref[tile], preferred_element_type=F32)
         sums_ref[pl.ds(start, TILE), :] = jnp.transpose(turned).astype(BF16)
 
 
-def feature_step(meta, total, expo, turned, proto_total):
+def feature_step(first, meta, total, expo, turned, proto_total, *sums):
     tiles, count, _ = expo.shape
     width = turned.shape[0]
     return pl.pallas_call(
-        functools.partial(feature_kernel, proto_total),
-        out_shape=jax.ShapeDtypeStruct((tiles * TILE, width), BF16),
-        in_specs=[smem()] + [vmem()] * 3,
+        functools.partial(feature_kernel, proto_total, first),
+        out_shape=pltpu.VMEM((tiles * TILE, width), BF16),
+        in_specs=[smem()] + [vmem()] * (3 + len(sums)),
         out_specs=vmem(),
+        input_output_aliases={4: 0} if sums else {},
         compiler_params=params(14),
-        cost_estimate=cost(count * tiles * TILE * width * 2),
+        cost_estimate=cost(count * tiles * TILE * width),
         name="feature_step",
-    )(meta, total, pinned(expo), turned)
+    )(meta, total, pinned(expo), turned, *[pinned(value) for value in sums])
 
 
 def join_kernel(place, meta, total_ref, valid_ref, rank_ref, stud_ref, plan_ref, keep_ref, give_ref, weight_ref, sums_ref):
@@ -653,6 +660,10 @@
     return jnp.stack(choose(low, half, swap(half, "xl")))
 
 
+def double(value, mask):
+    return jnp.stack([value, from_xor(value, "y", mask)])
+
+
 def gather_along(pair):
     return [pair] + [from_xor(pair, "y", mask) for mask in (1, 3, 2)]
 
@@ -700,7 +711,7 @@
     low_x, low_c = xl == 0, core == 0
     table = streamed(prototypes)
 
-    teach, stud = compact(masked.astype(F32)[None], streamed(teacher), streamed(student))
+    teach, stud = compact(masked, streamed(teacher), streamed(student))
     t_half, _ = choose(low_c, teach[:, :LANES], teach[:, LANES:])
     s_half, _ = choose(low_c, stud[:, :LANES], stud[:, LANES:])
     t_half, s_half, teach, stud = tie(t_half, s_half, teach, stud)
@@ -723,26 +734,30 @@
     mine, other, top, beside, soft, stud, s_pair = tie(mine, other, top, beside, soft, stud, s_pair)
 
     tops = gather_along(jnp.stack(choose(low_x, top, beside)))
+    s_mine = double(s_pair, 1)
     soft_two = row_soft(stud, table, rows, 1, 2)
-    mine, other, tops, soft, soft_two, s_pair, place = tie(mine, other, tops, soft, soft_two, s_pair, place)
-
-    s_mine = gather_along(s_pair)
+    mine, other, tops, soft, soft_two, s_mine, place = tie(mine, other, tops, soft, soft_two, s_mine, place)
     soft = jnp.stack(merged(soft, soft_two))
     soft = jnp.stack(merged(soft, swap(soft, "c")))
+    soft, tops, s_mine = tie(soft, tops, s_mine)
+
+    s_mine = [s_mine[0], s_mine[1], from_xor(s_mine, "y", 3)]
     soft_far = swap(soft, "xh")
     expo, col, valid, meta = expo_step(place, ordered(mine) + ordered(other), ordered(tops), prototypes)
-    s_mine, col, soft, soft_far = tie(s_mine, col, soft, soft_far)
+    col, soft, soft_far = tie(col, soft, soft_far)
 
     got = ring(col, "z")
     soft = merged(soft, soft_far)
     got, s_mine, col, soft = tie(got, s_mine, col, soft)
+    s_mine = [s_mine[0], s_mine[1], s_mine[2][0], s_mine[2][1]]
     col = total_of(col, got)
     mask_total = col[0, count]
-    row = row_step(place, meta, col, expo, proto_total, soft[0] / student_temp + jnp.log(soft[1]))
+    col, s_mine = tie(col, s_mine)
+    s_other = [swap(piece, "c") for piece in s_mine]
+    row = row_step(place, meta, col, expo, proto_total, soft[0] + student_temp * jnp.log(soft[1]))
+    row, s_mine, s_other = tie(row, s_mine, s_other)
     row = row + swap(row, "c")
-    row, s_mine = tie(row, s_mine)
     got = ring(row, "x")
-    s_other = [swap(piece, "c") for piece in s_mine]
     row, got, s_mine, s_other = tie(row, got, s_mine, s_other)
     row = total_of(row, got)
     got = ring(row, "y")
@@ -774,29 +789,30 @@
     row = row + swap(row, "c")
     row, turned = tie(row, turned)
     got = ring(row, "x")
-    plan_sums = feature_step(meta, col, expo, turned, proto_total)
+    plan_sums = feature_step(0, meta, col, expo, turned, proto_total)
     row, got, plan_sums = tie(row, got, plan_sums)
     row = total_of(row, got)
     got = ring(row, "y")
-    row, got = tie(row, got)
+    plan_sums = feature_step(1, meta, col, expo, turned, proto_total, plan_sums)
+    row, got, plan_sums = tie(row, got, plan_sums)
     row = total_of(row, got)
 
-    keep, give = join_step(place, meta, row, valid, rank, two[2], plan_sums)
+    keep, give = join_step(place, meta, row, valid, rank, two[2], pinned(plan_sums))
     keep, give, row = tie(keep, give, row)
     got = swap(give, "c")
     grads = grad_step(
         place, meta, row, valid, stud_rows, expo, col, tuple(one[:2]) + tuple(two[:2]), proto_total
     )
     keep, got, grads = tie(keep, got, grads)
+    pieces = scatter_protos(grads)
     keep = (keep.astype(F32) + got.astype(F32)).astype(BF16)
     parts = exchange(keep, ("y", "xl", "xh"))
-    pieces = scatter_protos(grads)
-    parts, pieces = tie(parts, pieces)
+    proto_grad = (
+        sum(piece.astype(F32) for piece in pieces) * (proto_total / jnp.sqrt(mask_total))
+    ).astype(BF16)
+    parts, proto_grad = tie(parts, proto_grad)
     feature_grad = (
         jnp.sum(parts.astype(F32), axis=0) * (math.sqrt(proto_total) / student_temp)
-    ).astype(BF16)
-    proto_grad = (
-        sum(piece.astype(F32) for piece in pieces) * (proto_total / jnp.sqrt(mask_total))
     ).astype(BF16)
     return feature_grad, proto_grad
 

time: 204 us -> 192 us (0.941)
  waiting for transfers between devices: 42 us -> 33.4 us
  starting transfers between devices: 79.8 us -> 77.3 us
    ppermute x27, waiting for transfers between devices: 21.5 us -> 11.9 us  [ring(): lax.ppermute(value, axes, [(i, i ^ mask) for i in range(4)])]
    ppermute x12 -> x11, starting transfers between devices: 17.5 us -> 16 us  [from_xor(): return lax.ppermute(value, axis, [(i, i ^ mask) for i in range(4)])]
    pallas_call x1 -> x2, Pallas kernels: 5.11 us -> 6.03 us  [feature_step(): pl.pallas_call(functools.partial(feature_kernel, proto_total, first), out...]
    ppermute x12 -> x11, waiting for transfers between devices: 13.8 us -> 13.8 us  [from_xor(): return lax.ppermute(value, axis, [(i, i ^ mask) for i in range(4)])]
  transfers between devices with their start and end apart: 59 -> 58, of which waited for: 26 -> 23; matrix products, arithmetic and copies ran while one was open for 0% -> 1% of each run, Pallas kernels for 28% -> 30%
where the time goes in v1:
time: 192 us
  starting transfers between devices  77.3 us (40%)
  Pallas kernels  73.9 us (38%)
  waiting for transfers between devices  33.4 us (17%)
  other arithmetic  3.75 us (2%)
  between operations  1.94 us (1%)
    ppermute x27, starting transfers between devices, ring(): lax.ppermute(value, axes, [(i, i ^ mask) for i in range(4)])  43.9 us
    ppermute x11, starting transfers between devices, from_xor(): return lax.ppermute(value, axis, [(i, i ^ mask) for i in range(4)])  16 us
    ppermute x11, waiting for transfers between devices, from_xor(): return lax.ppermute(value, axis, [(i, i ^ mask) for i in range(4)])  13.8 us
    pallas_call x2, Pallas kernels, row_soft(): pl.pallas_call(soft_kernel, grid=(steps,), out_shape=(jax.ShapeDtypeStruc...  13.6 us
    pallas_call x2, Pallas kernels, student_step(): pl.pallas_call(functools.partial(student_kernel, part), out_shape=outs, i...  13 us
    ppermute x19, starting transfers between devices, swap(): return lax.ppermute(value, axis, [(0, 1), (1, 0)])  12.3 us
    ppermute x27, waiting for transfers between devices, ring(): lax.ppermute(value, axes, [(i, i ^ mask) for i in range(4)])  11.9 us
    pallas_call x1, Pallas kernels, row_max(): pl.pallas_call(max_kernel, grid=(steps,), out_shape=jax.ShapeDtypeStruct(...  8.93 us
  transfers between devices with their start and end apart: 58, of which 23 were waited for; matrix products, arithmetic and copies ran while one was open for 1% of the time, Pallas kernels for 30%

profile of v1, /device:TPU:0, one launch (start us, length us, event | category | flops | bytes accessed | tf_op | source)
XLA Modules:
  0.0 191.6 jit_solution(3145626591326902450)
XLA Ops:
  5.1 8.9 %row_max.1 = f32[1,512]{1,0:T(1,128)S(1)} custom-call(bf16[528,256]{1,0:T(8,128)(2,1)S(1)} %get-tuple-element.190.teach_ref, bf16[16384,256]{1,0:T(8,128)(2,1)} %refs_8_.1), custom_call_target="tpu_custom_call" | custom-call | flops 4294967296 | bytes 1048576 | tf_op jit(solution)/shard_map/row_max/pallas_call | solution.py:137
  15.3 3.3 %collective-permute-start.5 = (bf16[2,528,128]{2,1,0:T(8,128)(2,1)S(1)}, bf16[2,528,128]{2,1,0:T(8,128)(2,1)S(1)}, u32[]{:S(2)}, u32[]{:S(2)}) collective-permute-start(bf16[2,528,128]{2,1,0:T(8,128)(2,1)S(1)} %pad_maximum_fusion.1.refs_0_), channel_id=1, source_target_pairs={{0,64},{32,96},{64,0},{96,32},{1,65},{33,97},{65,1},{97,33},{2,66}... | collective-permute-start | bytes 811016 | tf_op jit(solution)/shard_map/ppermute | solution.py:644
  19.7 3.0 %collective-permute-start.6 = (f32[1,512]{1,0:T(1,128)S(1)}, f32[1,512]{1,0:T(1,128)S(1)}, u32[]{:S(2)}, u32[]{:S(2)}) collective-permute-start(f32[1,512]{1,0:T(1,128)S(1)} %max.27), channel_id=1, source_target_pairs={{0,2},{2,0},{1,3},{3,1},{4,6},{6,4},{5,7},{7,5},{8,10},{10,8},{9,1... | collective-permute-start | bytes 6152 | tf_op jit(solution)/shard_map/ppermute | solution.py:640
  22.7 6.8 %row_soft.2 = (f32[1,512]{1,0:T(1,128)S(1)}, f32[1,512]{1,0:T(1,128)S(1)}) custom-call(bf16[528,256]{1,0:T(8,128)(2,1)S(1)} %get-tuple-element.224.feat_ref, bf16[16384,256]{1,0:T(8,128)(2,1)} %refs_8_.1), custom_call_target="tpu_custom_call" | custom-call | flops 3221225472 | bytes 1048576 | tf_op jit(solution)/shard_map/row_soft/pallas_call | solution.py:180
  36.3 2.1 %collective-permute-start.14 = (f32[2,1,512]{2,1,0:T(1,128)S(1)}, f32[2,1,512]{2,1,0:T(1,128)S(1)}, u32[]{:S(2)}, u32[]{:S(2)}) collective-permute-start(f32[2,1,512]{2,1,0:T(1,128)S(1)} %pad_maximum_fusion.3.refs_8_), channel_id=1, source_target_pairs={{0,64},{32,96},{64,0},{96,32},{1,65},{33,97},{65,1},{97,33},{2,66}... | collective-permute-start | bytes 12296 | tf_op jit(solution)/shard_map/ppermute | solution.py:644
  42.5 6.8 %row_soft.3 = (f32[1,512]{1,0:T(1,128)S(1)}, f32[1,512]{1,0:T(1,128)S(1)}) custom-call(bf16[528,256]{1,0:T(8,128)(2,1)S(1)} %get-tuple-element.224.feat_ref, bf16[16384,256]{1,0:T(8,128)(2,1)} %refs_8_.1), custom_call_target="tpu_custom_call" | custom-call | flops 3221225472 | bytes 1048576 | tf_op jit(solution)/shard_map/row_soft/pallas_call | solution.py:180
  50.7 3.1 %collective-permute-start.17 = (f32[2,1,512]{2,1,0:T(1,128)S(1)}, f32[2,1,512]{2,1,0:T(1,128)S(1)}, u32[]{:S(2)}, u32[]{:S(2)}) collective-permute-start(f32[2,1,512]{2,1,0:T(1,128)S(1)} %pad_maximum_fusion.5), channel_id=1, source_target_pairs={{0,2},{2,0},{1,3},{3,1},{4,6},{6,4},{5,7},{7,5},{8,10},{10,8},{9,1... | collective-permute-start | bytes 12296 | tf_op jit(solution)/shard_map/ppermute | solution.py:640
  55.0 6.7 %expo.1 = (bf16[8,2048,512]{2,1,0:T(8,128)(2,1)S(1)}, f32[1,2176]{1,0:T(1,128)S(1)}, f32[1,4096]{1,0:T(1,128)S(1)}, s32[24]{0:T(128)S(1)}) custom-call(s32[4]{0:T(128)S(1)} %pad_add_fusion.place, bf16[2,528,128]{2,1,0:T(8,128)(2,1)S(1)} %pad_maximum_fusion.1.refs_0_, bf16[2,528,128]{2,1,0:T(8,128)(2,1)S(1)} %collective-permute-done.3.refs_1_, ...), custom_call_target="tpu_custom_call" | custom-call | flops 4294967296 | bytes 1048576 | tf_op jit(solution)/shard_map/expo/pallas_call | solution.py:306
  61.8 4.1 %collective-permute-start.20 = (f32[1,2176]{1,0:T(1,128)S(1)}, f32[1,2176]{1,0:T(1,128)S(1)}, u32[]{:S(2)}, u32[]{:S(2)}) collective-permute-start(f32[1,2176]{1,0:T(1,128)S(1)} %get-tuple-element.257), channel_id=1, source_target_pairs={{0,12},{4,8},{8,4},{12,0},{1,13},{5,9},{9,5},{13,1},{2,14},{6,10},... | collective-permute-start | bytes 26120 | tf_op jit(solution)/shard_map/ppermute | solution.py:689
  72.3 2.5 %row_step.3 = f32[1,8192]{1,0:T(1,128)S(1)} custom-call(s32[4]{0:T(128)S(1)} %pad_add_fusion.place, s32[24]{0:T(128)S(1)} %get-tuple-element.250.meta, f32[1,2176]{1,0:T(1,128)S(1)} %add_add_fusion.6.total_ref, bf16[8,2048,512]{2,1,0:T(8,128)(2,1)S(1)} %get-tuple-element.265.expo_ref, f32[1,512]{1,0:T(1,128)S(1)} %multiply_add_fusion.refs_0_), custom_call_target="tpu_custom_call" | custom-call | flops 3355443200 | bytes 1048576 | tf_op jit(solution)/shard_map/row_step/pallas_call | solution.py:359
  77.4 3.6 %collective-permute-start.27 = (f32[1,8192]{1,0:T(1,128)S(1)}, f32[1,8192]{1,0:T(1,128)S(1)}, u32[]{:S(2)}, u32[]{:S(2)}) collective-permute-start(f32[1,8192]{1,0:T(1,128)S(1)} %add.133), channel_id=1, source_target_pairs={{0,2},{2,0},{16,18},{18,16},{1,3},{3,1},{17,19},{19,17},{4,6},{6,4... | collective-permute-start | bytes 98312 | tf_op jit(solution)/shard_map/ppermute | solution.py:689
  85.3 2.7 %collective-permute-start.30 = (f32[1,8192]{1,0:T(1,128)S(1)}, f32[1,8192]{1,0:T(1,128)S(1)}, u32[]{:S(2)}, u32[]{:S(2)}) collective-permute-start(f32[1,8192]{1,0:T(1,128)S(1)} %add_add_fusion.1), channel_id=1, source_target_pairs={{0,64},{32,96},{64,0},{96,32},{1,65},{33,97},{65,1},{97,33},{2,66}... | collective-permute-start | bytes 98312 | tf_op jit(solution)/shard_map/ppermute | solution.py:689
  88.0 2.2 %load_student.1 = (bf16[4608,256]{1,0:T(8,128)(2,1)S(1)}, f32[8,512]{1,0:T(8,128)S(1)}, bf16[2048,256]{1,0:T(8,128)(2,1)S(1)}, bf16[256,2048]{1,0:T(8,128)(2,1)S(1)}) custom-call(s32[4]{0:T(128)S(1)} %pad_add_fusion.place, s32[24]{0:T(128)S(1)} %get-tuple-element.250.meta, bf16[2,528,128]{2,1,0:T(8,128)(2,1)S(1)} %get-tuple-element.285.refs_0_, ...), custom_call_target="tpu_custom_call" | custom-call | flops 2147483648 | bytes 1048576 | tf_op jit(solution)/shard_map/load_student/pallas_call | solution.py:439
  90.8 3.2 %col_step.2 = f32[1,2048]{1,0:T(1,128)S(1)} custom-call(s32[24]{0:T(128)S(1)} %get-tuple-element.250.meta, f32[1,8192]{1,0:T(1,128)S(1)} %add_add_fusion.total_ref.all_ref, f32[1,4096]{1,0:T(1,128)S(1)} %get-tuple-element.301.valid_ref, bf16[8,2048,512]{2,1,0:T(8,128)(2,1)S(1)} %get-tuple-element.265.expo_ref), custom_call_target="tpu_custom_call" | custom-call | flops 3355443200 | bytes 1048576 | tf_op jit(solution)/shard_map/col_step/pallas_call | solution.py:392
  96.2 2.6 %collective-permute-start.33 = (f32[1,2048]{1,0:T(1,128)S(1)}, f32[1,2048]{1,0:T(1,128)S(1)}, u32[]{:S(2)}, u32[]{:S(2)}) collective-permute-start(f32[1,2048]{1,0:T(1,128)S(1)} %col_step.2), channel_id=1, source_target_pairs={{0,8},{4,12},{8,0},{12,4},{1,9},{5,13},{9,1},{13,5},{2,10},{6,14},... | collective-permute-start | bytes 24584 | tf_op jit(solution)/shard_map/ppermute | solution.py:689
  98.8 6.5 %student.2 = (bf16[512,256]{1,0:T(8,128)(2,1)S(1)}, bf16[512,256]{1,0:T(8,128)(2,1)S(1)}, bf16[4096,256]{1,0:T(8,128)(2,1)S(1)}) custom-call(s32[4]{0:T(128)S(1)} %pad_add_fusion.place, s32[24]{0:T(128)S(1)} %get-tuple-element.250.meta, bf16[4608,256]{1,0:T(8,128)(2,1)S(1)} %get-tuple-element.304.rows_ref, f32[1,8192]{1,0:T(1,128)S(1)} %add_add_fusion.total_ref.all_ref, ...), custom_call_target="tpu_custom_call" | custom-call | flops 6442450944 | bytes 1048576 | tf_op jit(solution)/shard_map/student/pallas_call | solution.py:499
  105.3 2.5 %row_step.4 = f32[1,4096]{1,0:T(1,128)S(1)} custom-call(s32[4]{0:T(128)S(1)} %pad_add_fusion.place, s32[24]{0:T(128)S(1)} %get-tuple-element.250.meta, f32[1,2048]{1,0:T(1,128)S(1)} %add_add_fusion.8.total_ref, bf16[8,2048,512]{2,1,0:T(8,128)(2,1)S(1)} %get-tuple-element.265.expo_ref), custom_call_target="tpu_custom_call" | custom-call | flops 3355443200 | bytes 1048576 | tf_op jit(solution)/shard_map/row_step/pallas_call | solution.py:359
  113.9 6.5 %student.3 = (bf16[512,256]{1,0:T(8,128)(2,1)S(1)}, bf16[512,256]{1,0:T(8,128)(2,1)S(1)}, bf16[4096,256]{1,0:T(8,128)(2,1)S(1)}) custom-call(s32[4]{0:T(128)S(1)} %pad_add_fusion.place, s32[24]{0:T(128)S(1)} %get-tuple-element.250.meta, bf16[4608,256]{1,0:T(8,128)(2,1)S(1)} %get-tuple-element.304.rows_ref, f32[1,8192]{1,0:T(1,128)S(1)} %add_add_fusion.total_ref.all_ref, ...), custom_call_target="tpu_custom_call" | custom-call | flops 6442450944 | bytes 1048576 | tf_op jit(solution)/shard_map/student/pallas_call | solution.py:499
  125.8 2.7 %collective-permute-done.40 = f32[1,4096]{1,0:T(1,128)S(1)} collective-permute-done((f32[1,4096]{1,0:T(1,128)S(1)}, f32[1,4096]{1,0:T(1,128)S(1)}, u32[]{:S(2)}, u32[]{:S(2)}) %collective-permute-start.40) | collective-permute-done | bytes 16416 | tf_op jit(solution)/shard_map/ppermute | solution.py:689
  128.5 3.2 %col_step.3 = f32[1,2048]{1,0:T(1,128)S(1)} custom-call(s32[24]{0:T(128)S(1)} %get-tuple-element.250.meta, f32[1,4096]{1,0:T(1,128)S(1)} %add_add_fusion.4.total_ref, f32[1,4096]{1,0:T(1,128)S(1)} %get-tuple-element.301.valid_ref, bf16[8,2048,512]{2,1,0:T(8,128)(2,1)S(1)} %get-tuple-element.265.expo_ref), custom_call_target="tpu_custom_call" | custom-call | flops 3355443200 | bytes 1048576 | tf_op jit(solution)/shard_map/col_step/pallas_call | solution.py:392
  133.6 2.8 %collective-permute-start.43 = (f32[1,2048]{1,0:T(1,128)S(1)}, f32[1,2048]{1,0:T(1,128)S(1)}, u32[]{:S(2)}, u32[]{:S(2)}) collective-permute-start(f32[1,2048]{1,0:T(1,128)S(1)} %col_step.3), channel_id=1, source_target_pairs={{0,8},{4,12},{8,0},{12,4},{1,9},{5,13},{9,1},{13,5},{2,10},{6,14},... | collective-permute-start | bytes 24584 | tf_op jit(solution)/shard_map/ppermute | solution.py:689
  138.8 2.5 %row_step.5 = f32[1,4096]{1,0:T(1,128)S(1)} custom-call(s32[4]{0:T(128)S(1)} %pad_add_fusion.place, s32[24]{0:T(128)S(1)} %get-tuple-element.250.meta, f32[1,2048]{1,0:T(1,128)S(1)} %add_add_fusion.7.total_ref.col_ref, bf16[8,2048,512]{2,1,0:T(8,128)(2,1)S(1)} %get-tuple-element.265.expo_ref), custom_call_target="tpu_custom_call" | custom-call | flops 3355443200 | bytes 1048576 | tf_op jit(solution)/shard_map/row_step/pallas_call | solution.py:359
  144.6 2.8 %collective-permute-start.47 = (f32[1,4096]{1,0:T(1,128)S(1)}, f32[1,4096]{1,0:T(1,128)S(1)}, u32[]{:S(2)}, u32[]{:S(2)}) collective-permute-start(f32[1,4096]{1,0:T(1,128)S(1)} %add.153), channel_id=1, source_target_pairs={{0,2},{2,0},{16,18},{18,16},{1,3},{3,1},{17,19},{19,17},{4,6},{6,4... | collective-permute-start | bytes 49160 | tf_op jit(solution)/shard_map/ppermute | solution.py:689
  147.3 3.5 %feature_step.2.refs_0_ = bf16[4096,256]{1,0:T(8,128)(2,1)S(1)} custom-call(s32[24]{0:T(128)S(1)} %get-tuple-element.250.meta, f32[1,2048]{1,0:T(1,128)S(1)} %add_add_fusion.7.total_ref.col_ref, bf16[8,2048,512]{2,1,0:T(8,128)(2,1)S(1)} %get-tuple-element.265.expo_ref, bf16[256,2048]{1,0:T(8,128)(2,1)S(1)} %get-tuple-element.336.turned_ref), custom_call_target="tpu_custom_call" | custom-call | flops 2147483648 | bytes 1048576 | tf_op jit(solution)/shard_map/feature_step/pallas_call | solution.py:542
  152.5 3.2 %collective-permute-start.50 = (f32[1,4096]{1,0:T(1,128)S(1)}, f32[1,4096]{1,0:T(1,128)S(1)}, u32[]{:S(2)}, u32[]{:S(2)}) collective-permute-start(f32[1,4096]{1,0:T(1,128)S(1)} %add_add_fusion.3), channel_id=1, source_target_pairs={{0,64},{32,96},{64,0},{96,32},{1,65},{33,97},{65,1},{97,33},{2,66}... | collective-permute-start | bytes 49160 | tf_op jit(solution)/shard_map/ppermute | solution.py:689
  155.7 2.5 %feature_step.3.plan_ref = bf16[4096,256]{1,0:T(8,128)(2,1)S(1)} custom-call(s32[24]{0:T(128)S(1)} %get-tuple-element.250.meta, f32[1,2048]{1,0:T(1,128)S(1)} %add_add_fusion.7.total_ref.col_ref, bf16[8,2048,512]{2,1,0:T(8,128)(2,1)S(1)} %get-tuple-element.265.expo_ref, ...), custom_call_target="tpu_custom_call", output_to_operand_aliasing={{}: (4, {})} | custom-call | flops 2147483648 | bytes 1048576 | tf_op jit(solution)/shard_map/feature_step/pallas_call | solution.py:542
  158.3 2.6 %join_step.1 = (bf16[16,128,256]{2,1,0:T(8,128)(2,1)S(1)}, bf16[16,128,256]{2,1,0:T(8,128)(2,1)S(1)}) custom-call(s32[4]{0:T(128)S(1)} %pad_add_fusion.place, s32[24]{0:T(128)S(1)} %get-tuple-element.250.meta, f32[1,4096]{1,0:T(1,128)S(1)} %add_add_fusion.2.total_ref, f32[1,4096]{1,0:T(1,128)S(1)} %get-tuple-element.301.valid_ref, ...), custom_call_target="tpu_custom_call" | custom-call | flops 2147483648 | bytes 1048576 | tf_op jit(solution)/shard_map/join_step/pallas_call | solution.py:586
  161.0 5.3 %grad_step.1 = (bf16[512,256]{1,0:T(8,128)(2,1)S(1)}, bf16[512,256]{1,0:T(8,128)(2,1)S(1)}, bf16[512,256]{1,0:T(8,128)(2,1)S(1)}, bf16[512,256]{1,0:T(8,128)(2,1)S(1)}) custom-call(s32[4]{0:T(128)S(1)} %pad_add_fusion.place, s32[24]{0:T(128)S(1)} %get-tuple-element.250.meta, f32[1,4096]{1,0:T(1,128)S(1)} %add_add_fusion.2.total_ref, ...), custom_call_target="tpu_custom_call" | custom-call | flops 4294967296 | bytes 1048576 | tf_op jit(solution)/shard_map/grad_step/pallas_call | solution.py:627
  167.7 5.2 %all-to-all-start = ((bf16[16,128,256]{2,1,0:T(8,128)(2,1)}), bf16[16,128,256]{2,1,0:T(8,128)(2,1)S(1)}, u32[]{:S(2)}, u32[]{:S(2)}) async-start(bf16[16,128,256]{2,1,0:T(8,128)(2,1)} %add_convert_fusion), calls=%async_computation | async-start | bytes 2097152 | tf_op jit(solution)/shard_map/all_to_all | solution.py:648
  172.9 2.1 %collective-permute-start.54 = (bf16[512,256]{1,0:T(8,128)(2,1)S(1)}, bf16[512,256]{1,0:T(8,128)(2,1)S(1)}, u32[]{:S(2)}, u32[]{:S(2)}) collective-permute-start(bf16[512,256]{1,0:T(8,128)(2,1)S(1)} %get-tuple-element.365), channel_id=1, source_target_pairs={{0,4},{4,0},{8,12},{12,8},{1,5},{5,1},{9,13},{13,9},{2,6},{6,2},{1... | collective-permute-start | bytes 786440 | tf_op jit(solution)/shard_map/ppermute | solution.py:644
  178.3 3.7 %collective-permute-done.54 = bf16[512,256]{1,0:T(8,128)(2,1)S(1)} collective-permute-done((bf16[512,256]{1,0:T(8,128)(2,1)S(1)}, bf16[512,256]{1,0:T(8,128)(2,1)S(1)}, u32[]{:S(2)}, u32[]{:S(2)}) %collective-permute-start.54) | collective-permute-done | bytes 262176 | tf_op jit(solution)/shard_map/ppermute | solution.py:644
  182.1 7.9 %collective-permute-done.55 = bf16[512,256]{1,0:T(8,128)(2,1)S(1)} collective-permute-done((bf16[512,256]{1,0:T(8,128)(2,1)S(1)}, bf16[512,256]{1,0:T(8,128)(2,1)S(1)}, u32[]{:S(2)}, u32[]{:S(2)}) %collective-permute-start.55) | collective-permute-done | bytes 262176 | tf_op jit(solution)/shard_map/ppermute | solution.py:644
  (139 shorter events, 62.6 us)
Async XLA Ops:
  3.0 11.1 %collective-permute-start = (bf16[528,128]{1,0:T(8,128)(2,1)S(1)}, bf16[528,128]{1,0:T(8,128)(2,1)S(1)}, u32[]{:S(2)}, u32[]{:S(2)}) collective-permute-start(bf16[528,128]{1,0:T(8,128)(2,1)S(1)} %get-tuple-element.188), channel_id=1, source_target_pairs={{0,16},{16,0},{1,17},{17,1},{2,18},{18,2},{3,19},{19,3},{4,20},{20... | collective-permute-start | bytes 405512 | tf_op jit(solution)/shard_map/ppermute | solution.py:640
  4.7 9.4 %collective-permute-start.1 = (bf16[528,128]{1,0:T(8,128)(2,1)S(1)}, bf16[528,128]{1,0:T(8,128)(2,1)S(1)}, u32[]{:S(2)}, u32[]{:S(2)}) collective-permute-start(bf16[528,128]{1,0:T(8,128)(2,1)S(1)} %get-tuple-element.189), channel_id=1, source_target_pairs={{0,16},{16,0},{1,17},{17,1},{2,18},{18,2},{3,19},{19,3},{4,20},{20... | collective-permute-start | bytes 405512 | tf_op jit(solution)/shard_map/ppermute | solution.py:640
  15.3 14.2 %collective-permute-start.5 = (bf16[2,528,128]{2,1,0:T(8,128)(2,1)S(1)}, bf16[2,528,128]{2,1,0:T(8,128)(2,1)S(1)}, u32[]{:S(2)}, u32[]{:S(2)}) collective-permute-start(bf16[2,528,128]{2,1,0:T(8,128)(2,1)S(1)} %pad_maximum_fusion.1.refs_0_), channel_id=1, source_target_pairs={{0,64},{32,96},{64,0},{96,32},{1,65},{33,97},{65,1},{97,33},{2,66}... | collective-permute-start | bytes 811016 | tf_op jit(solution)/shard_map/ppermute | solution.py:644
  18.6 12.6 %collective-permute-start.4 = (bf16[2,528,128]{2,1,0:T(8,128)(2,1)S(1)}, bf16[2,528,128]{2,1,0:T(8,128)(2,1)S(1)}, u32[]{:S(2)}, u32[]{:S(2)}) collective-permute-start(bf16[2,528,128]{2,1,0:T(8,128)(2,1)S(1)} %pad_maximum_fusion.1.refs_0_), channel_id=1, source_target_pairs={{0,96},{32,64},{64,32},{96,0},{1,97},{33,65},{65,33},{97,1},{2,98}... | collective-permute-start | bytes 811016 | tf_op jit(solution)/shard_map/ppermute | solution.py:644
  19.7 12.0 %collective-permute-start.3 = (bf16[2,528,128]{2,1,0:T(8,128)(2,1)S(1)}, bf16[2,528,128]{2,1,0:T(8,128)(2,1)S(1)}, u32[]{:S(2)}, u32[]{:S(2)}) collective-permute-start(bf16[2,528,128]{2,1,0:T(8,128)(2,1)S(1)} %pad_maximum_fusion.1.refs_0_), channel_id=1, source_target_pairs={{0,32},{32,0},{64,96},{96,64},{1,33},{33,1},{65,97},{97,65},{2,34}... | collective-permute-start | bytes 811016 | tf_op jit(solution)/shard_map/ppermute | solution.py:644
  19.7 9.8 %collective-permute-start.6 = (f32[1,512]{1,0:T(1,128)S(1)}, f32[1,512]{1,0:T(1,128)S(1)}, u32[]{:S(2)}, u32[]{:S(2)}) collective-permute-start(f32[1,512]{1,0:T(1,128)S(1)} %max.27), channel_id=1, source_target_pairs={{0,2},{2,0},{1,3},{3,1},{4,6},{6,4},{5,7},{7,5},{8,10},{10,8},{9,1... | collective-permute-start | bytes 6152 | tf_op jit(solution)/shard_map/ppermute | solution.py:640
  36.3 13.0 %collective-permute-start.14 = (f32[2,1,512]{2,1,0:T(1,128)S(1)}, f32[2,1,512]{2,1,0:T(1,128)S(1)}, u32[]{:S(2)}, u32[]{:S(2)}) collective-permute-start(f32[2,1,512]{2,1,0:T(1,128)S(1)} %pad_maximum_fusion.3.refs_8_), channel_id=1, source_target_pairs={{0,64},{32,96},{64,0},{96,32},{1,65},{33,97},{65,1},{97,33},{2,66}... | collective-permute-start | bytes 12296 | tf_op jit(solution)/shard_map/ppermute | solution.py:644
  38.4 10.9 %collective-permute-start.13 = (f32[2,1,512]{2,1,0:T(1,128)S(1)}, f32[2,1,512]{2,1,0:T(1,128)S(1)}, u32[]{:S(2)}, u32[]{:S(2)}) collective-permute-start(f32[2,1,512]{2,1,0:T(1,128)S(1)} %pad_maximum_fusion.3.refs_8_), channel_id=1, source_target_pairs={{0,96},{32,64},{64,32},{96,0},{1,97},{33,65},{65,33},{97,1},{2,98}... | collective-permute-start | bytes 12296 | tf_op jit(solution)/shard_map/ppermute | solution.py:644
  40.4 8.9 %collective-permute-start.12 = (f32[2,1,512]{2,1,0:T(1,128)S(1)}, f32[2,1,512]{2,1,0:T(1,128)S(1)}, u32[]{:S(2)}, u32[]{:S(2)}) collective-permute-start(f32[2,1,512]{2,1,0:T(1,128)S(1)} %pad_maximum_fusion.3.refs_8_), channel_id=1, source_target_pairs={{0,32},{32,0},{64,96},{96,64},{1,33},{33,1},{65,97},{97,65},{2,34}... | collective-permute-start | bytes 12296 | tf_op jit(solution)/shard_map/ppermute | solution.py:644
  40.4 8.8 %collective-permute-start.15 = (bf16[2,528,128]{2,1,0:T(8,128)(2,1)S(1)}, bf16[2,528,128]{2,1,0:T(8,128)(2,1)S(1)}, u32[]{:S(2)}, u32[]{:S(2)}) collective-permute-start(bf16[2,528,128]{2,1,0:T(8,128)(2,1)S(1)} %pad_maximum_fusion.2), channel_id=1, source_target_pairs={{0,32},{32,0},{64,96},{96,64},{1,33},{33,1},{65,97},{97,65},{2,34}... | collective-permute-start | bytes 811016 | tf_op jit(solution)/shard_map/ppermute | solution.py:644
  50.7 11.1 %collective-permute-start.17 = (f32[2,1,512]{2,1,0:T(1,128)S(1)}, f32[2,1,512]{2,1,0:T(1,128)S(1)}, u32[]{:S(2)}, u32[]{:S(2)}) collective-permute-start(f32[2,1,512]{2,1,0:T(1,128)S(1)} %pad_maximum_fusion.5), channel_id=1, source_target_pairs={{0,2},{2,0},{1,3},{3,1},{4,6},{6,4},{5,7},{7,5},{8,10},{10,8},{9,1... | collective-permute-start | bytes 12296 | tf_op jit(solution)/shard_map/ppermute | solution.py:640
  53.8 17.3 %collective-permute-start.21 = (bf16[2,2,528,128]{3,2,1,0:T(8,128)(2,1)S(1)}, bf16[2,2,528,128]{3,2,1,0:T(8,128)(2,1)S(1)}, u32[]{:S(2)}, u32[]{:S(2)}) collective-permute-start(bf16[2,2,528,128]{3,2,1,0:T(8,128)(2,1)S(1)} %pad_maximum_fusion), channel_id=1, source_target_pairs={{0,96},{32,64},{64,32},{96,0},{1,97},{33,65},{65,33},{97,1},{2,98}... | collective-permute-start | bytes 1622024 | tf_op jit(solution)/shard_map/ppermute | solution.py:644
  61.8 5.8 %collective-permute-start.20 = (f32[1,2176]{1,0:T(1,128)S(1)}, f32[1,2176]{1,0:T(1,128)S(1)}, u32[]{:S(2)}, u32[]{:S(2)}) collective-permute-start(f32[1,2176]{1,0:T(1,128)S(1)} %get-tuple-element.257), channel_id=1, source_target_pairs={{0,12},{4,8},{8,4},{12,0},{1,13},{5,9},{9,5},{13,1},{2,14},{6,10},... | collective-permute-start | bytes 26120 | tf_op jit(solution)/shard_map/ppermute | solution.py:689
  77.4 5.8 %collective-permute-start.27 = (f32[1,8192]{1,0:T(1,128)S(1)}, f32[1,8192]{1,0:T(1,128)S(1)}, u32[]{:S(2)}, u32[]{:S(2)}) collective-permute-start(f32[1,8192]{1,0:T(1,128)S(1)} %add.133), channel_id=1, source_target_pairs={{0,2},{2,0},{16,18},{18,16},{1,3},{3,1},{17,19},{19,17},{4,6},{6,4... | collective-permute-start | bytes 98312 | tf_op jit(solution)/shard_map/ppermute | solution.py:689
  83.2 7.0 %collective-permute-start.32 = (f32[1,8192]{1,0:T(1,128)S(1)}, f32[1,8192]{1,0:T(1,128)S(1)}, u32[]{:S(2)}, u32[]{:S(2)}) collective-permute-start(f32[1,8192]{1,0:T(1,128)S(1)} %add_add_fusion.1), channel_id=1, source_target_pairs={{0,96},{32,64},{64,32},{96,0},{1,97},{33,65},{65,33},{97,1},{2,98}... | collective-permute-start | bytes 98312 | tf_op jit(solution)/shard_map/ppermute | solution.py:689
  85.3 5.4 %collective-permute-start.30 = (f32[1,8192]{1,0:T(1,128)S(1)}, f32[1,8192]{1,0:T(1,128)S(1)}, u32[]{:S(2)}, u32[]{:S(2)}) collective-permute-start(f32[1,8192]{1,0:T(1,128)S(1)} %add_add_fusion.1), channel_id=1, source_target_pairs={{0,64},{32,96},{64,0},{96,32},{1,65},{33,97},{65,1},{97,33},{2,66}... | collective-permute-start | bytes 98312 | tf_op jit(solution)/shard_map/ppermute | solution.py:689
  94.0 11.3 %collective-permute-start.35 = (f32[1,2048]{1,0:T(1,128)S(1)}, f32[1,2048]{1,0:T(1,128)S(1)}, u32[]{:S(2)}, u32[]{:S(2)}) collective-permute-start(f32[1,2048]{1,0:T(1,128)S(1)} %col_step.2), channel_id=1, source_target_pairs={{0,12},{4,8},{8,4},{12,0},{1,13},{5,9},{9,5},{13,1},{2,14},{6,10},... | collective-permute-start | bytes 24584 | tf_op jit(solution)/shard_map/ppermute | solution.py:689
  95.6 9.7 %collective-permute-start.34 = (f32[1,2048]{1,0:T(1,128)S(1)}, f32[1,2048]{1,0:T(1,128)S(1)}, u32[]{:S(2)}, u32[]{:S(2)}) collective-permute-start(f32[1,2048]{1,0:T(1,128)S(1)} %col_step.2), channel_id=1, source_target_pairs={{0,4},{4,0},{8,12},{12,8},{1,5},{5,1},{9,13},{13,9},{2,6},{6,2},{1... | collective-permute-start | bytes 24584 | tf_op jit(solution)/shard_map/ppermute | solution.py:689
  96.2 9.1 %collective-permute-start.33 = (f32[1,2048]{1,0:T(1,128)S(1)}, f32[1,2048]{1,0:T(1,128)S(1)}, u32[]{:S(2)}, u32[]{:S(2)}) collective-permute-start(f32[1,2048]{1,0:T(1,128)S(1)} %col_step.2), channel_id=1, source_target_pairs={{0,8},{4,12},{8,0},{12,4},{1,9},{5,13},{9,1},{13,5},{2,10},{6,14},... | collective-permute-start | bytes 24584 | tf_op jit(solution)/shard_map/ppermute | solution.py:689
  109.1 11.3 %collective-permute-start.39 = (f32[1,4096]{1,0:T(1,128)S(1)}, f32[1,4096]{1,0:T(1,128)S(1)}, u32[]{:S(2)}, u32[]{:S(2)}) collective-permute-start(f32[1,4096]{1,0:T(1,128)S(1)} %add.143), channel_id=1, source_target_pairs={{0,18},{2,16},{16,2},{18,0},{1,19},{3,17},{17,3},{19,1},{4,22},{6,... | collective-permute-start | bytes 49160 | tf_op jit(solution)/shard_map/ppermute | solution.py:689
  110.9 9.5 %collective-permute-start.38 = (f32[1,4096]{1,0:T(1,128)S(1)}, f32[1,4096]{1,0:T(1,128)S(1)}, u32[]{:S(2)}, u32[]{:S(2)}) collective-permute-start(f32[1,4096]{1,0:T(1,128)S(1)} %add.143), channel_id=1, source_target_pairs={{0,16},{2,18},{16,0},{18,2},{1,17},{3,19},{17,1},{19,3},{4,20},{6,... | collective-permute-start | bytes 49160 | tf_op jit(solution)/shard_map/ppermute | solution.py:689
  112.3 8.1 %collective-permute-start.37 = (f32[1,4096]{1,0:T(1,128)S(1)}, f32[1,4096]{1,0:T(1,128)S(1)}, u32[]{:S(2)}, u32[]{:S(2)}) collective-permute-start(f32[1,4096]{1,0:T(1,128)S(1)} %add.143), channel_id=1, source_target_pairs={{0,2},{2,0},{16,18},{18,16},{1,3},{3,1},{17,19},{19,17},{4,6},{6,4... | collective-permute-start | bytes 49160 | tf_op jit(solution)/shard_map/ppermute | solution.py:689
  142.6 8.3 %collective-permute-start.49 = (f32[1,4096]{1,0:T(1,128)S(1)}, f32[1,4096]{1,0:T(1,128)S(1)}, u32[]{:S(2)}, u32[]{:S(2)}) collective-permute-start(f32[1,4096]{1,0:T(1,128)S(1)} %add.153), channel_id=1, source_target_pairs={{0,18},{2,16},{16,2},{18,0},{1,19},{3,17},{17,3},{19,1},{4,22},{6,... | collective-permute-start | bytes 49160 | tf_op jit(solution)/shard_map/ppermute | solution.py:689
  144.4 6.5 %collective-permute-start.48 = (f32[1,4096]{1,0:T(1,128)S(1)}, f32[1,4096]{1,0:T(1,128)S(1)}, u32[]{:S(2)}, u32[]{:S(2)}) collective-permute-start(f32[1,4096]{1,0:T(1,128)S(1)} %add.153), channel_id=1, source_target_pairs={{0,16},{2,18},{16,0},{18,2},{1,17},{3,19},{17,1},{19,3},{4,20},{6,... | collective-permute-start | bytes 49160 | tf_op jit(solution)/shard_map/ppermute | solution.py:689
  144.6 6.3 %collective-permute-start.47 = (f32[1,4096]{1,0:T(1,128)S(1)}, f32[1,4096]{1,0:T(1,128)S(1)}, u32[]{:S(2)}, u32[]{:S(2)}) collective-permute-start(f32[1,4096]{1,0:T(1,128)S(1)} %add.153), channel_id=1, source_target_pairs={{0,2},{2,0},{16,18},{18,16},{1,3},{3,1},{17,19},{19,17},{4,6},{6,4... | collective-permute-start | bytes 49160 | tf_op jit(solution)/shard_map/ppermute | solution.py:689
  150.9 7.3 %collective-permute-start.52 = (f32[1,4096]{1,0:T(1,128)S(1)}, f32[1,4096]{1,0:T(1,128)S(1)}, u32[]{:S(2)}, u32[]{:S(2)}) collective-permute-start(f32[1,4096]{1,0:T(1,128)S(1)} %add_add_fusion.3), channel_id=1, source_target_pairs={{0,96},{32,64},{64,32},{96,0},{1,97},{33,65},{65,33},{97,1},{2,98}... | collective-permute-start | bytes 49160 | tf_op jit(solution)/shard_map/ppermute | solution.py:689
  152.3 5.9 %collective-permute-start.51 = (f32[1,4096]{1,0:T(1,128)S(1)}, f32[1,4096]{1,0:T(1,128)S(1)}, u32[]{:S(2)}, u32[]{:S(2)}) collective-permute-start(f32[1,4096]{1,0:T(1,128)S(1)} %add_add_fusion.3), channel_id=1, source_target_pairs={{0,32},{32,0},{64,96},{96,64},{1,33},{33,1},{65,97},{97,65},{2,34}... | collective-permute-start | bytes 49160 | tf_op jit(solution)/shard_map/ppermute | solution.py:689
  152.5 5.8 %collective-permute-start.50 = (f32[1,4096]{1,0:T(1,128)S(1)}, f32[1,4096]{1,0:T(1,128)S(1)}, u32[]{:S(2)}, u32[]{:S(2)}) collective-permute-start(f32[1,4096]{1,0:T(1,128)S(1)} %add_add_fusion.3), channel_id=1, source_target_pairs={{0,64},{32,96},{64,0},{96,32},{1,65},{33,97},{65,1},{97,33},{2,66}... | collective-permute-start | bytes 49160 | tf_op jit(solution)/shard_map/ppermute | solution.py:689
  167.7 23.2 %all-to-all-start = ((bf16[16,128,256]{2,1,0:T(8,128)(2,1)}), bf16[16,128,256]{2,1,0:T(8,128)(2,1)S(1)}, u32[]{:S(2)}, u32[]{:S(2)}) async-start(bf16[16,128,256]{2,1,0:T(8,128)(2,1)} %add_convert_fusion), calls=%async_computation | async-start | bytes 2097152 | tf_op jit(solution)/shard_map/all_to_all | solution.py:648
  172.9 9.2 %collective-permute-start.54 = (bf16[512,256]{1,0:T(8,128)(2,1)S(1)}, bf16[512,256]{1,0:T(8,128)(2,1)S(1)}, u32[]{:S(2)}, u32[]{:S(2)}) collective-permute-start(bf16[512,256]{1,0:T(8,128)(2,1)S(1)} %get-tuple-element.365), channel_id=1, source_target_pairs={{0,4},{4,0},{8,12},{12,8},{1,5},{5,1},{9,13},{13,9},{2,6},{6,2},{1... | collective-permute-start | bytes 786440 | tf_op jit(solution)/shard_map/ppermute | solution.py:644
  175.0 15.0 %collective-permute-start.55 = (bf16[512,256]{1,0:T(8,128)(2,1)S(1)}, bf16[512,256]{1,0:T(8,128)(2,1)S(1)}, u32[]{:S(2)}, u32[]{:S(2)}) collective-permute-start(bf16[512,256]{1,0:T(8,128)(2,1)S(1)} %get-tuple-element.366), channel_id=1, source_target_pairs={{0,12},{4,8},{8,4},{12,0},{1,13},{5,9},{9,5},{13,1},{2,14},{6,10},... | collective-permute-start | bytes 786440 | tf_op jit(solution)/shard_map/ppermute | solution.py:644
  176.3 13.7 %collective-permute-start.56 = (bf16[512,256]{1,0:T(8,128)(2,1)S(1)}, bf16[512,256]{1,0:T(8,128)(2,1)S(1)}, u32[]{:S(2)}, u32[]{:S(2)}) collective-permute-start(bf16[512,256]{1,0:T(8,128)(2,1)S(1)} %get-tuple-element.367), channel_id=1, source_target_pairs={{0,8},{4,12},{8,0},{12,4},{1,9},{5,13},{9,1},{13,5},{2,10},{6,14},... | collective-permute-start | bytes 786440 | tf_op jit(solution)/shard_map/ppermute | solution.py:644
  (27 other events, 97.3 us)

commit v2 on v1

--- a/solution.py
+++ b/solution.py
@@ -681,7 +681,7 @@
     return jnp.where(first, one, two), jnp.where(first, two, one)
 
 
-RINGS = {"x": (("xl", "xh"), (1, 2, 3)), "y": ("y", (2, 1, 3)), "z": ("z", (2, 1, 3))}
+RINGS = {"x": (("xl", "xh"), (2, 3, 1)), "y": ("y", (1, 3, 2)), "z": ("z", (1, 3, 2))}
 
 
 def ring(value, name):

time: 192 us -> 187 us (0.974)
  starting transfers between devices: 77.3 us -> 68 us
  waiting for transfers between devices: 33.4 us -> 37.1 us
    ppermute x27, starting transfers between devices: 43.9 us -> 34.7 us  [ring(): lax.ppermute(value, axes, [(i, i ^ mask) for i in range(4)])]
    ppermute x27, waiting for transfers between devices: 11.9 us -> 17 us  [ring(): lax.ppermute(value, axes, [(i, i ^ mask) for i in range(4)])]
  transfers between devices with their start and end apart: 58 -> 58, of which waited for: 23 -> 24; matrix products, arithmetic and copies ran while one was open for 1% -> 1% of each run, Pallas kernels for 30% -> 31%
where the time goes in v2:
time: 187 us; the launch traced here: 186 us
  Pallas kernels  73.9 us (40%)
  starting transfers between devices  68 us (36%)
  waiting for transfers between devices  37.1 us (20%)
  other arithmetic  3.74 us (2%)
  between operations  1.92 us (1%)
    ppermute x27, starting transfers between devices, ring(): lax.ppermute(value, axes, [(i, i ^ mask) for i in range(4)])  34.7 us
    ppermute x27, waiting for transfers between devices, ring(): lax.ppermute(value, axes, [(i, i ^ mask) for i in range(4)])  17 us
    ppermute x11, starting transfers between devices, from_xor(): return lax.ppermute(value, axis, [(i, i ^ mask) for i in range(4)])  15.9 us
    pallas_call x2, Pallas kernels, row_soft(): pl.pallas_call(soft_kernel, grid=(steps,), out_shape=(jax.ShapeDtypeStruc...  13.6 us
    pallas_call x2, Pallas kernels, student_step(): pl.pallas_call(functools.partial(student_kernel, part), out_shape=outs, i...  13 us
    ppermute x11, waiting for transfers between devices, from_xor(): return lax.ppermute(value, axis, [(i, i ^ mask) for i in range(4)])  12.4 us
    ppermute x19, starting transfers between devices, swap(): return lax.ppermute(value, axis, [(0, 1), (1, 0)])  12.3 us
    pallas_call x1, Pallas kernels, row_max(): pl.pallas_call(max_kernel, grid=(steps,), out_shape=jax.ShapeDtypeStruct(...  8.93 us
  transfers between devices with their start and end apart: 58, of which 24 were waited for; matrix products, arithmetic and copies ran while one was open for 1% of the time, Pallas kernels for 31%

profile of v2, /device:TPU:0, one launch (start us, length us, event | category | flops | bytes accessed | tf_op | source)
XLA Modules:
  0.0 185.9 jit_solution(8016089369163844676)
XLA Ops:
  5.1 8.9 %row_max.1 = f32[1,512]{1,0:T(1,128)S(1)} custom-call(bf16[528,256]{1,0:T(8,128)(2,1)S(1)} %get-tuple-element.190.teach_ref, bf16[16384,256]{1,0:T(8,128)(2,1)} %refs_8_.1), custom_call_target="tpu_custom_call" | custom-call | flops 4294967296 | bytes 1048576 | tf_op jit(solution)/shard_map/row_max/pallas_call | solution.py:137
  15.3 3.3 %collective-permute-start.5 = (bf16[2,528,128]{2,1,0:T(8,128)(2,1)S(1)}, bf16[2,528,128]{2,1,0:T(8,128)(2,1)S(1)}, u32[]{:S(2)}, u32[]{:S(2)}) collective-permute-start(bf16[2,528,128]{2,1,0:T(8,128)(2,1)S(1)} %pad_maximum_fusion.1.refs_0_), channel_id=1, source_target_pairs={{0,64},{32,96},{64,0},{96,32},{1,65},{33,97},{65,1},{97,33},{2,66}... | collective-permute-start | bytes 811016 | tf_op jit(solution)/shard_map/ppermute | solution.py:644
  19.7 3.0 %collective-permute-start.6 = (f32[1,512]{1,0:T(1,128)S(1)}, f32[1,512]{1,0:T(1,128)S(1)}, u32[]{:S(2)}, u32[]{:S(2)}) collective-permute-start(f32[1,512]{1,0:T(1,128)S(1)} %max.27), channel_id=1, source_target_pairs={{0,2},{2,0},{1,3},{3,1},{4,6},{6,4},{5,7},{7,5},{8,10},{10,8},{9,1... | collective-permute-start | bytes 6152 | tf_op jit(solution)/shard_map/ppermute | solution.py:640
  22.7 6.8 %row_soft.2 = (f32[1,512]{1,0:T(1,128)S(1)}, f32[1,512]{1,0:T(1,128)S(1)}) custom-call(bf16[528,256]{1,0:T(8,128)(2,1)S(1)} %get-tuple-element.224.feat_ref, bf16[16384,256]{1,0:T(8,128)(2,1)} %refs_8_.1), custom_call_target="tpu_custom_call" | custom-call | flops 3221225472 | bytes 1048576 | tf_op jit(solution)/shard_map/row_soft/pallas_call | solution.py:180
  36.3 2.1 %collective-permute-start.14 = (f32[2,1,512]{2,1,0:T(1,128)S(1)}, f32[2,1,512]{2,1,0:T(1,128)S(1)}, u32[]{:S(2)}, u32[]{:S(2)}) collective-permute-start(f32[2,1,512]{2,1,0:T(1,128)S(1)} %pad_maximum_fusion.3.refs_8_), channel_id=1, source_target_pairs={{0,64},{32,96},{64,0},{96,32},{1,65},{33,97},{65,1},{97,33},{2,66}... | collective-permute-start | bytes 12296 | tf_op jit(solution)/shard_map/ppermute | solution.py:644
  42.5 6.8 %row_soft.3 = (f32[1,512]{1,0:T(1,128)S(1)}, f32[1,512]{1,0:T(1,128)S(1)}) custom-call(bf16[528,256]{1,0:T(8,128)(2,1)S(1)} %get-tuple-element.224.feat_ref, bf16[16384,256]{1,0:T(8,128)(2,1)} %refs_8_.1), custom_call_target="tpu_custom_call" | custom-call | flops 3221225472 | bytes 1048576 | tf_op jit(solution)/shard_map/row_soft/pallas_call | solution.py:180
  50.7 3.1 %collective-permute-start.17 = (f32[2,1,512]{2,1,0:T(1,128)S(1)}, f32[2,1,512]{2,1,0:T(1,128)S(1)}, u32[]{:S(2)}, u32[]{:S(2)}) collective-permute-start(f32[2,1,512]{2,1,0:T(1,128)S(1)} %pad_maximum_fusion.5), channel_id=1, source_target_pairs={{0,2},{2,0},{1,3},{3,1},{4,6},{6,4},{5,7},{7,5},{8,10},{10,8},{9,1... | collective-permute-start | bytes 12296 | tf_op jit(solution)/shard_map/ppermute | solution.py:640
  55.0 6.7 %expo.1 = (bf16[8,2048,512]{2,1,0:T(8,128)(2,1)S(1)}, f32[1,2176]{1,0:T(1,128)S(1)}, f32[1,4096]{1,0:T(1,128)S(1)}, s32[24]{0:T(128)S(1)}) custom-call(s32[4]{0:T(128)S(1)} %pad_add_fusion.place, bf16[2,528,128]{2,1,0:T(8,128)(2,1)S(1)} %pad_maximum_fusion.1.refs_0_, bf16[2,528,128]{2,1,0:T(8,128)(2,1)S(1)} %collective-permute-done.3.refs_1_, ...), custom_call_target="tpu_custom_call" | custom-call | flops 4294967296 | bytes 1048576 | tf_op jit(solution)/shard_map/expo/pallas_call | solution.py:306
  61.8 4.0 %collective-permute-start.20 = (f32[1,2176]{1,0:T(1,128)S(1)}, f32[1,2176]{1,0:T(1,128)S(1)}, u32[]{:S(2)}, u32[]{:S(2)}) collective-permute-start(f32[1,2176]{1,0:T(1,128)S(1)} %get-tuple-element.257), channel_id=1, source_target_pairs={{0,8},{4,12},{8,0},{12,4},{1,9},{5,13},{9,1},{13,5},{2,10},{6,14},... | collective-permute-start | bytes 26120 | tf_op jit(solution)/shard_map/ppermute | solution.py:689
  67.4 3.2 %collective-permute-done.19 = f32[1,2176]{1,0:T(1,128)S(1)} collective-permute-done((f32[1,2176]{1,0:T(1,128)S(1)}, f32[1,2176]{1,0:T(1,128)S(1)}, u32[]{:S(2)}, u32[]{:S(2)}) %collective-permute-start.19) | collective-permute-done | bytes 8736 | tf_op jit(solution)/shard_map/ppermute | solution.py:689
  71.8 2.5 %row_step.3 = f32[1,8192]{1,0:T(1,128)S(1)} custom-call(s32[4]{0:T(128)S(1)} %pad_add_fusion.place, s32[24]{0:T(128)S(1)} %get-tuple-element.250.meta, f32[1,2176]{1,0:T(1,128)S(1)} %add_add_fusion.6.total_ref, bf16[8,2048,512]{2,1,0:T(8,128)(2,1)S(1)} %get-tuple-element.265.expo_ref, f32[1,512]{1,0:T(1,128)S(1)} %multiply_add_fusion.refs_0_), custom_call_target="tpu_custom_call" | custom-call | flops 3355443200 | bytes 1048576 | tf_op jit(solution)/shard_map/row_step/pallas_call | solution.py:359
  76.3 2.8 %collective-permute-start.28 = (f32[1,8192]{1,0:T(1,128)S(1)}, f32[1,8192]{1,0:T(1,128)S(1)}, u32[]{:S(2)}, u32[]{:S(2)}) collective-permute-start(f32[1,8192]{1,0:T(1,128)S(1)} %add.133), channel_id=1, source_target_pairs={{0,18},{2,16},{16,2},{18,0},{1,19},{3,17},{17,3},{19,1},{4,22},{6,... | collective-permute-start | bytes 98312 | tf_op jit(solution)/shard_map/ppermute | solution.py:689
  86.6 2.2 %load_student.1 = (bf16[4608,256]{1,0:T(8,128)(2,1)S(1)}, f32[8,512]{1,0:T(8,128)S(1)}, bf16[2048,256]{1,0:T(8,128)(2,1)S(1)}, bf16[256,2048]{1,0:T(8,128)(2,1)S(1)}) custom-call(s32[4]{0:T(128)S(1)} %pad_add_fusion.place, s32[24]{0:T(128)S(1)} %get-tuple-element.250.meta, bf16[2,528,128]{2,1,0:T(8,128)(2,1)S(1)} %get-tuple-element.285.refs_0_, ...), custom_call_target="tpu_custom_call" | custom-call | flops 2147483648 | bytes 1048576 | tf_op jit(solution)/shard_map/load_student/pallas_call | solution.py:439
  90.0 3.2 %col_step.2 = f32[1,2048]{1,0:T(1,128)S(1)} custom-call(s32[24]{0:T(128)S(1)} %get-tuple-element.250.meta, f32[1,8192]{1,0:T(1,128)S(1)} %add_add_fusion.total_ref.all_ref, f32[1,4096]{1,0:T(1,128)S(1)} %get-tuple-element.301.valid_ref, bf16[8,2048,512]{2,1,0:T(8,128)(2,1)S(1)} %get-tuple-element.265.expo_ref), custom_call_target="tpu_custom_call" | custom-call | flops 3355443200 | bytes 1048576 | tf_op jit(solution)/shard_map/col_step/pallas_call | solution.py:392
  96.8 6.5 %student.2 = (bf16[512,256]{1,0:T(8,128)(2,1)S(1)}, bf16[512,256]{1,0:T(8,128)(2,1)S(1)}, bf16[4096,256]{1,0:T(8,128)(2,1)S(1)}) custom-call(s32[4]{0:T(128)S(1)} %pad_add_fusion.place, s32[24]{0:T(128)S(1)} %get-tuple-element.250.meta, bf16[4608,256]{1,0:T(8,128)(2,1)S(1)} %get-tuple-element.304.rows_ref, f32[1,8192]{1,0:T(1,128)S(1)} %add_add_fusion.total_ref.all_ref, ...), custom_call_target="tpu_custom_call" | custom-call | flops 6442450944 | bytes 1048576 | tf_op jit(solution)/shard_map/student/pallas_call | solution.py:499
  103.3 2.5 %row_step.4 = f32[1,4096]{1,0:T(1,128)S(1)} custom-call(s32[4]{0:T(128)S(1)} %pad_add_fusion.place, s32[24]{0:T(128)S(1)} %get-tuple-element.250.meta, f32[1,2048]{1,0:T(1,128)S(1)} %add_add_fusion.8.total_ref, bf16[8,2048,512]{2,1,0:T(8,128)(2,1)S(1)} %get-tuple-element.265.expo_ref), custom_call_target="tpu_custom_call" | custom-call | flops 3355443200 | bytes 1048576 | tf_op jit(solution)/shard_map/row_step/pallas_call | solution.py:359
  108.0 2.1 %collective-permute-start.38 = (f32[1,4096]{1,0:T(1,128)S(1)}, f32[1,4096]{1,0:T(1,128)S(1)}, u32[]{:S(2)}, u32[]{:S(2)}) collective-permute-start(f32[1,4096]{1,0:T(1,128)S(1)} %add.143), channel_id=1, source_target_pairs={{0,18},{2,16},{16,2},{18,0},{1,19},{3,17},{17,3},{19,1},{4,22},{6,... | collective-permute-start | bytes 49160 | tf_op jit(solution)/shard_map/ppermute | solution.py:689
  110.7 6.5 %student.3 = (bf16[512,256]{1,0:T(8,128)(2,1)S(1)}, bf16[512,256]{1,0:T(8,128)(2,1)S(1)}, bf16[4096,256]{1,0:T(8,128)(2,1)S(1)}) custom-call(s32[4]{0:T(128)S(1)} %pad_add_fusion.place, s32[24]{0:T(128)S(1)} %get-tuple-element.250.meta, bf16[4608,256]{1,0:T(8,128)(2,1)S(1)} %get-tuple-element.304.rows_ref, f32[1,8192]{1,0:T(1,128)S(1)} %add_add_fusion.total_ref.all_ref, ...), custom_call_target="tpu_custom_call" | custom-call | flops 6442450944 | bytes 1048576 | tf_op jit(solution)/shard_map/student/pallas_call | solution.py:499
  117.2 2.1 %collective-permute-start.42 = (f32[1,4096]{1,0:T(1,128)S(1)}, f32[1,4096]{1,0:T(1,128)S(1)}, u32[]{:S(2)}, u32[]{:S(2)}) collective-permute-start(f32[1,4096]{1,0:T(1,128)S(1)} %add_add_fusion.5), channel_id=1, source_target_pairs={{0,64},{32,96},{64,0},{96,32},{1,65},{33,97},{65,1},{97,33},{2,66}... | collective-permute-start | bytes 49160 | tf_op jit(solution)/shard_map/ppermute | solution.py:689
  124.3 3.2 %col_step.3 = f32[1,2048]{1,0:T(1,128)S(1)} custom-call(s32[24]{0:T(128)S(1)} %get-tuple-element.250.meta, f32[1,4096]{1,0:T(1,128)S(1)} %add_add_fusion.4.total_ref, f32[1,4096]{1,0:T(1,128)S(1)} %get-tuple-element.301.valid_ref, bf16[8,2048,512]{2,1,0:T(8,128)(2,1)S(1)} %get-tuple-element.265.expo_ref), custom_call_target="tpu_custom_call" | custom-call | flops 3355443200 | bytes 1048576 | tf_op jit(solution)/shard_map/col_step/pallas_call | solution.py:392
  127.5 3.6 %collective-permute-start.45 = (f32[1,2048]{1,0:T(1,128)S(1)}, f32[1,2048]{1,0:T(1,128)S(1)}, u32[]{:S(2)}, u32[]{:S(2)}) collective-permute-start(f32[1,2048]{1,0:T(1,128)S(1)} %col_step.3), channel_id=1, source_target_pairs={{0,8},{4,12},{8,0},{12,4},{1,9},{5,13},{9,1},{13,5},{2,10},{6,14},... | collective-permute-start | bytes 24584 | tf_op jit(solution)/shard_map/ppermute | solution.py:689
  132.8 3.2 %collective-permute-done.44 = f32[1,2048]{1,0:T(1,128)S(1)} collective-permute-done((f32[1,2048]{1,0:T(1,128)S(1)}, f32[1,2048]{1,0:T(1,128)S(1)}, u32[]{:S(2)}, u32[]{:S(2)}) %collective-permute-start.44) | collective-permute-done | bytes 8224 | tf_op jit(solution)/shard_map/ppermute | solution.py:689
  136.0 2.5 %row_step.5 = f32[1,4096]{1,0:T(1,128)S(1)} custom-call(s32[4]{0:T(128)S(1)} %pad_add_fusion.place, s32[24]{0:T(128)S(1)} %get-tuple-element.250.meta, f32[1,2048]{1,0:T(1,128)S(1)} %add_add_fusion.7.total_ref.col_ref, bf16[8,2048,512]{2,1,0:T(8,128)(2,1)S(1)} %get-tuple-element.265.expo_ref), custom_call_target="tpu_custom_call" | custom-call | flops 3355443200 | bytes 1048576 | tf_op jit(solution)/shard_map/row_step/pallas_call | solution.py:359
  139.8 2.1 %collective-permute-start.49 = (f32[1,4096]{1,0:T(1,128)S(1)}, f32[1,4096]{1,0:T(1,128)S(1)}, u32[]{:S(2)}, u32[]{:S(2)}) collective-permute-start(f32[1,4096]{1,0:T(1,128)S(1)} %add.153), channel_id=1, source_target_pairs={{0,2},{2,0},{16,18},{18,16},{1,3},{3,1},{17,19},{19,17},{4,6},{6,4... | collective-permute-start | bytes 49160 | tf_op jit(solution)/shard_map/ppermute | solution.py:689
  143.9 3.5 %feature_step.2.refs_0_ = bf16[4096,256]{1,0:T(8,128)(2,1)S(1)} custom-call(s32[24]{0:T(128)S(1)} %get-tuple-element.250.meta, f32[1,2048]{1,0:T(1,128)S(1)} %add_add_fusion.7.total_ref.col_ref, bf16[8,2048,512]{2,1,0:T(8,128)(2,1)S(1)} %get-tuple-element.265.expo_ref, bf16[256,2048]{1,0:T(8,128)(2,1)S(1)} %get-tuple-element.336.turned_ref), custom_call_target="tpu_custom_call" | custom-call | flops 2147483648 | bytes 1048576 | tf_op jit(solution)/shard_map/feature_step/pallas_call | solution.py:542
  151.2 2.5 %feature_step.3.plan_ref = bf16[4096,256]{1,0:T(8,128)(2,1)S(1)} custom-call(s32[24]{0:T(128)S(1)} %get-tuple-element.250.meta, f32[1,2048]{1,0:T(1,128)S(1)} %add_add_fusion.7.total_ref.col_ref, bf16[8,2048,512]{2,1,0:T(8,128)(2,1)S(1)} %get-tuple-element.265.expo_ref, ...), custom_call_target="tpu_custom_call", output_to_operand_aliasing={{}: (4, {})} | custom-call | flops 2147483648 | bytes 1048576 | tf_op jit(solution)/shard_map/feature_step/pallas_call | solution.py:542
  154.2 2.6 %join_step.1 = (bf16[16,128,256]{2,1,0:T(8,128)(2,1)S(1)}, bf16[16,128,256]{2,1,0:T(8,128)(2,1)S(1)}) custom-call(s32[4]{0:T(128)S(1)} %pad_add_fusion.place, s32[24]{0:T(128)S(1)} %get-tuple-element.250.meta, f32[1,4096]{1,0:T(1,128)S(1)} %add_add_fusion.2.total_ref, f32[1,4096]{1,0:T(1,128)S(1)} %get-tuple-element.301.valid_ref, ...), custom_call_target="tpu_custom_call" | custom-call | flops 2147483648 | bytes 1048576 | tf_op jit(solution)/shard_map/join_step/pallas_call | solution.py:586
  156.9 5.3 %grad_step.1 = (bf16[512,256]{1,0:T(8,128)(2,1)S(1)}, bf16[512,256]{1,0:T(8,128)(2,1)S(1)}, bf16[512,256]{1,0:T(8,128)(2,1)S(1)}, bf16[512,256]{1,0:T(8,128)(2,1)S(1)}) custom-call(s32[4]{0:T(128)S(1)} %pad_add_fusion.place, s32[24]{0:T(128)S(1)} %get-tuple-element.250.meta, f32[1,4096]{1,0:T(1,128)S(1)} %add_add_fusion.2.total_ref, ...), custom_call_target="tpu_custom_call" | custom-call | flops 4294967296 | bytes 1048576 | tf_op jit(solution)/shard_map/grad_step/pallas_call | solution.py:627
  163.6 5.1 %all-to-all-start = ((bf16[16,128,256]{2,1,0:T(8,128)(2,1)}), bf16[16,128,256]{2,1,0:T(8,128)(2,1)S(1)}, u32[]{:S(2)}, u32[]{:S(2)}) async-start(bf16[16,128,256]{2,1,0:T(8,128)(2,1)} %add_convert_fusion), calls=%async_computation | async-start | bytes 2097152 | tf_op jit(solution)/shard_map/all_to_all | solution.py:648
  168.8 2.1 %collective-permute-start.55 = (bf16[512,256]{1,0:T(8,128)(2,1)S(1)}, bf16[512,256]{1,0:T(8,128)(2,1)S(1)}, u32[]{:S(2)}, u32[]{:S(2)}) collective-permute-start(bf16[512,256]{1,0:T(8,128)(2,1)S(1)} %get-tuple-element.366), channel_id=1, source_target_pairs={{0,12},{4,8},{8,4},{12,0},{1,13},{5,9},{9,5},{13,1},{2,14},{6,10},... | collective-permute-start | bytes 786440 | tf_op jit(solution)/shard_map/ppermute | solution.py:644
  174.0 3.8 %collective-permute-done.54 = bf16[512,256]{1,0:T(8,128)(2,1)S(1)} collective-permute-done((bf16[512,256]{1,0:T(8,128)(2,1)S(1)}, bf16[512,256]{1,0:T(8,128)(2,1)S(1)}, u32[]{:S(2)}, u32[]{:S(2)}) %collective-permute-start.54) | collective-permute-done | bytes 262176 | tf_op jit(solution)/shard_map/ppermute | solution.py:644
  177.9 4.6 %collective-permute-done.55 = bf16[512,256]{1,0:T(8,128)(2,1)S(1)} collective-permute-done((bf16[512,256]{1,0:T(8,128)(2,1)S(1)}, bf16[512,256]{1,0:T(8,128)(2,1)S(1)}, u32[]{:S(2)}, u32[]{:S(2)}) %collective-permute-start.55) | collective-permute-done | bytes 262176 | tf_op jit(solution)/shard_map/ppermute | solution.py:644
  (139 shorter events, 61.6 us)
Async XLA Ops:
  3.0 11.1 %collective-permute-start = (bf16[528,128]{1,0:T(8,128)(2,1)S(1)}, bf16[528,128]{1,0:T(8,128)(2,1)S(1)}, u32[]{:S(2)}, u32[]{:S(2)}) collective-permute-start(bf16[528,128]{1,0:T(8,128)(2,1)S(1)} %get-tuple-element.188), channel_id=1, source_target_pairs={{0,16},{16,0},{1,17},{17,1},{2,18},{18,2},{3,19},{19,3},{4,20},{20... | collective-permute-start | bytes 405512 | tf_op jit(solution)/shard_map/ppermute | solution.py:640
  4.7 9.4 %collective-permute-start.1 = (bf16[528,128]{1,0:T(8,128)(2,1)S(1)}, bf16[528,128]{1,0:T(8,128)(2,1)S(1)}, u32[]{:S(2)}, u32[]{:S(2)}) collective-permute-start(bf16[528,128]{1,0:T(8,128)(2,1)S(1)} %get-tuple-element.189), channel_id=1, source_target_pairs={{0,16},{16,0},{1,17},{17,1},{2,18},{18,2},{3,19},{19,3},{4,20},{20... | collective-permute-start | bytes 405512 | tf_op jit(solution)/shard_map/ppermute | solution.py:640
  15.3 14.2 %collective-permute-start.5 = (bf16[2,528,128]{2,1,0:T(8,128)(2,1)S(1)}, bf16[2,528,128]{2,1,0:T(8,128)(2,1)S(1)}, u32[]{:S(2)}, u32[]{:S(2)}) collective-permute-start(bf16[2,528,128]{2,1,0:T(8,128)(2,1)S(1)} %pad_maximum_fusion.1.refs_0_), channel_id=1, source_target_pairs={{0,64},{32,96},{64,0},{96,32},{1,65},{33,97},{65,1},{97,33},{2,66}... | collective-permute-start | bytes 811016 | tf_op jit(solution)/shard_map/ppermute | solution.py:644
  18.6 12.6 %collective-permute-start.4 = (bf16[2,528,128]{2,1,0:T(8,128)(2,1)S(1)}, bf16[2,528,128]{2,1,0:T(8,128)(2,1)S(1)}, u32[]{:S(2)}, u32[]{:S(2)}) collective-permute-start(bf16[2,528,128]{2,1,0:T(8,128)(2,1)S(1)} %pad_maximum_fusion.1.refs_0_), channel_id=1, source_target_pairs={{0,96},{32,64},{64,32},{96,0},{1,97},{33,65},{65,33},{97,1},{2,98}... | collective-permute-start | bytes 811016 | tf_op jit(solution)/shard_map/ppermute | solution.py:644
  19.7 12.0 %collective-permute-start.3 = (bf16[2,528,128]{2,1,0:T(8,128)(2,1)S(1)}, bf16[2,528,128]{2,1,0:T(8,128)(2,1)S(1)}, u32[]{:S(2)}, u32[]{:S(2)}) collective-permute-start(bf16[2,528,128]{2,1,0:T(8,128)(2,1)S(1)} %pad_maximum_fusion.1.refs_0_), channel_id=1, source_target_pairs={{0,32},{32,0},{64,96},{96,64},{1,33},{33,1},{65,97},{97,65},{2,34}... | collective-permute-start | bytes 811016 | tf_op jit(solution)/shard_map/ppermute | solution.py:644
  19.7 9.8 %collective-permute-start.6 = (f32[1,512]{1,0:T(1,128)S(1)}, f32[1,512]{1,0:T(1,128)S(1)}, u32[]{:S(2)}, u32[]{:S(2)}) collective-permute-start(f32[1,512]{1,0:T(1,128)S(1)} %max.27), channel_id=1, source_target_pairs={{0,2},{2,0},{1,3},{3,1},{4,6},{6,4},{5,7},{7,5},{8,10},{10,8},{9,1... | collective-permute-start | bytes 6152 | tf_op jit(solution)/shard_map/ppermute | solution.py:640
  36.3 13.0 %collective-permute-start.14 = (f32[2,1,512]{2,1,0:T(1,128)S(1)}, f32[2,1,512]{2,1,0:T(1,128)S(1)}, u32[]{:S(2)}, u32[]{:S(2)}) collective-permute-start(f32[2,1,512]{2,1,0:T(1,128)S(1)} %pad_maximum_fusion.3.refs_8_), channel_id=1, source_target_pairs={{0,64},{32,96},{64,0},{96,32},{1,65},{33,97},{65,1},{97,33},{2,66}... | collective-permute-start | bytes 12296 | tf_op jit(solution)/shard_map/ppermute | solution.py:644
  38.4 10.9 %collective-permute-start.13 = (f32[2,1,512]{2,1,0:T(1,128)S(1)}, f32[2,1,512]{2,1,0:T(1,128)S(1)}, u32[]{:S(2)}, u32[]{:S(2)}) collective-permute-start(f32[2,1,512]{2,1,0:T(1,128)S(1)} %pad_maximum_fusion.3.refs_8_), channel_id=1, source_target_pairs={{0,96},{32,64},{64,32},{96,0},{1,97},{33,65},{65,33},{97,1},{2,98}... | collective-permute-start | bytes 12296 | tf_op jit(solution)/shard_map/ppermute | solution.py:644
  40.4 8.9 %collective-permute-start.12 = (f32[2,1,512]{2,1,0:T(1,128)S(1)}, f32[2,1,512]{2,1,0:T(1,128)S(1)}, u32[]{:S(2)}, u32[]{:S(2)}) collective-permute-start(f32[2,1,512]{2,1,0:T(1,128)S(1)} %pad_maximum_fusion.3.refs_8_), channel_id=1, source_target_pairs={{0,32},{32,0},{64,96},{96,64},{1,33},{33,1},{65,97},{97,65},{2,34}... | collective-permute-start | bytes 12296 | tf_op jit(solution)/shard_map/ppermute | solution.py:644
  40.4 8.8 %collective-permute-start.15 = (bf16[2,528,128]{2,1,0:T(8,128)(2,1)S(1)}, bf16[2,528,128]{2,1,0:T(8,128)(2,1)S(1)}, u32[]{:S(2)}, u32[]{:S(2)}) collective-permute-start(bf16[2,528,128]{2,1,0:T(8,128)(2,1)S(1)} %pad_maximum_fusion.2), channel_id=1, source_target_pairs={{0,32},{32,0},{64,96},{96,64},{1,33},{33,1},{65,97},{97,65},{2,34}... | collective-permute-start | bytes 811016 | tf_op jit(solution)/shard_map/ppermute | solution.py:644
  50.7 11.1 %collective-permute-start.17 = (f32[2,1,512]{2,1,0:T(1,128)S(1)}, f32[2,1,512]{2,1,0:T(1,128)S(1)}, u32[]{:S(2)}, u32[]{:S(2)}) collective-permute-start(f32[2,1,512]{2,1,0:T(1,128)S(1)} %pad_maximum_fusion.5), channel_id=1, source_target_pairs={{0,2},{2,0},{1,3},{3,1},{4,6},{6,4},{5,7},{7,5},{8,10},{10,8},{9,1... | collective-permute-start | bytes 12296 | tf_op jit(solution)/shard_map/ppermute | solution.py:640
  53.8 16.8 %collective-permute-start.21 = (bf16[2,2,528,128]{3,2,1,0:T(8,128)(2,1)S(1)}, bf16[2,2,528,128]{3,2,1,0:T(8,128)(2,1)S(1)}, u32[]{:S(2)}, u32[]{:S(2)}) collective-permute-start(bf16[2,2,528,128]{3,2,1,0:T(8,128)(2,1)S(1)} %pad_maximum_fusion), channel_id=1, source_target_pairs={{0,96},{32,64},{64,32},{96,0},{1,97},{33,65},{65,33},{97,1},{2,98}... | collective-permute-start | bytes 1622024 | tf_op jit(solution)/shard_map/ppermute | solution.py:644
  61.8 5.6 %collective-permute-start.20 = (f32[1,2176]{1,0:T(1,128)S(1)}, f32[1,2176]{1,0:T(1,128)S(1)}, u32[]{:S(2)}, u32[]{:S(2)}) collective-permute-start(f32[1,2176]{1,0:T(1,128)S(1)} %get-tuple-element.257), channel_id=1, source_target_pairs={{0,8},{4,12},{8,0},{12,4},{1,9},{5,13},{9,1},{13,5},{2,10},{6,14},... | collective-permute-start | bytes 26120 | tf_op jit(solution)/shard_map/ppermute | solution.py:689
  75.7 5.5 %collective-permute-start.29 = (f32[1,8192]{1,0:T(1,128)S(1)}, f32[1,8192]{1,0:T(1,128)S(1)}, u32[]{:S(2)}, u32[]{:S(2)}) collective-permute-start(f32[1,8192]{1,0:T(1,128)S(1)} %add.133), channel_id=1, source_target_pairs={{0,2},{2,0},{16,18},{18,16},{1,3},{3,1},{17,19},{19,17},{4,6},{6,4... | collective-permute-start | bytes 98312 | tf_op jit(solution)/shard_map/ppermute | solution.py:689
  76.3 5.3 %collective-permute-start.28 = (f32[1,8192]{1,0:T(1,128)S(1)}, f32[1,8192]{1,0:T(1,128)S(1)}, u32[]{:S(2)}, u32[]{:S(2)}) collective-permute-start(f32[1,8192]{1,0:T(1,128)S(1)} %add.133), channel_id=1, source_target_pairs={{0,18},{2,16},{16,2},{18,0},{1,19},{3,17},{17,3},{19,1},{4,22},{6,... | collective-permute-start | bytes 98312 | tf_op jit(solution)/shard_map/ppermute | solution.py:689
  83.0 5.8 %collective-permute-start.32 = (f32[1,8192]{1,0:T(1,128)S(1)}, f32[1,8192]{1,0:T(1,128)S(1)}, u32[]{:S(2)}, u32[]{:S(2)}) collective-permute-start(f32[1,8192]{1,0:T(1,128)S(1)} %add_add_fusion.1), channel_id=1, source_target_pairs={{0,64},{32,96},{64,0},{96,32},{1,65},{33,97},{65,1},{97,33},{2,66}... | collective-permute-start | bytes 98312 | tf_op jit(solution)/shard_map/ppermute | solution.py:689
  93.2 10.1 %collective-permute-start.35 = (f32[1,2048]{1,0:T(1,128)S(1)}, f32[1,2048]{1,0:T(1,128)S(1)}, u32[]{:S(2)}, u32[]{:S(2)}) collective-permute-start(f32[1,2048]{1,0:T(1,128)S(1)} %col_step.2), channel_id=1, source_target_pairs={{0,8},{4,12},{8,0},{12,4},{1,9},{5,13},{9,1},{13,5},{2,10},{6,14},... | collective-permute-start | bytes 24584 | tf_op jit(solution)/shard_map/ppermute | solution.py:689
  95.2 8.1 %collective-permute-start.34 = (f32[1,2048]{1,0:T(1,128)S(1)}, f32[1,2048]{1,0:T(1,128)S(1)}, u32[]{:S(2)}, u32[]{:S(2)}) collective-permute-start(f32[1,2048]{1,0:T(1,128)S(1)} %col_step.2), channel_id=1, source_target_pairs={{0,12},{4,8},{8,4},{12,0},{1,13},{5,9},{9,5},{13,1},{2,14},{6,10},... | collective-permute-start | bytes 24584 | tf_op jit(solution)/shard_map/ppermute | solution.py:689
  95.8 7.5 %collective-permute-start.33 = (f32[1,2048]{1,0:T(1,128)S(1)}, f32[1,2048]{1,0:T(1,128)S(1)}, u32[]{:S(2)}, u32[]{:S(2)}) collective-permute-start(f32[1,2048]{1,0:T(1,128)S(1)} %col_step.2), channel_id=1, source_target_pairs={{0,4},{4,0},{8,12},{12,8},{1,5},{5,1},{9,13},{13,9},{2,6},{6,2},{1... | collective-permute-start | bytes 24584 | tf_op jit(solution)/shard_map/ppermute | solution.py:689
  107.1 10.1 %collective-permute-start.39 = (f32[1,4096]{1,0:T(1,128)S(1)}, f32[1,4096]{1,0:T(1,128)S(1)}, u32[]{:S(2)}, u32[]{:S(2)}) collective-permute-start(f32[1,4096]{1,0:T(1,128)S(1)} %add.143), channel_id=1, source_target_pairs={{0,2},{2,0},{16,18},{18,16},{1,3},{3,1},{17,19},{19,17},{4,6},{6,4... | collective-permute-start | bytes 49160 | tf_op jit(solution)/shard_map/ppermute | solution.py:689
  108.0 9.2 %collective-permute-start.38 = (f32[1,4096]{1,0:T(1,128)S(1)}, f32[1,4096]{1,0:T(1,128)S(1)}, u32[]{:S(2)}, u32[]{:S(2)}) collective-permute-start(f32[1,4096]{1,0:T(1,128)S(1)} %add.143), channel_id=1, source_target_pairs={{0,18},{2,16},{16,2},{18,0},{1,19},{3,17},{17,3},{19,1},{4,22},{6,... | collective-permute-start | bytes 49160 | tf_op jit(solution)/shard_map/ppermute | solution.py:689
  110.1 7.1 %collective-permute-start.37 = (f32[1,4096]{1,0:T(1,128)S(1)}, f32[1,4096]{1,0:T(1,128)S(1)}, u32[]{:S(2)}, u32[]{:S(2)}) collective-permute-start(f32[1,4096]{1,0:T(1,128)S(1)} %add.143), channel_id=1, source_target_pairs={{0,16},{2,18},{16,0},{18,2},{1,17},{3,19},{17,1},{19,3},{4,20},{6,... | collective-permute-start | bytes 49160 | tf_op jit(solution)/shard_map/ppermute | solution.py:689
  117.2 5.3 %collective-permute-start.42 = (f32[1,4096]{1,0:T(1,128)S(1)}, f32[1,4096]{1,0:T(1,128)S(1)}, u32[]{:S(2)}, u32[]{:S(2)}) collective-permute-start(f32[1,4096]{1,0:T(1,128)S(1)} %add_add_fusion.5), channel_id=1, source_target_pairs={{0,64},{32,96},{64,0},{96,32},{1,65},{33,97},{65,1},{97,33},{2,66}... | collective-permute-start | bytes 49160 | tf_op jit(solution)/shard_map/ppermute | solution.py:689
  127.5 5.2 %collective-permute-start.45 = (f32[1,2048]{1,0:T(1,128)S(1)}, f32[1,2048]{1,0:T(1,128)S(1)}, u32[]{:S(2)}, u32[]{:S(2)}) collective-permute-start(f32[1,2048]{1,0:T(1,128)S(1)} %col_step.3), channel_id=1, source_target_pairs={{0,8},{4,12},{8,0},{12,4},{1,9},{5,13},{9,1},{13,5},{2,10},{6,14},... | collective-permute-start | bytes 24584 | tf_op jit(solution)/shard_map/ppermute | solution.py:689
  139.8 7.7 %collective-permute-start.49 = (f32[1,4096]{1,0:T(1,128)S(1)}, f32[1,4096]{1,0:T(1,128)S(1)}, u32[]{:S(2)}, u32[]{:S(2)}) collective-permute-start(f32[1,4096]{1,0:T(1,128)S(1)} %add.153), channel_id=1, source_target_pairs={{0,2},{2,0},{16,18},{18,16},{1,3},{3,1},{17,19},{19,17},{4,6},{6,4... | collective-permute-start | bytes 49160 | tf_op jit(solution)/shard_map/ppermute | solution.py:689
  141.8 5.6 %collective-permute-start.48 = (f32[1,4096]{1,0:T(1,128)S(1)}, f32[1,4096]{1,0:T(1,128)S(1)}, u32[]{:S(2)}, u32[]{:S(2)}) collective-permute-start(f32[1,4096]{1,0:T(1,128)S(1)} %add.153), channel_id=1, source_target_pairs={{0,18},{2,16},{16,2},{18,0},{1,19},{3,17},{17,3},{19,1},{4,22},{6,... | collective-permute-start | bytes 49160 | tf_op jit(solution)/shard_map/ppermute | solution.py:689
  147.7 6.1 %collective-permute-start.52 = (f32[1,4096]{1,0:T(1,128)S(1)}, f32[1,4096]{1,0:T(1,128)S(1)}, u32[]{:S(2)}, u32[]{:S(2)}) collective-permute-start(f32[1,4096]{1,0:T(1,128)S(1)} %add_add_fusion.3), channel_id=1, source_target_pairs={{0,64},{32,96},{64,0},{96,32},{1,65},{33,97},{65,1},{97,33},{2,66}... | collective-permute-start | bytes 49160 | tf_op jit(solution)/shard_map/ppermute | solution.py:689
  156.8 5.4 %collective-permute-start.53 = (bf16[16,128,256]{2,1,0:T(8,128)(2,1)S(1)}, bf16[16,128,256]{2,1,0:T(8,128)(2,1)S(1)}, u32[]{:S(2)}, u32[]{:S(2)}) collective-permute-start(bf16[16,128,256]{2,1,0:T(8,128)(2,1)S(1)} %get-tuple-element.352), channel_id=1, source_target_pairs={{0,1},{1,0},{2,3},{3,2},{4,5},{5,4},{6,7},{7,6},{8,9},{9,8},{10,11... | collective-permute-start | bytes 3145736 | tf_op jit(solution)/shard_map/ppermute | solution.py:640
  163.6 21.6 %all-to-all-start = ((bf16[16,128,256]{2,1,0:T(8,128)(2,1)}), bf16[16,128,256]{2,1,0:T(8,128)(2,1)S(1)}, u32[]{:S(2)}, u32[]{:S(2)}) async-start(bf16[16,128,256]{2,1,0:T(8,128)(2,1)} %add_convert_fusion), calls=%async_computation | async-start | bytes 2097152 | tf_op jit(solution)/shard_map/all_to_all | solution.py:648
  168.7 9.2 %collective-permute-start.54 = (bf16[512,256]{1,0:T(8,128)(2,1)S(1)}, bf16[512,256]{1,0:T(8,128)(2,1)S(1)}, u32[]{:S(2)}, u32[]{:S(2)}) collective-permute-start(bf16[512,256]{1,0:T(8,128)(2,1)S(1)} %get-tuple-element.365), channel_id=1, source_target_pairs={{0,4},{4,0},{8,12},{12,8},{1,5},{5,1},{9,13},{13,9},{2,6},{6,2},{1... | collective-permute-start | bytes 786440 | tf_op jit(solution)/shard_map/ppermute | solution.py:644
  168.8 13.7 %collective-permute-start.55 = (bf16[512,256]{1,0:T(8,128)(2,1)S(1)}, bf16[512,256]{1,0:T(8,128)(2,1)S(1)}, u32[]{:S(2)}, u32[]{:S(2)}) collective-permute-start(bf16[512,256]{1,0:T(8,128)(2,1)S(1)} %get-tuple-element.366), channel_id=1, source_target_pairs={{0,12},{4,8},{8,4},{12,0},{1,13},{5,9},{9,5},{13,1},{2,14},{6,10},... | collective-permute-start | bytes 786440 | tf_op jit(solution)/shard_map/ppermute | solution.py:644
  170.9 13.4 %collective-permute-start.56 = (bf16[512,256]{1,0:T(8,128)(2,1)S(1)}, bf16[512,256]{1,0:T(8,128)(2,1)S(1)}, u32[]{:S(2)}, u32[]{:S(2)}) collective-permute-start(bf16[512,256]{1,0:T(8,128)(2,1)S(1)} %get-tuple-element.367), channel_id=1, source_target_pairs={{0,8},{4,12},{8,0},{12,4},{1,9},{5,13},{9,1},{13,5},{2,10},{6,14},... | collective-permute-start | bytes 786440 | tf_op jit(solution)/shard_map/ppermute | solution.py:644
  (27 other events, 93.5 us)

commit v3 on v2

--- a/solution.py
+++ b/solution.py
@@ -130,22 +130,21 @@
     out_ref[...] = best
 
 
-def row_max(feats, protos, rows, part, parts):
+def row_max(feats, protos, rows, first, steps):
     count, width = protos.shape
     block = 2048
-    steps = count // block // parts
     return pl.pallas_call(
         max_kernel,
         grid=(steps,),
         out_shape=jax.ShapeDtypeStruct((1, rows), F32),
         in_specs=[
             pl.BlockSpec(feats.shape, lambda i: (0, 0)),
-            pl.BlockSpec((block, width), lambda i: (i + part * steps, 0)),
+            pl.BlockSpec((block, width), lambda i: (i + first, 0)),
         ],
         out_specs=pl.BlockSpec((1, rows), lambda i: (0, 0)),
         scratch_shapes=[pltpu.VMEM((width, rows), BF16)],
         compiler_params=params(14),
-        cost_estimate=cost(2 * count * width * rows // parts),
+        cost_estimate=cost(3 * steps * block * width * rows),
         name="row_max",
     )(feats, protos)
 
@@ -714,19 +713,20 @@
     teach, stud = compact(masked, streamed(teacher), streamed(student))
     t_half, _ = choose(low_c, teach[:, :LANES], teach[:, LANES:])
     s_half, _ = choose(low_c, stud[:, :LANES], stud[:, LANES:])
-    t_half, s_half, teach, stud = tie(t_half, s_half, teach, stud)
-    t_beside, s_beside = swap(t_half, "xl"), swap(s_half, "xl")
-    top = row_max(teach, table, rows, 0, 1)
-    t_beside, s_beside, top, stud = tie(t_beside, s_beside, top, stud)
+    t_half, teach, stud = tie(t_half, teach, stud)
+    t_beside = swap(t_half, "xl")
+    top = row_max(teach, table, rows, 0, 8)
+    t_beside, top, stud, s_half = tie(t_beside, top, stud, s_half)
     t_pair = jnp.stack(choose(low_x, t_half, t_beside))
-    s_pair = jnp.stack(choose(low_x, s_half, s_beside))
+
+    t_pair, top, stud = tie(t_pair, top, stud)
+    mine = gather_along(t_pair)
+    s_beside = swap(s_half, "xl")
     top = jnp.maximum(top, swap(top, "c"))
-
-    t_pair, s_pair, top, stud = tie(t_pair, s_pair, top, stud)
-    mine = gather_along(t_pair)
     far = swap(top, "xh")
     soft = row_soft(stud, table, rows, 0, 2)
-    mine, far, soft, top, stud, s_pair = tie(mine, far, soft, top, stud, s_pair)
+    mine, far, soft, top, stud, s_beside = tie(mine, far, soft, top, stud, s_beside)
+    s_pair = jnp.stack(choose(low_x, s_half, s_beside))
 
     top = jnp.maximum(top, far)
     other = [swap(piece, "c") for piece in mine]
@@ -739,7 +739,7 @@
     mine, other, tops, soft, soft_two, s_mine, place = tie(mine, other, tops, soft, soft_two, s_mine, place)
     soft = jnp.stack(merged(soft, soft_two))
     soft = jnp.stack(merged(soft, swap(soft, "c")))
-    soft, tops, s_mine = tie(soft, tops, s_mine)
+    soft, tops = tie(soft, tops)
 
     s_mine = [s_mine[0], s_mine[1], from_xor(s_mine, "y", 3)]
     soft_far = swap(soft, "xh")

time: 187 us -> 183 us (0.979)
  waiting for transfers between devices: 37.1 us -> 35.2 us
    ppermute x19, waiting for transfers between devices: 7.71 us -> 5.5 us  [swap(): return lax.ppermute(value, axis, [(0, 1), (1, 0)])]
  transfers between devices with their start and end apart: 58 -> 58, of which waited for: 24 -> 24; matrix products, arithmetic and copies ran while one was open for 1% -> 1% of each run, Pallas kernels for 31% -> 32%
where the time goes in v3:
time: 183 us
  Pallas kernels  73.9 us (40%)
  starting transfers between devices  66.5 us (36%)
  waiting for transfers between devices  35.2 us (19%)
  other arithmetic  3.77 us (2%)
  between operations  1.9 us (1%)
    ppermute x27, starting transfers between devices, ring(): lax.ppermute(value, axes, [(i, i ^ mask) for i in range(4)])  34.2 us
    ppermute x27, waiting for transfers between devices, ring(): lax.ppermute(value, axes, [(i, i ^ mask) for i in range(4)])  17.6 us
    ppermute x11, starting transfers between devices, from_xor(): return lax.ppermute(value, axis, [(i, i ^ mask) for i in range(4)])  16 us
    pallas_call x2, Pallas kernels, row_soft(): pl.pallas_call(soft_kernel, grid=(steps,), out_shape=(jax.ShapeDtypeStruc...  13.6 us
    pallas_call x2, Pallas kernels, student_step(): pl.pallas_call(functools.partial(student_kernel, part), out_shape=outs, i...  13 us
    ppermute x11, waiting for transfers between devices, from_xor(): return lax.ppermute(value, axis, [(i, i ^ mask) for i in range(4)])  12 us
    ppermute x19, starting transfers between devices, swap(): return lax.ppermute(value, axis, [(0, 1), (1, 0)])  11.2 us
    pallas_call x1, Pallas kernels, row_max(): pl.pallas_call(max_kernel, grid=(steps,), out_shape=jax.ShapeDtypeStruct(...  8.92 us
  transfers between devices with their start and end apart: 58, of which 24 were waited for; matrix products, arithmetic and copies ran while one was open for 1% of the time, Pallas kernels for 32%

profile of v3, /device:TPU:0, one launch (start us, length us, event | category | flops | bytes accessed | tf_op | source)
XLA Modules:
  0.0 182.5 jit_solution(528986246149536793)
XLA Ops:
  4.7 8.9 %row_max.1 = f32[1,512]{1,0:T(1,128)S(1)} custom-call(bf16[528,256]{1,0:T(8,128)(2,1)S(1)} %get-tuple-element.186.teach_ref, bf16[16384,256]{1,0:T(8,128)(2,1)} %refs_8_.1), custom_call_target="tpu_custom_call" | custom-call | flops 6442450944 | bytes 1048576 | tf_op jit(solution)/shard_map/row_max/pallas_call | solution.py:136
  13.9 3.2 %collective-permute-start.3 = (bf16[2,528,128]{2,1,0:T(8,128)(2,1)S(1)}, bf16[2,528,128]{2,1,0:T(8,128)(2,1)S(1)}, u32[]{:S(2)}, u32[]{:S(2)}) collective-permute-start(bf16[2,528,128]{2,1,0:T(8,128)(2,1)S(1)} %pad_maximum_fusion.1.refs_0_), channel_id=1, source_target_pairs={{0,64},{32,96},{64,0},{96,32},{1,65},{33,97},{65,1},{97,33},{2,66}... | collective-permute-start | bytes 811016 | tf_op jit(solution)/shard_map/ppermute | solution.py:643
  18.7 3.1 %collective-permute-start.5 = (f32[1,512]{1,0:T(1,128)S(1)}, f32[1,512]{1,0:T(1,128)S(1)}, u32[]{:S(2)}, u32[]{:S(2)}) collective-permute-start(f32[1,512]{1,0:T(1,128)S(1)} %max.27), channel_id=1, source_target_pairs={{0,2},{2,0},{1,3},{3,1},{4,6},{6,4},{5,7},{7,5},{8,10},{10,8},{9,1... | collective-permute-start | bytes 6152 | tf_op jit(solution)/shard_map/ppermute | solution.py:639
  21.8 6.8 %row_soft.2 = (f32[1,512]{1,0:T(1,128)S(1)}, f32[1,512]{1,0:T(1,128)S(1)}) custom-call(bf16[528,256]{1,0:T(8,128)(2,1)S(1)} %get-tuple-element.219.feat_ref, bf16[16384,256]{1,0:T(8,128)(2,1)} %refs_8_.1), custom_call_target="tpu_custom_call" | custom-call | flops 3221225472 | bytes 1048576 | tf_op jit(solution)/shard_map/row_soft/pallas_call | solution.py:179
  34.1 2.2 %collective-permute-start.14 = (f32[2,1,512]{2,1,0:T(1,128)S(1)}, f32[2,1,512]{2,1,0:T(1,128)S(1)}, u32[]{:S(2)}, u32[]{:S(2)}) collective-permute-start(f32[2,1,512]{2,1,0:T(1,128)S(1)} %pad_maximum_fusion.3.refs_8_), channel_id=1, source_target_pairs={{0,64},{32,96},{64,0},{96,32},{1,65},{33,97},{65,1},{97,33},{2,66}... | collective-permute-start | bytes 12296 | tf_op jit(solution)/shard_map/ppermute | solution.py:643
  40.2 6.8 %row_soft.3 = (f32[1,512]{1,0:T(1,128)S(1)}, f32[1,512]{1,0:T(1,128)S(1)}) custom-call(bf16[528,256]{1,0:T(8,128)(2,1)S(1)} %get-tuple-element.219.feat_ref, bf16[16384,256]{1,0:T(8,128)(2,1)} %refs_8_.1), custom_call_target="tpu_custom_call" | custom-call | flops 3221225472 | bytes 1048576 | tf_op jit(solution)/shard_map/row_soft/pallas_call | solution.py:179
  48.8 2.8 %collective-permute-start.17 = (f32[2,1,512]{2,1,0:T(1,128)S(1)}, f32[2,1,512]{2,1,0:T(1,128)S(1)}, u32[]{:S(2)}, u32[]{:S(2)}) collective-permute-start(f32[2,1,512]{2,1,0:T(1,128)S(1)} %pad_maximum_fusion.5), channel_id=1, source_target_pairs={{0,2},{2,0},{1,3},{3,1},{4,6},{6,4},{5,7},{7,5},{8,10},{10,8},{9,1... | collective-permute-start | bytes 12296 | tf_op jit(solution)/shard_map/ppermute | solution.py:639
  51.6 6.7 %expo.1 = (bf16[8,2048,512]{2,1,0:T(8,128)(2,1)S(1)}, f32[1,2176]{1,0:T(1,128)S(1)}, f32[1,4096]{1,0:T(1,128)S(1)}, s32[24]{0:T(128)S(1)}) custom-call(s32[4]{0:T(128)S(1)} %pad_add_fusion.place, bf16[2,528,128]{2,1,0:T(8,128)(2,1)S(1)} %pad_maximum_fusion.1.refs_0_, bf16[2,528,128]{2,1,0:T(8,128)(2,1)S(1)} %collective-permute-done.1.refs_1_, ...), custom_call_target="tpu_custom_call" | custom-call | flops 4294967296 | bytes 1048576 | tf_op jit(solution)/shard_map/expo/pallas_call | solution.py:305
  58.3 4.0 %collective-permute-start.20 = (f32[1,2176]{1,0:T(1,128)S(1)}, f32[1,2176]{1,0:T(1,128)S(1)}, u32[]{:S(2)}, u32[]{:S(2)}) collective-permute-start(f32[1,2176]{1,0:T(1,128)S(1)} %get-tuple-element.251), channel_id=1, source_target_pairs={{0,8},{4,12},{8,0},{12,4},{1,9},{5,13},{9,1},{13,5},{2,10},{6,14},... | collective-permute-start | bytes 26120 | tf_op jit(solution)/shard_map/ppermute | solution.py:688
  63.9 3.2 %collective-permute-done.19 = f32[1,2176]{1,0:T(1,128)S(1)} collective-permute-done((f32[1,2176]{1,0:T(1,128)S(1)}, f32[1,2176]{1,0:T(1,128)S(1)}, u32[]{:S(2)}, u32[]{:S(2)}) %collective-permute-start.19) | collective-permute-done | bytes 8736 | tf_op jit(solution)/shard_map/ppermute | solution.py:688
  68.3 2.5 %row_step.3 = f32[1,8192]{1,0:T(1,128)S(1)} custom-call(s32[4]{0:T(128)S(1)} %pad_add_fusion.place, s32[24]{0:T(128)S(1)} %get-tuple-element.244.meta, f32[1,2176]{1,0:T(1,128)S(1)} %add_add_fusion.6.total_ref, bf16[8,2048,512]{2,1,0:T(8,128)(2,1)S(1)} %get-tuple-element.259.expo_ref, f32[1,512]{1,0:T(1,128)S(1)} %multiply_add_fusion.refs_0_), custom_call_target="tpu_custom_call" | custom-call | flops 3355443200 | bytes 1048576 | tf_op jit(solution)/shard_map/row_step/pallas_call | solution.py:358
  73.1 2.4 %collective-permute-start.28 = (f32[1,8192]{1,0:T(1,128)S(1)}, f32[1,8192]{1,0:T(1,128)S(1)}, u32[]{:S(2)}, u32[]{:S(2)}) collective-permute-start(f32[1,8192]{1,0:T(1,128)S(1)} %add.133), channel_id=1, source_target_pairs={{0,18},{2,16},{16,2},{18,0},{1,19},{3,17},{17,3},{19,1},{4,22},{6,... | collective-permute-start | bytes 98312 | tf_op jit(solution)/shard_map/ppermute | solution.py:688
  83.0 2.2 %load_student.1 = (bf16[4608,256]{1,0:T(8,128)(2,1)S(1)}, f32[8,512]{1,0:T(8,128)S(1)}, bf16[2048,256]{1,0:T(8,128)(2,1)S(1)}, bf16[256,2048]{1,0:T(8,128)(2,1)S(1)}) custom-call(s32[4]{0:T(128)S(1)} %pad_add_fusion.place, s32[24]{0:T(128)S(1)} %get-tuple-element.244.meta, bf16[2,528,128]{2,1,0:T(8,128)(2,1)S(1)} %get-tuple-element.279.refs_0_, ...), custom_call_target="tpu_custom_call" | custom-call | flops 2147483648 | bytes 1048576 | tf_op jit(solution)/shard_map/load_student/pallas_call | solution.py:438
  86.7 3.2 %col_step.2 = f32[1,2048]{1,0:T(1,128)S(1)} custom-call(s32[24]{0:T(128)S(1)} %get-tuple-element.244.meta, f32[1,8192]{1,0:T(1,128)S(1)} %add_add_fusion.total_ref.all_ref, f32[1,4096]{1,0:T(1,128)S(1)} %get-tuple-element.295.valid_ref, bf16[8,2048,512]{2,1,0:T(8,128)(2,1)S(1)} %get-tuple-element.259.expo_ref), custom_call_target="tpu_custom_call" | custom-call | flops 3355443200 | bytes 1048576 | tf_op jit(solution)/shard_map/col_step/pallas_call | solution.py:391
  93.5 6.5 %student.2 = (bf16[512,256]{1,0:T(8,128)(2,1)S(1)}, bf16[512,256]{1,0:T(8,128)(2,1)S(1)}, bf16[4096,256]{1,0:T(8,128)(2,1)S(1)}) custom-call(s32[4]{0:T(128)S(1)} %pad_add_fusion.place, s32[24]{0:T(128)S(1)} %get-tuple-element.244.meta, bf16[4608,256]{1,0:T(8,128)(2,1)S(1)} %get-tuple-element.298.rows_ref, f32[1,8192]{1,0:T(1,128)S(1)} %add_add_fusion.total_ref.all_ref, ...), custom_call_target="tpu_custom_call" | custom-call | flops 6442450944 | bytes 1048576 | tf_op jit(solution)/shard_map/student/pallas_call | solution.py:498
  100.0 2.5 %row_step.4 = f32[1,4096]{1,0:T(1,128)S(1)} custom-call(s32[4]{0:T(128)S(1)} %pad_add_fusion.place, s32[24]{0:T(128)S(1)} %get-tuple-element.244.meta, f32[1,2048]{1,0:T(1,128)S(1)} %add_add_fusion.8.total_ref, bf16[8,2048,512]{2,1,0:T(8,128)(2,1)S(1)} %get-tuple-element.259.expo_ref), custom_call_target="tpu_custom_call" | custom-call | flops 3355443200 | bytes 1048576 | tf_op jit(solution)/shard_map/row_step/pallas_call | solution.py:358
  104.7 2.1 %collective-permute-start.38 = (f32[1,4096]{1,0:T(1,128)S(1)}, f32[1,4096]{1,0:T(1,128)S(1)}, u32[]{:S(2)}, u32[]{:S(2)}) collective-permute-start(f32[1,4096]{1,0:T(1,128)S(1)} %add.143), channel_id=1, source_target_pairs={{0,18},{2,16},{16,2},{18,0},{1,19},{3,17},{17,3},{19,1},{4,22},{6,... | collective-permute-start | bytes 49160 | tf_op jit(solution)/shard_map/ppermute | solution.py:688
  107.3 6.5 %student.3 = (bf16[512,256]{1,0:T(8,128)(2,1)S(1)}, bf16[512,256]{1,0:T(8,128)(2,1)S(1)}, bf16[4096,256]{1,0:T(8,128)(2,1)S(1)}) custom-call(s32[4]{0:T(128)S(1)} %pad_add_fusion.place, s32[24]{0:T(128)S(1)} %get-tuple-element.244.meta, bf16[4608,256]{1,0:T(8,128)(2,1)S(1)} %get-tuple-element.298.rows_ref, f32[1,8192]{1,0:T(1,128)S(1)} %add_add_fusion.total_ref.all_ref, ...), custom_call_target="tpu_custom_call" | custom-call | flops 6442450944 | bytes 1048576 | tf_op jit(solution)/shard_map/student/pallas_call | solution.py:498
  120.8 3.2 %col_step.3 = f32[1,2048]{1,0:T(1,128)S(1)} custom-call(s32[24]{0:T(128)S(1)} %get-tuple-element.244.meta, f32[1,4096]{1,0:T(1,128)S(1)} %add_add_fusion.4.total_ref, f32[1,4096]{1,0:T(1,128)S(1)} %get-tuple-element.295.valid_ref, bf16[8,2048,512]{2,1,0:T(8,128)(2,1)S(1)} %get-tuple-element.259.expo_ref), custom_call_target="tpu_custom_call" | custom-call | flops 3355443200 | bytes 1048576 | tf_op jit(solution)/shard_map/col_step/pallas_call | solution.py:391
  124.0 3.2 %collective-permute-start.45 = (f32[1,2048]{1,0:T(1,128)S(1)}, f32[1,2048]{1,0:T(1,128)S(1)}, u32[]{:S(2)}, u32[]{:S(2)}) collective-permute-start(f32[1,2048]{1,0:T(1,128)S(1)} %col_step.3), channel_id=1, source_target_pairs={{0,8},{4,12},{8,0},{12,4},{1,9},{5,13},{9,1},{13,5},{2,10},{6,14},... | collective-permute-start | bytes 24584 | tf_op jit(solution)/shard_map/ppermute | solution.py:688
  129.2 2.8 %collective-permute-done.44 = f32[1,2048]{1,0:T(1,128)S(1)} collective-permute-done((f32[1,2048]{1,0:T(1,128)S(1)}, f32[1,2048]{1,0:T(1,128)S(1)}, u32[]{:S(2)}, u32[]{:S(2)}) %collective-permute-start.44) | collective-permute-done | bytes 8224 | tf_op jit(solution)/shard_map/ppermute | solution.py:688
  132.1 2.5 %row_step.5 = f32[1,4096]{1,0:T(1,128)S(1)} custom-call(s32[4]{0:T(128)S(1)} %pad_add_fusion.place, s32[24]{0:T(128)S(1)} %get-tuple-element.244.meta, f32[1,2048]{1,0:T(1,128)S(1)} %add_add_fusion.7.total_ref.col_ref, bf16[8,2048,512]{2,1,0:T(8,128)(2,1)S(1)} %get-tuple-element.259.expo_ref), custom_call_target="tpu_custom_call" | custom-call | flops 3355443200 | bytes 1048576 | tf_op jit(solution)/shard_map/row_step/pallas_call | solution.py:358
  135.8 2.1 %collective-permute-start.49 = (f32[1,4096]{1,0:T(1,128)S(1)}, f32[1,4096]{1,0:T(1,128)S(1)}, u32[]{:S(2)}, u32[]{:S(2)}) collective-permute-start(f32[1,4096]{1,0:T(1,128)S(1)} %add.153), channel_id=1, source_target_pairs={{0,2},{2,0},{16,18},{18,16},{1,3},{3,1},{17,19},{19,17},{4,6},{6,4... | collective-permute-start | bytes 49160 | tf_op jit(solution)/shard_map/ppermute | solution.py:688
  137.9 2.1 %collective-permute-start.48 = (f32[1,4096]{1,0:T(1,128)S(1)}, f32[1,4096]{1,0:T(1,128)S(1)}, u32[]{:S(2)}, u32[]{:S(2)}) collective-permute-start(f32[1,4096]{1,0:T(1,128)S(1)} %add.153), channel_id=1, source_target_pairs={{0,18},{2,16},{16,2},{18,0},{1,19},{3,17},{17,3},{19,1},{4,22},{6,... | collective-permute-start | bytes 49160 | tf_op jit(solution)/shard_map/ppermute | solution.py:688
  139.9 3.5 %feature_step.2.refs_0_ = bf16[4096,256]{1,0:T(8,128)(2,1)S(1)} custom-call(s32[24]{0:T(128)S(1)} %get-tuple-element.244.meta, f32[1,2048]{1,0:T(1,128)S(1)} %add_add_fusion.7.total_ref.col_ref, bf16[8,2048,512]{2,1,0:T(8,128)(2,1)S(1)} %get-tuple-element.259.expo_ref, bf16[256,2048]{1,0:T(8,128)(2,1)S(1)} %get-tuple-element.330.turned_ref), custom_call_target="tpu_custom_call" | custom-call | flops 2147483648 | bytes 1048576 | tf_op jit(solution)/shard_map/feature_step/pallas_call | solution.py:541
  147.3 2.5 %feature_step.3.plan_ref = bf16[4096,256]{1,0:T(8,128)(2,1)S(1)} custom-call(s32[24]{0:T(128)S(1)} %get-tuple-element.244.meta, f32[1,2048]{1,0:T(1,128)S(1)} %add_add_fusion.7.total_ref.col_ref, bf16[8,2048,512]{2,1,0:T(8,128)(2,1)S(1)} %get-tuple-element.259.expo_ref, ...), custom_call_target="tpu_custom_call", output_to_operand_aliasing={{}: (4, {})} | custom-call | flops 2147483648 | bytes 1048576 | tf_op jit(solution)/shard_map/feature_step/pallas_call | solution.py:541
  150.7 2.6 %join_step.1 = (bf16[16,128,256]{2,1,0:T(8,128)(2,1)S(1)}, bf16[16,128,256]{2,1,0:T(8,128)(2,1)S(1)}) custom-call(s32[4]{0:T(128)S(1)} %pad_add_fusion.place, s32[24]{0:T(128)S(1)} %get-tuple-element.244.meta, f32[1,4096]{1,0:T(1,128)S(1)} %add_add_fusion.2.total_ref, f32[1,4096]{1,0:T(1,128)S(1)} %get-tuple-element.295.valid_ref, ...), custom_call_target="tpu_custom_call" | custom-call | flops 2147483648 | bytes 1048576 | tf_op jit(solution)/shard_map/join_step/pallas_call | solution.py:585
  153.4 5.3 %grad_step.1 = (bf16[512,256]{1,0:T(8,128)(2,1)S(1)}, bf16[512,256]{1,0:T(8,128)(2,1)S(1)}, bf16[512,256]{1,0:T(8,128)(2,1)S(1)}, bf16[512,256]{1,0:T(8,128)(2,1)S(1)}) custom-call(s32[4]{0:T(128)S(1)} %pad_add_fusion.place, s32[24]{0:T(128)S(1)} %get-tuple-element.244.meta, f32[1,4096]{1,0:T(1,128)S(1)} %add_add_fusion.2.total_ref, ...), custom_call_target="tpu_custom_call" | custom-call | flops 4294967296 | bytes 1048576 | tf_op jit(solution)/shard_map/grad_step/pallas_call | solution.py:626
  160.1 5.2 %all-to-all-start = ((bf16[16,128,256]{2,1,0:T(8,128)(2,1)}), bf16[16,128,256]{2,1,0:T(8,128)(2,1)S(1)}, u32[]{:S(2)}, u32[]{:S(2)}) async-start(bf16[16,128,256]{2,1,0:T(8,128)(2,1)} %add_convert_fusion), calls=%async_computation | async-start | bytes 2097152 | tf_op jit(solution)/shard_map/all_to_all | solution.py:647
  165.4 2.1 %collective-permute-start.55 = (bf16[512,256]{1,0:T(8,128)(2,1)S(1)}, bf16[512,256]{1,0:T(8,128)(2,1)S(1)}, u32[]{:S(2)}, u32[]{:S(2)}) collective-permute-start(bf16[512,256]{1,0:T(8,128)(2,1)S(1)} %get-tuple-element.360), channel_id=1, source_target_pairs={{0,12},{4,8},{8,4},{12,0},{1,13},{5,9},{9,5},{13,1},{2,14},{6,10},... | collective-permute-start | bytes 786440 | tf_op jit(solution)/shard_map/ppermute | solution.py:643
  170.6 3.8 %collective-permute-done.54 = bf16[512,256]{1,0:T(8,128)(2,1)S(1)} collective-permute-done((bf16[512,256]{1,0:T(8,128)(2,1)S(1)}, bf16[512,256]{1,0:T(8,128)(2,1)S(1)}, u32[]{:S(2)}, u32[]{:S(2)}) %collective-permute-start.54) | collective-permute-done | bytes 262176 | tf_op jit(solution)/shard_map/ppermute | solution.py:643
  174.5 4.6 %collective-permute-done.55 = bf16[512,256]{1,0:T(8,128)(2,1)S(1)} collective-permute-done((bf16[512,256]{1,0:T(8,128)(2,1)S(1)}, bf16[512,256]{1,0:T(8,128)(2,1)S(1)}, u32[]{:S(2)}, u32[]{:S(2)}) %collective-permute-start.55) | collective-permute-done | bytes 262176 | tf_op jit(solution)/shard_map/ppermute | solution.py:643
  (140 shorter events, 59.6 us)
Async XLA Ops:
  3.0 10.6 %collective-permute-start = (bf16[528,128]{1,0:T(8,128)(2,1)S(1)}, bf16[528,128]{1,0:T(8,128)(2,1)S(1)}, u32[]{:S(2)}, u32[]{:S(2)}) collective-permute-start(bf16[528,128]{1,0:T(8,128)(2,1)S(1)} %slice_select_fusion.1), channel_id=1, source_target_pairs={{0,16},{16,0},{1,17},{17,1},{2,18},{18,2},{3,19},{19,3},{4,20},{20... | collective-permute-start | bytes 405512 | tf_op jit(solution)/shard_map/ppermute | solution.py:639
  13.9 14.7 %collective-permute-start.3 = (bf16[2,528,128]{2,1,0:T(8,128)(2,1)S(1)}, bf16[2,528,128]{2,1,0:T(8,128)(2,1)S(1)}, u32[]{:S(2)}, u32[]{:S(2)}) collective-permute-start(bf16[2,528,128]{2,1,0:T(8,128)(2,1)S(1)} %pad_maximum_fusion.1.refs_0_), channel_id=1, source_target_pairs={{0,64},{32,96},{64,0},{96,32},{1,65},{33,97},{65,1},{97,33},{2,66}... | collective-permute-start | bytes 811016 | tf_op jit(solution)/shard_map/ppermute | solution.py:643
  17.1 13.0 %collective-permute-start.2 = (bf16[2,528,128]{2,1,0:T(8,128)(2,1)S(1)}, bf16[2,528,128]{2,1,0:T(8,128)(2,1)S(1)}, u32[]{:S(2)}, u32[]{:S(2)}) collective-permute-start(bf16[2,528,128]{2,1,0:T(8,128)(2,1)S(1)} %pad_maximum_fusion.1.refs_0_), channel_id=1, source_target_pairs={{0,96},{32,64},{64,32},{96,0},{1,97},{33,65},{65,33},{97,1},{2,98}... | collective-permute-start | bytes 811016 | tf_op jit(solution)/shard_map/ppermute | solution.py:643
  18.1 12.3 %collective-permute-start.1 = (bf16[2,528,128]{2,1,0:T(8,128)(2,1)S(1)}, bf16[2,528,128]{2,1,0:T(8,128)(2,1)S(1)}, u32[]{:S(2)}, u32[]{:S(2)}) collective-permute-start(bf16[2,528,128]{2,1,0:T(8,128)(2,1)S(1)} %pad_maximum_fusion.1.refs_0_), channel_id=1, source_target_pairs={{0,32},{32,0},{64,96},{96,64},{1,33},{33,1},{65,97},{97,65},{2,34}... | collective-permute-start | bytes 811016 | tf_op jit(solution)/shard_map/ppermute | solution.py:643
  18.1 10.5 %collective-permute-start.6 = (bf16[528,128]{1,0:T(8,128)(2,1)S(1)}, bf16[528,128]{1,0:T(8,128)(2,1)S(1)}, u32[]{:S(2)}, u32[]{:S(2)}) collective-permute-start(bf16[528,128]{1,0:T(8,128)(2,1)S(1)} %slice_select_fusion), channel_id=1, source_target_pairs={{0,16},{16,0},{1,17},{17,1},{2,18},{18,2},{3,19},{19,3},{4,20},{20... | collective-permute-start | bytes 405512 | tf_op jit(solution)/shard_map/ppermute | solution.py:639
  18.7 9.9 %collective-permute-start.5 = (f32[1,512]{1,0:T(1,128)S(1)}, f32[1,512]{1,0:T(1,128)S(1)}, u32[]{:S(2)}, u32[]{:S(2)}) collective-permute-start(f32[1,512]{1,0:T(1,128)S(1)} %max.27), channel_id=1, source_target_pairs={{0,2},{2,0},{1,3},{3,1},{4,6},{6,4},{5,7},{7,5},{8,10},{10,8},{9,1... | collective-permute-start | bytes 6152 | tf_op jit(solution)/shard_map/ppermute | solution.py:639
  34.1 13.0 %collective-permute-start.14 = (f32[2,1,512]{2,1,0:T(1,128)S(1)}, f32[2,1,512]{2,1,0:T(1,128)S(1)}, u32[]{:S(2)}, u32[]{:S(2)}) collective-permute-start(f32[2,1,512]{2,1,0:T(1,128)S(1)} %pad_maximum_fusion.3.refs_8_), channel_id=1, source_target_pairs={{0,64},{32,96},{64,0},{96,32},{1,65},{33,97},{65,1},{97,33},{2,66}... | collective-permute-start | bytes 12296 | tf_op jit(solution)/shard_map/ppermute | solution.py:643
  36.3 10.8 %collective-permute-start.13 = (f32[2,1,512]{2,1,0:T(1,128)S(1)}, f32[2,1,512]{2,1,0:T(1,128)S(1)}, u32[]{:S(2)}, u32[]{:S(2)}) collective-permute-start(f32[2,1,512]{2,1,0:T(1,128)S(1)} %pad_maximum_fusion.3.refs_8_), channel_id=1, source_target_pairs={{0,96},{32,64},{64,32},{96,0},{1,97},{33,65},{65,33},{97,1},{2,98}... | collective-permute-start | bytes 12296 | tf_op jit(solution)/shard_map/ppermute | solution.py:643
  38.2 8.9 %collective-permute-start.12 = (f32[2,1,512]{2,1,0:T(1,128)S(1)}, f32[2,1,512]{2,1,0:T(1,128)S(1)}, u32[]{:S(2)}, u32[]{:S(2)}) collective-permute-start(f32[2,1,512]{2,1,0:T(1,128)S(1)} %pad_maximum_fusion.3.refs_8_), channel_id=1, source_target_pairs={{0,32},{32,0},{64,96},{96,64},{1,33},{33,1},{65,97},{97,65},{2,34}... | collective-permute-start | bytes 12296 | tf_op jit(solution)/shard_map/ppermute | solution.py:643
  38.2 8.8 %collective-permute-start.15 = (bf16[2,528,128]{2,1,0:T(8,128)(2,1)S(1)}, bf16[2,528,128]{2,1,0:T(8,128)(2,1)S(1)}, u32[]{:S(2)}, u32[]{:S(2)}) collective-permute-start(bf16[2,528,128]{2,1,0:T(8,128)(2,1)S(1)} %pad_maximum_fusion.2), channel_id=1, source_target_pairs={{0,32},{32,0},{64,96},{96,64},{1,33},{33,1},{65,97},{97,65},{2,34}... | collective-permute-start | bytes 811016 | tf_op jit(solution)/shard_map/ppermute | solution.py:643
  47.3 19.8 %collective-permute-start.21 = (bf16[2,2,528,128]{3,2,1,0:T(8,128)(2,1)S(1)}, bf16[2,2,528,128]{3,2,1,0:T(8,128)(2,1)S(1)}, u32[]{:S(2)}, u32[]{:S(2)}) collective-permute-start(bf16[2,2,528,128]{3,2,1,0:T(8,128)(2,1)S(1)} %pad_maximum_fusion), channel_id=1, source_target_pairs={{0,96},{32,64},{64,32},{96,0},{1,97},{33,65},{65,33},{97,1},{2,98}... | collective-permute-start | bytes 1622024 | tf_op jit(solution)/shard_map/ppermute | solution.py:643
  48.8 9.5 %collective-permute-start.17 = (f32[2,1,512]{2,1,0:T(1,128)S(1)}, f32[2,1,512]{2,1,0:T(1,128)S(1)}, u32[]{:S(2)}, u32[]{:S(2)}) collective-permute-start(f32[2,1,512]{2,1,0:T(1,128)S(1)} %pad_maximum_fusion.5), channel_id=1, source_target_pairs={{0,2},{2,0},{1,3},{3,1},{4,6},{6,4},{5,7},{7,5},{8,10},{10,8},{9,1... | collective-permute-start | bytes 12296 | tf_op jit(solution)/shard_map/ppermute | solution.py:639
  58.3 5.6 %collective-permute-start.20 = (f32[1,2176]{1,0:T(1,128)S(1)}, f32[1,2176]{1,0:T(1,128)S(1)}, u32[]{:S(2)}, u32[]{:S(2)}) collective-permute-start(f32[1,2176]{1,0:T(1,128)S(1)} %get-tuple-element.251), channel_id=1, source_target_pairs={{0,8},{4,12},{8,0},{12,4},{1,9},{5,13},{9,1},{13,5},{2,10},{6,14},... | collective-permute-start | bytes 26120 | tf_op jit(solution)/shard_map/ppermute | solution.py:688
  72.2 5.5 %collective-permute-start.29 = (f32[1,8192]{1,0:T(1,128)S(1)}, f32[1,8192]{1,0:T(1,128)S(1)}, u32[]{:S(2)}, u32[]{:S(2)}) collective-permute-start(f32[1,8192]{1,0:T(1,128)S(1)} %add.133), channel_id=1, source_target_pairs={{0,2},{2,0},{16,18},{18,16},{1,3},{3,1},{17,19},{19,17},{4,6},{6,4... | collective-permute-start | bytes 98312 | tf_op jit(solution)/shard_map/ppermute | solution.py:688
  73.1 5.1 %collective-permute-start.28 = (f32[1,8192]{1,0:T(1,128)S(1)}, f32[1,8192]{1,0:T(1,128)S(1)}, u32[]{:S(2)}, u32[]{:S(2)}) collective-permute-start(f32[1,8192]{1,0:T(1,128)S(1)} %add.133), channel_id=1, source_target_pairs={{0,18},{2,16},{16,2},{18,0},{1,19},{3,17},{17,3},{19,1},{4,22},{6,... | collective-permute-start | bytes 98312 | tf_op jit(solution)/shard_map/ppermute | solution.py:688
  79.4 5.8 %collective-permute-start.32 = (f32[1,8192]{1,0:T(1,128)S(1)}, f32[1,8192]{1,0:T(1,128)S(1)}, u32[]{:S(2)}, u32[]{:S(2)}) collective-permute-start(f32[1,8192]{1,0:T(1,128)S(1)} %add_add_fusion.1), channel_id=1, source_target_pairs={{0,64},{32,96},{64,0},{96,32},{1,65},{33,97},{65,1},{97,33},{2,66}... | collective-permute-start | bytes 98312 | tf_op jit(solution)/shard_map/ppermute | solution.py:688
  89.9 10.1 %collective-permute-start.35 = (f32[1,2048]{1,0:T(1,128)S(1)}, f32[1,2048]{1,0:T(1,128)S(1)}, u32[]{:S(2)}, u32[]{:S(2)}) collective-permute-start(f32[1,2048]{1,0:T(1,128)S(1)} %col_step.2), channel_id=1, source_target_pairs={{0,8},{4,12},{8,0},{12,4},{1,9},{5,13},{9,1},{13,5},{2,10},{6,14},... | collective-permute-start | bytes 24584 | tf_op jit(solution)/shard_map/ppermute | solution.py:688
  91.9 8.1 %collective-permute-start.34 = (f32[1,2048]{1,0:T(1,128)S(1)}, f32[1,2048]{1,0:T(1,128)S(1)}, u32[]{:S(2)}, u32[]{:S(2)}) collective-permute-start(f32[1,2048]{1,0:T(1,128)S(1)} %col_step.2), channel_id=1, source_target_pairs={{0,12},{4,8},{8,4},{12,0},{1,13},{5,9},{9,5},{13,1},{2,14},{6,10},... | collective-permute-start | bytes 24584 | tf_op jit(solution)/shard_map/ppermute | solution.py:688
  92.5 7.5 %collective-permute-start.33 = (f32[1,2048]{1,0:T(1,128)S(1)}, f32[1,2048]{1,0:T(1,128)S(1)}, u32[]{:S(2)}, u32[]{:S(2)}) collective-permute-start(f32[1,2048]{1,0:T(1,128)S(1)} %col_step.2), channel_id=1, source_target_pairs={{0,4},{4,0},{8,12},{12,8},{1,5},{5,1},{9,13},{13,9},{2,6},{6,2},{1... | collective-permute-start | bytes 24584 | tf_op jit(solution)/shard_map/ppermute | solution.py:688
  103.8 10.1 %collective-permute-start.39 = (f32[1,4096]{1,0:T(1,128)S(1)}, f32[1,4096]{1,0:T(1,128)S(1)}, u32[]{:S(2)}, u32[]{:S(2)}) collective-permute-start(f32[1,4096]{1,0:T(1,128)S(1)} %add.143), channel_id=1, source_target_pairs={{0,2},{2,0},{16,18},{18,16},{1,3},{3,1},{17,19},{19,17},{4,6},{6,4... | collective-permute-start | bytes 49160 | tf_op jit(solution)/shard_map/ppermute | solution.py:688
  104.7 9.2 %collective-permute-start.38 = (f32[1,4096]{1,0:T(1,128)S(1)}, f32[1,4096]{1,0:T(1,128)S(1)}, u32[]{:S(2)}, u32[]{:S(2)}) collective-permute-start(f32[1,4096]{1,0:T(1,128)S(1)} %add.143), channel_id=1, source_target_pairs={{0,18},{2,16},{16,2},{18,0},{1,19},{3,17},{17,3},{19,1},{4,22},{6,... | collective-permute-start | bytes 49160 | tf_op jit(solution)/shard_map/ppermute | solution.py:688
  106.7 7.1 %collective-permute-start.37 = (f32[1,4096]{1,0:T(1,128)S(1)}, f32[1,4096]{1,0:T(1,128)S(1)}, u32[]{:S(2)}, u32[]{:S(2)}) collective-permute-start(f32[1,4096]{1,0:T(1,128)S(1)} %add.143), channel_id=1, source_target_pairs={{0,16},{2,18},{16,0},{18,2},{1,17},{3,19},{17,1},{19,3},{4,20},{6,... | collective-permute-start | bytes 49160 | tf_op jit(solution)/shard_map/ppermute | solution.py:688
  113.9 5.3 %collective-permute-start.42 = (f32[1,4096]{1,0:T(1,128)S(1)}, f32[1,4096]{1,0:T(1,128)S(1)}, u32[]{:S(2)}, u32[]{:S(2)}) collective-permute-start(f32[1,4096]{1,0:T(1,128)S(1)} %add_add_fusion.5), channel_id=1, source_target_pairs={{0,64},{32,96},{64,0},{96,32},{1,65},{33,97},{65,1},{97,33},{2,66}... | collective-permute-start | bytes 49160 | tf_op jit(solution)/shard_map/ppermute | solution.py:688
  124.0 5.2 %collective-permute-start.45 = (f32[1,2048]{1,0:T(1,128)S(1)}, f32[1,2048]{1,0:T(1,128)S(1)}, u32[]{:S(2)}, u32[]{:S(2)}) collective-permute-start(f32[1,2048]{1,0:T(1,128)S(1)} %col_step.3), channel_id=1, source_target_pairs={{0,8},{4,12},{8,0},{12,4},{1,9},{5,13},{9,1},{13,5},{2,10},{6,14},... | collective-permute-start | bytes 24584 | tf_op jit(solution)/shard_map/ppermute | solution.py:688
  135.8 7.7 %collective-permute-start.49 = (f32[1,4096]{1,0:T(1,128)S(1)}, f32[1,4096]{1,0:T(1,128)S(1)}, u32[]{:S(2)}, u32[]{:S(2)}) collective-permute-start(f32[1,4096]{1,0:T(1,128)S(1)} %add.153), channel_id=1, source_target_pairs={{0,2},{2,0},{16,18},{18,16},{1,3},{3,1},{17,19},{19,17},{4,6},{6,4... | collective-permute-start | bytes 49160 | tf_op jit(solution)/shard_map/ppermute | solution.py:688
  137.9 5.6 %collective-permute-start.48 = (f32[1,4096]{1,0:T(1,128)S(1)}, f32[1,4096]{1,0:T(1,128)S(1)}, u32[]{:S(2)}, u32[]{:S(2)}) collective-permute-start(f32[1,4096]{1,0:T(1,128)S(1)} %add.153), channel_id=1, source_target_pairs={{0,18},{2,16},{16,2},{18,0},{1,19},{3,17},{17,3},{19,1},{4,22},{6,... | collective-permute-start | bytes 49160 | tf_op jit(solution)/shard_map/ppermute | solution.py:688
  143.7 6.1 %collective-permute-start.52 = (f32[1,4096]{1,0:T(1,128)S(1)}, f32[1,4096]{1,0:T(1,128)S(1)}, u32[]{:S(2)}, u32[]{:S(2)}) collective-permute-start(f32[1,4096]{1,0:T(1,128)S(1)} %add_add_fusion.3), channel_id=1, source_target_pairs={{0,64},{32,96},{64,0},{96,32},{1,65},{33,97},{65,1},{97,33},{2,66}... | collective-permute-start | bytes 49160 | tf_op jit(solution)/shard_map/ppermute | solution.py:688
  153.3 5.4 %collective-permute-start.53 = (bf16[16,128,256]{2,1,0:T(8,128)(2,1)S(1)}, bf16[16,128,256]{2,1,0:T(8,128)(2,1)S(1)}, u32[]{:S(2)}, u32[]{:S(2)}) collective-permute-start(bf16[16,128,256]{2,1,0:T(8,128)(2,1)S(1)} %get-tuple-element.346), channel_id=1, source_target_pairs={{0,1},{1,0},{2,3},{3,2},{4,5},{5,4},{6,7},{7,6},{8,9},{9,8},{10,11... | collective-permute-start | bytes 3145736 | tf_op jit(solution)/shard_map/ppermute | solution.py:639
  160.1 21.6 %all-to-all-start = ((bf16[16,128,256]{2,1,0:T(8,128)(2,1)}), bf16[16,128,256]{2,1,0:T(8,128)(2,1)S(1)}, u32[]{:S(2)}, u32[]{:S(2)}) async-start(bf16[16,128,256]{2,1,0:T(8,128)(2,1)} %add_convert_fusion), calls=%async_computation | async-start | bytes 2097152 | tf_op jit(solution)/shard_map/all_to_all | solution.py:647
  165.3 9.2 %collective-permute-start.54 = (bf16[512,256]{1,0:T(8,128)(2,1)S(1)}, bf16[512,256]{1,0:T(8,128)(2,1)S(1)}, u32[]{:S(2)}, u32[]{:S(2)}) collective-permute-start(bf16[512,256]{1,0:T(8,128)(2,1)S(1)} %get-tuple-element.359), channel_id=1, source_target_pairs={{0,4},{4,0},{8,12},{12,8},{1,5},{5,1},{9,13},{13,9},{2,6},{6,2},{1... | collective-permute-start | bytes 786440 | tf_op jit(solution)/shard_map/ppermute | solution.py:643
  165.4 13.7 %collective-permute-start.55 = (bf16[512,256]{1,0:T(8,128)(2,1)S(1)}, bf16[512,256]{1,0:T(8,128)(2,1)S(1)}, u32[]{:S(2)}, u32[]{:S(2)}) collective-permute-start(bf16[512,256]{1,0:T(8,128)(2,1)S(1)} %get-tuple-element.360), channel_id=1, source_target_pairs={{0,12},{4,8},{8,4},{12,0},{1,13},{5,9},{9,5},{13,1},{2,14},{6,10},... | collective-permute-start | bytes 786440 | tf_op jit(solution)/shard_map/ppermute | solution.py:643
  167.5 13.4 %collective-permute-start.56 = (bf16[512,256]{1,0:T(8,128)(2,1)S(1)}, bf16[512,256]{1,0:T(8,128)(2,1)S(1)}, u32[]{:S(2)}, u32[]{:S(2)}) collective-permute-start(bf16[512,256]{1,0:T(8,128)(2,1)S(1)} %get-tuple-element.361), channel_id=1, source_target_pairs={{0,8},{4,12},{8,0},{12,4},{1,9},{5,13},{9,1},{13,5},{2,10},{6,14},... | collective-permute-start | bytes 786440 | tf_op jit(solution)/shard_map/ppermute | solution.py:643
  (27 other events, 91.3 us)

commit v4 on v3

--- a/solution.py
+++ b/solution.py
@@ -673,7 +673,7 @@
 
 
 def scatter_protos(pieces):
-    return [pieces[0]] + [from_xor(pieces[mask], "z", mask) for mask in (1, 3, 2)]
+    return [pieces[0]] + [from_xor(pieces[mask], "z", mask) for mask in (2, 3, 1)]
 
 
 def choose(first, one, two):

time: 183 us -> 184 us (level)
  transfers between devices with their start and end apart: 58 -> 58, of which waited for: 24 -> 23; matrix products, arithmetic and copies ran while one was open for 1% -> 1% of each run, Pallas kernels for 32% -> 32%
where the time goes in v4:
time: 184 us; the launch traced here: 183 us
  Pallas kernels  73.9 us (40%)
  starting transfers between devices  65.9 us (36%)
  waiting for transfers between devices  35.8 us (19%)
  other arithmetic  3.77 us (2%)
  between operations  1.89 us (1%)
    ppermute x27, starting transfers between devices, ring(): lax.ppermute(value, axes, [(i, i ^ mask) for i in range(4)])  34.2 us
    ppermute x27, waiting for transfers between devices, ring(): lax.ppermute(value, axes, [(i, i ^ mask) for i in range(4)])  17.6 us
    ppermute x11, starting transfers between devices, from_xor(): return lax.ppermute(value, axis, [(i, i ^ mask) for i in range(4)])  15.4 us
    pallas_call x2, Pallas kernels, row_soft(): pl.pallas_call(soft_kernel, grid=(steps,), out_shape=(jax.ShapeDtypeStruc...  13.6 us
    pallas_call x2, Pallas kernels, student_step(): pl.pallas_call(functools.partial(student_kernel, part), out_shape=outs, i...  13 us
    ppermute x11, waiting for transfers between devices, from_xor(): return lax.ppermute(value, axis, [(i, i ^ mask) for i in range(4)])  12.7 us
    ppermute x19, starting transfers between devices, swap(): return lax.ppermute(value, axis, [(0, 1), (1, 0)])  11.2 us
    pallas_call x1, Pallas kernels, row_max(): pl.pallas_call(max_kernel, grid=(steps,), out_shape=jax.ShapeDtypeStruct(...  8.92 us
  transfers between devices with their start and end apart: 58, of which 23 were waited for; matrix products, arithmetic and copies ran while one was open for 1% of the time, Pallas kernels for 32%

profile of v4, /device:TPU:0, one launch (start us, length us, event | category | flops | bytes accessed | tf_op | source)
XLA Modules:
  0.0 182.6 jit_solution(12188021726530573697)
XLA Ops:
  4.7 8.9 %row_max.1 = f32[1,512]{1,0:T(1,128)S(1)} custom-call(bf16[528,256]{1,0:T(8,128)(2,1)S(1)} %get-tuple-element.186.teach_ref, bf16[16384,256]{1,0:T(8,128)(2,1)} %refs_8_.1), custom_call_target="tpu_custom_call" | custom-call | flops 6442450944 | bytes 1048576 | tf_op jit(solution)/shard_map/row_max/pallas_call | solution.py:136
  13.9 3.2 %collective-permute-start.3 = (bf16[2,528,128]{2,1,0:T(8,128)(2,1)S(1)}, bf16[2,528,128]{2,1,0:T(8,128)(2,1)S(1)}, u32[]{:S(2)}, u32[]{:S(2)}) collective-permute-start(bf16[2,528,128]{2,1,0:T(8,128)(2,1)S(1)} %pad_maximum_fusion.1.refs_0_), channel_id=1, source_target_pairs={{0,64},{32,96},{64,0},{96,32},{1,65},{33,97},{65,1},{97,33},{2,66}... | collective-permute-start | bytes 811016 | tf_op jit(solution)/shard_map/ppermute | solution.py:643
  18.7 3.1 %collective-permute-start.5 = (f32[1,512]{1,0:T(1,128)S(1)}, f32[1,512]{1,0:T(1,128)S(1)}, u32[]{:S(2)}, u32[]{:S(2)}) collective-permute-start(f32[1,512]{1,0:T(1,128)S(1)} %max.27), channel_id=1, source_target_pairs={{0,2},{2,0},{1,3},{3,1},{4,6},{6,4},{5,7},{7,5},{8,10},{10,8},{9,1... | collective-permute-start | bytes 6152 | tf_op jit(solution)/shard_map/ppermute | solution.py:639
  21.8 6.8 %row_soft.2 = (f32[1,512]{1,0:T(1,128)S(1)}, f32[1,512]{1,0:T(1,128)S(1)}) custom-call(bf16[528,256]{1,0:T(8,128)(2,1)S(1)} %get-tuple-element.219.feat_ref, bf16[16384,256]{1,0:T(8,128)(2,1)} %refs_8_.1), custom_call_target="tpu_custom_call" | custom-call | flops 3221225472 | bytes 1048576 | tf_op jit(solution)/shard_map/row_soft/pallas_call | solution.py:179
  34.1 2.2 %collective-permute-start.14 = (f32[2,1,512]{2,1,0:T(1,128)S(1)}, f32[2,1,512]{2,1,0:T(1,128)S(1)}, u32[]{:S(2)}, u32[]{:S(2)}) collective-permute-start(f32[2,1,512]{2,1,0:T(1,128)S(1)} %pad_maximum_fusion.3.refs_8_), channel_id=1, source_target_pairs={{0,64},{32,96},{64,0},{96,32},{1,65},{33,97},{65,1},{97,33},{2,66}... | collective-permute-start | bytes 12296 | tf_op jit(solution)/shard_map/ppermute | solution.py:643
  38.2 2.0 %collective-permute-start.15 = (bf16[2,528,128]{2,1,0:T(8,128)(2,1)S(1)}, bf16[2,528,128]{2,1,0:T(8,128)(2,1)S(1)}, u32[]{:S(2)}, u32[]{:S(2)}) collective-permute-start(bf16[2,528,128]{2,1,0:T(8,128)(2,1)S(1)} %pad_maximum_fusion.2), channel_id=1, source_target_pairs={{0,32},{32,0},{64,96},{96,64},{1,33},{33,1},{65,97},{97,65},{2,34}... | collective-permute-start | bytes 811016 | tf_op jit(solution)/shard_map/ppermute | solution.py:643
  40.2 6.8 %row_soft.3 = (f32[1,512]{1,0:T(1,128)S(1)}, f32[1,512]{1,0:T(1,128)S(1)}) custom-call(bf16[528,256]{1,0:T(8,128)(2,1)S(1)} %get-tuple-element.219.feat_ref, bf16[16384,256]{1,0:T(8,128)(2,1)} %refs_8_.1), custom_call_target="tpu_custom_call" | custom-call | flops 3221225472 | bytes 1048576 | tf_op jit(solution)/shard_map/row_soft/pallas_call | solution.py:179
  48.8 2.8 %collective-permute-start.17 = (f32[2,1,512]{2,1,0:T(1,128)S(1)}, f32[2,1,512]{2,1,0:T(1,128)S(1)}, u32[]{:S(2)}, u32[]{:S(2)}) collective-permute-start(f32[2,1,512]{2,1,0:T(1,128)S(1)} %pad_maximum_fusion.5), channel_id=1, source_target_pairs={{0,2},{2,0},{1,3},{3,1},{4,6},{6,4},{5,7},{7,5},{8,10},{10,8},{9,1... | collective-permute-start | bytes 12296 | tf_op jit(solution)/shard_map/ppermute | solution.py:639
  51.6 6.7 %expo.1 = (bf16[8,2048,512]{2,1,0:T(8,128)(2,1)S(1)}, f32[1,2176]{1,0:T(1,128)S(1)}, f32[1,4096]{1,0:T(1,128)S(1)}, s32[24]{0:T(128)S(1)}) custom-call(s32[4]{0:T(128)S(1)} %pad_add_fusion.place, bf16[2,528,128]{2,1,0:T(8,128)(2,1)S(1)} %pad_maximum_fusion.1.refs_0_, bf16[2,528,128]{2,1,0:T(8,128)(2,1)S(1)} %collective-permute-done.1.refs_1_, ...), custom_call_target="tpu_custom_call" | custom-call | flops 4294967296 | bytes 1048576 | tf_op jit(solution)/shard_map/expo/pallas_call | solution.py:305
  58.3 4.0 %collective-permute-start.20 = (f32[1,2176]{1,0:T(1,128)S(1)}, f32[1,2176]{1,0:T(1,128)S(1)}, u32[]{:S(2)}, u32[]{:S(2)}) collective-permute-start(f32[1,2176]{1,0:T(1,128)S(1)} %get-tuple-element.251), channel_id=1, source_target_pairs={{0,8},{4,12},{8,0},{12,4},{1,9},{5,13},{9,1},{13,5},{2,10},{6,14},... | collective-permute-start | bytes 26120 | tf_op jit(solution)/shard_map/ppermute | solution.py:688
  63.9 3.2 %collective-permute-done.19 = f32[1,2176]{1,0:T(1,128)S(1)} collective-permute-done((f32[1,2176]{1,0:T(1,128)S(1)}, f32[1,2176]{1,0:T(1,128)S(1)}, u32[]{:S(2)}, u32[]{:S(2)}) %collective-permute-start.19) | collective-permute-done | bytes 8736 | tf_op jit(solution)/shard_map/ppermute | solution.py:688
  68.3 2.5 %row_step.3 = f32[1,8192]{1,0:T(1,128)S(1)} custom-call(s32[4]{0:T(128)S(1)} %pad_add_fusion.place, s32[24]{0:T(128)S(1)} %get-tuple-element.244.meta, f32[1,2176]{1,0:T(1,128)S(1)} %add_add_fusion.6.total_ref, bf16[8,2048,512]{2,1,0:T(8,128)(2,1)S(1)} %get-tuple-element.259.expo_ref, f32[1,512]{1,0:T(1,128)S(1)} %multiply_add_fusion.refs_0_), custom_call_target="tpu_custom_call" | custom-call | flops 3355443200 | bytes 1048576 | tf_op jit(solution)/shard_map/row_step/pallas_call | solution.py:358
  73.1 2.4 %collective-permute-start.28 = (f32[1,8192]{1,0:T(1,128)S(1)}, f32[1,8192]{1,0:T(1,128)S(1)}, u32[]{:S(2)}, u32[]{:S(2)}) collective-permute-start(f32[1,8192]{1,0:T(1,128)S(1)} %add.133), channel_id=1, source_target_pairs={{0,18},{2,16},{16,2},{18,0},{1,19},{3,17},{17,3},{19,1},{4,22},{6,... | collective-permute-start | bytes 98312 | tf_op jit(solution)/shard_map/ppermute | solution.py:688
  83.0 2.2 %load_student.1 = (bf16[4608,256]{1,0:T(8,128)(2,1)S(1)}, f32[8,512]{1,0:T(8,128)S(1)}, bf16[2048,256]{1,0:T(8,128)(2,1)S(1)}, bf16[256,2048]{1,0:T(8,128)(2,1)S(1)}) custom-call(s32[4]{0:T(128)S(1)} %pad_add_fusion.place, s32[24]{0:T(128)S(1)} %get-tuple-element.244.meta, bf16[2,528,128]{2,1,0:T(8,128)(2,1)S(1)} %get-tuple-element.279.refs_0_, ...), custom_call_target="tpu_custom_call" | custom-call | flops 2147483648 | bytes 1048576 | tf_op jit(solution)/shard_map/load_student/pallas_call | solution.py:438
  86.7 3.2 %col_step.2 = f32[1,2048]{1,0:T(1,128)S(1)} custom-call(s32[24]{0:T(128)S(1)} %get-tuple-element.244.meta, f32[1,8192]{1,0:T(1,128)S(1)} %add_add_fusion.total_ref.all_ref, f32[1,4096]{1,0:T(1,128)S(1)} %get-tuple-element.295.valid_ref, bf16[8,2048,512]{2,1,0:T(8,128)(2,1)S(1)} %get-tuple-element.259.expo_ref), custom_call_target="tpu_custom_call" | custom-call | flops 3355443200 | bytes 1048576 | tf_op jit(solution)/shard_map/col_step/pallas_call | solution.py:391
  93.5 6.5 %student.2 = (bf16[512,256]{1,0:T(8,128)(2,1)S(1)}, bf16[512,256]{1,0:T(8,128)(2,1)S(1)}, bf16[4096,256]{1,0:T(8,128)(2,1)S(1)}) custom-call(s32[4]{0:T(128)S(1)} %pad_add_fusion.place, s32[24]{0:T(128)S(1)} %get-tuple-element.244.meta, bf16[4608,256]{1,0:T(8,128)(2,1)S(1)} %get-tuple-element.298.rows_ref, f32[1,8192]{1,0:T(1,128)S(1)} %add_add_fusion.total_ref.all_ref, ...), custom_call_target="tpu_custom_call" | custom-call | flops 6442450944 | bytes 1048576 | tf_op jit(solution)/shard_map/student/pallas_call | solution.py:498
  100.0 2.5 %row_step.4 = f32[1,4096]{1,0:T(1,128)S(1)} custom-call(s32[4]{0:T(128)S(1)} %pad_add_fusion.place, s32[24]{0:T(128)S(1)} %get-tuple-element.244.meta, f32[1,2048]{1,0:T(1,128)S(1)} %add_add_fusion.8.total_ref, bf16[8,2048,512]{2,1,0:T(8,128)(2,1)S(1)} %get-tuple-element.259.expo_ref), custom_call_target="tpu_custom_call" | custom-call | flops 3355443200 | bytes 1048576 | tf_op jit(solution)/shard_map/row_step/pallas_call | solution.py:358
  104.7 2.1 %collective-permute-start.38 = (f32[1,4096]{1,0:T(1,128)S(1)}, f32[1,4096]{1,0:T(1,128)S(1)}, u32[]{:S(2)}, u32[]{:S(2)}) collective-permute-start(f32[1,4096]{1,0:T(1,128)S(1)} %add.143), channel_id=1, source_target_pairs={{0,18},{2,16},{16,2},{18,0},{1,19},{3,17},{17,3},{19,1},{4,22},{6,... | collective-permute-start | bytes 49160 | tf_op jit(solution)/shard_map/ppermute | solution.py:688
  107.3 6.5 %student.3 = (bf16[512,256]{1,0:T(8,128)(2,1)S(1)}, bf16[512,256]{1,0:T(8,128)(2,1)S(1)}, bf16[4096,256]{1,0:T(8,128)(2,1)S(1)}) custom-call(s32[4]{0:T(128)S(1)} %pad_add_fusion.place, s32[24]{0:T(128)S(1)} %get-tuple-element.244.meta, bf16[4608,256]{1,0:T(8,128)(2,1)S(1)} %get-tuple-element.298.rows_ref, f32[1,8192]{1,0:T(1,128)S(1)} %add_add_fusion.total_ref.all_ref, ...), custom_call_target="tpu_custom_call" | custom-call | flops 6442450944 | bytes 1048576 | tf_op jit(solution)/shard_map/student/pallas_call | solution.py:498
  120.8 3.2 %col_step.3 = f32[1,2048]{1,0:T(1,128)S(1)} custom-call(s32[24]{0:T(128)S(1)} %get-tuple-element.244.meta, f32[1,4096]{1,0:T(1,128)S(1)} %add_add_fusion.4.total_ref, f32[1,4096]{1,0:T(1,128)S(1)} %get-tuple-element.295.valid_ref, bf16[8,2048,512]{2,1,0:T(8,128)(2,1)S(1)} %get-tuple-element.259.expo_ref), custom_call_target="tpu_custom_call" | custom-call | flops 3355443200 | bytes 1048576 | tf_op jit(solution)/shard_map/col_step/pallas_call | solution.py:391
  124.0 3.2 %collective-permute-start.45 = (f32[1,2048]{1,0:T(1,128)S(1)}, f32[1,2048]{1,0:T(1,128)S(1)}, u32[]{:S(2)}, u32[]{:S(2)}) collective-permute-start(f32[1,2048]{1,0:T(1,128)S(1)} %col_step.3), channel_id=1, source_target_pairs={{0,8},{4,12},{8,0},{12,4},{1,9},{5,13},{9,1},{13,5},{2,10},{6,14},... | collective-permute-start | bytes 24584 | tf_op jit(solution)/shard_map/ppermute | solution.py:688
  129.2 2.8 %collective-permute-done.44 = f32[1,2048]{1,0:T(1,128)S(1)} collective-permute-done((f32[1,2048]{1,0:T(1,128)S(1)}, f32[1,2048]{1,0:T(1,128)S(1)}, u32[]{:S(2)}, u32[]{:S(2)}) %collective-permute-start.44) | collective-permute-done | bytes 8224 | tf_op jit(solution)/shard_map/ppermute | solution.py:688
  132.1 2.5 %row_step.5 = f32[1,4096]{1,0:T(1,128)S(1)} custom-call(s32[4]{0:T(128)S(1)} %pad_add_fusion.place, s32[24]{0:T(128)S(1)} %get-tuple-element.244.meta, f32[1,2048]{1,0:T(1,128)S(1)} %add_add_fusion.7.total_ref.col_ref, bf16[8,2048,512]{2,1,0:T(8,128)(2,1)S(1)} %get-tuple-element.259.expo_ref), custom_call_target="tpu_custom_call" | custom-call | flops 3355443200 | bytes 1048576 | tf_op jit(solution)/shard_map/row_step/pallas_call | solution.py:358
  135.8 2.1 %collective-permute-start.49 = (f32[1,4096]{1,0:T(1,128)S(1)}, f32[1,4096]{1,0:T(1,128)S(1)}, u32[]{:S(2)}, u32[]{:S(2)}) collective-permute-start(f32[1,4096]{1,0:T(1,128)S(1)} %add.153), channel_id=1, source_target_pairs={{0,2},{2,0},{16,18},{18,16},{1,3},{3,1},{17,19},{19,17},{4,6},{6,4... | collective-permute-start | bytes 49160 | tf_op jit(solution)/shard_map/ppermute | solution.py:688
  137.9 2.1 %collective-permute-start.48 = (f32[1,4096]{1,0:T(1,128)S(1)}, f32[1,4096]{1,0:T(1,128)S(1)}, u32[]{:S(2)}, u32[]{:S(2)}) collective-permute-start(f32[1,4096]{1,0:T(1,128)S(1)} %add.153), channel_id=1, source_target_pairs={{0,18},{2,16},{16,2},{18,0},{1,19},{3,17},{17,3},{19,1},{4,22},{6,... | collective-permute-start | bytes 49160 | tf_op jit(solution)/shard_map/ppermute | solution.py:688
  139.9 3.5 %feature_step.2.refs_0_ = bf16[4096,256]{1,0:T(8,128)(2,1)S(1)} custom-call(s32[24]{0:T(128)S(1)} %get-tuple-element.244.meta, f32[1,2048]{1,0:T(1,128)S(1)} %add_add_fusion.7.total_ref.col_ref, bf16[8,2048,512]{2,1,0:T(8,128)(2,1)S(1)} %get-tuple-element.259.expo_ref, bf16[256,2048]{1,0:T(8,128)(2,1)S(1)} %get-tuple-element.330.turned_ref), custom_call_target="tpu_custom_call" | custom-call | flops 2147483648 | bytes 1048576 | tf_op jit(solution)/shard_map/feature_step/pallas_call | solution.py:541
  147.3 2.5 %feature_step.3.plan_ref = bf16[4096,256]{1,0:T(8,128)(2,1)S(1)} custom-call(s32[24]{0:T(128)S(1)} %get-tuple-element.244.meta, f32[1,2048]{1,0:T(1,128)S(1)} %add_add_fusion.7.total_ref.col_ref, bf16[8,2048,512]{2,1,0:T(8,128)(2,1)S(1)} %get-tuple-element.259.expo_ref, ...), custom_call_target="tpu_custom_call", output_to_operand_aliasing={{}: (4, {})} | custom-call | flops 2147483648 | bytes 1048576 | tf_op jit(solution)/shard_map/feature_step/pallas_call | solution.py:541
  150.7 2.6 %join_step.1 = (bf16[16,128,256]{2,1,0:T(8,128)(2,1)S(1)}, bf16[16,128,256]{2,1,0:T(8,128)(2,1)S(1)}) custom-call(s32[4]{0:T(128)S(1)} %pad_add_fusion.place, s32[24]{0:T(128)S(1)} %get-tuple-element.244.meta, f32[1,4096]{1,0:T(1,128)S(1)} %add_add_fusion.2.total_ref, f32[1,4096]{1,0:T(1,128)S(1)} %get-tuple-element.295.valid_ref, ...), custom_call_target="tpu_custom_call" | custom-call | flops 2147483648 | bytes 1048576 | tf_op jit(solution)/shard_map/join_step/pallas_call | solution.py:585
  153.4 5.3 %grad_step.1 = (bf16[512,256]{1,0:T(8,128)(2,1)S(1)}, bf16[512,256]{1,0:T(8,128)(2,1)S(1)}, bf16[512,256]{1,0:T(8,128)(2,1)S(1)}, bf16[512,256]{1,0:T(8,128)(2,1)S(1)}) custom-call(s32[4]{0:T(128)S(1)} %pad_add_fusion.place, s32[24]{0:T(128)S(1)} %get-tuple-element.244.meta, f32[1,4096]{1,0:T(1,128)S(1)} %add_add_fusion.2.total_ref, ...), custom_call_target="tpu_custom_call" | custom-call | flops 4294967296 | bytes 1048576 | tf_op jit(solution)/shard_map/grad_step/pallas_call | solution.py:626
  160.1 5.2 %all-to-all-start = ((bf16[16,128,256]{2,1,0:T(8,128)(2,1)}), bf16[16,128,256]{2,1,0:T(8,128)(2,1)S(1)}, u32[]{:S(2)}, u32[]{:S(2)}) async-start(bf16[16,128,256]{2,1,0:T(8,128)(2,1)} %add_convert_fusion), calls=%async_computation | async-start | bytes 2097152 | tf_op jit(solution)/shard_map/all_to_all | solution.py:647
  170.0 6.0 %collective-permute-done.54 = bf16[512,256]{1,0:T(8,128)(2,1)S(1)} collective-permute-done((bf16[512,256]{1,0:T(8,128)(2,1)S(1)}, bf16[512,256]{1,0:T(8,128)(2,1)S(1)}, u32[]{:S(2)}, u32[]{:S(2)}) %collective-permute-start.54) | collective-permute-done | bytes 262176 | tf_op jit(solution)/shard_map/ppermute | solution.py:643
  176.0 4.9 %collective-permute-done.55 = bf16[512,256]{1,0:T(8,128)(2,1)S(1)} collective-permute-done((bf16[512,256]{1,0:T(8,128)(2,1)S(1)}, bf16[512,256]{1,0:T(8,128)(2,1)S(1)}, u32[]{:S(2)}, u32[]{:S(2)}) %collective-permute-start.55) | collective-permute-done | bytes 262176 | tf_op jit(solution)/shard_map/ppermute | solution.py:643
  (140 shorter events, 57.3 us)
Async XLA Ops:
  3.0 10.6 %collective-permute-start = (bf16[528,128]{1,0:T(8,128)(2,1)S(1)}, bf16[528,128]{1,0:T(8,128)(2,1)S(1)}, u32[]{:S(2)}, u32[]{:S(2)}) collective-permute-start(bf16[528,128]{1,0:T(8,128)(2,1)S(1)} %slice_select_fusion.1), channel_id=1, source_target_pairs={{0,16},{16,0},{1,17},{17,1},{2,18},{18,2},{3,19},{19,3},{4,20},{20... | collective-permute-start | bytes 405512 | tf_op jit(solution)/shard_map/ppermute | solution.py:639
  13.9 14.7 %collective-permute-start.3 = (bf16[2,528,128]{2,1,0:T(8,128)(2,1)S(1)}, bf16[2,528,128]{2,1,0:T(8,128)(2,1)S(1)}, u32[]{:S(2)}, u32[]{:S(2)}) collective-permute-start(bf16[2,528,128]{2,1,0:T(8,128)(2,1)S(1)} %pad_maximum_fusion.1.refs_0_), channel_id=1, source_target_pairs={{0,64},{32,96},{64,0},{96,32},{1,65},{33,97},{65,1},{97,33},{2,66}... | collective-permute-start | bytes 811016 | tf_op jit(solution)/shard_map/ppermute | solution.py:643
  17.1 13.0 %collective-permute-start.2 = (bf16[2,528,128]{2,1,0:T(8,128)(2,1)S(1)}, bf16[2,528,128]{2,1,0:T(8,128)(2,1)S(1)}, u32[]{:S(2)}, u32[]{:S(2)}) collective-permute-start(bf16[2,528,128]{2,1,0:T(8,128)(2,1)S(1)} %pad_maximum_fusion.1.refs_0_), channel_id=1, source_target_pairs={{0,96},{32,64},{64,32},{96,0},{1,97},{33,65},{65,33},{97,1},{2,98}... | collective-permute-start | bytes 811016 | tf_op jit(solution)/shard_map/ppermute | solution.py:643
  18.1 12.3 %collective-permute-start.1 = (bf16[2,528,128]{2,1,0:T(8,128)(2,1)S(1)}, bf16[2,528,128]{2,1,0:T(8,128)(2,1)S(1)}, u32[]{:S(2)}, u32[]{:S(2)}) collective-permute-start(bf16[2,528,128]{2,1,0:T(8,128)(2,1)S(1)} %pad_maximum_fusion.1.refs_0_), channel_id=1, source_target_pairs={{0,32},{32,0},{64,96},{96,64},{1,33},{33,1},{65,97},{97,65},{2,34}... | collective-permute-start | bytes 811016 | tf_op jit(solution)/shard_map/ppermute | solution.py:643
  18.1 10.5 %collective-permute-start.6 = (bf16[528,128]{1,0:T(8,128)(2,1)S(1)}, bf16[528,128]{1,0:T(8,128)(2,1)S(1)}, u32[]{:S(2)}, u32[]{:S(2)}) collective-permute-start(bf16[528,128]{1,0:T(8,128)(2,1)S(1)} %slice_select_fusion), channel_id=1, source_target_pairs={{0,16},{16,0},{1,17},{17,1},{2,18},{18,2},{3,19},{19,3},{4,20},{20... | collective-permute-start | bytes 405512 | tf_op jit(solution)/shard_map/ppermute | solution.py:639
  18.7 9.9 %collective-permute-start.5 = (f32[1,512]{1,0:T(1,128)S(1)}, f32[1,512]{1,0:T(1,128)S(1)}, u32[]{:S(2)}, u32[]{:S(2)}) collective-permute-start(f32[1,512]{1,0:T(1,128)S(1)} %max.27), channel_id=1, source_target_pairs={{0,2},{2,0},{1,3},{3,1},{4,6},{6,4},{5,7},{7,5},{8,10},{10,8},{9,1... | collective-permute-start | bytes 6152 | tf_op jit(solution)/shard_map/ppermute | solution.py:639
  34.1 13.0 %collective-permute-start.14 = (f32[2,1,512]{2,1,0:T(1,128)S(1)}, f32[2,1,512]{2,1,0:T(1,128)S(1)}, u32[]{:S(2)}, u32[]{:S(2)}) collective-permute-start(f32[2,1,512]{2,1,0:T(1,128)S(1)} %pad_maximum_fusion.3.refs_8_), channel_id=1, source_target_pairs={{0,64},{32,96},{64,0},{96,32},{1,65},{33,97},{65,1},{97,33},{2,66}... | collective-permute-start | bytes 12296 | tf_op jit(solution)/shard_map/ppermute | solution.py:643
  36.3 10.8 %collective-permute-start.13 = (f32[2,1,512]{2,1,0:T(1,128)S(1)}, f32[2,1,512]{2,1,0:T(1,128)S(1)}, u32[]{:S(2)}, u32[]{:S(2)}) collective-permute-start(f32[2,1,512]{2,1,0:T(1,128)S(1)} %pad_maximum_fusion.3.refs_8_), channel_id=1, source_target_pairs={{0,96},{32,64},{64,32},{96,0},{1,97},{33,65},{65,33},{97,1},{2,98}... | collective-permute-start | bytes 12296 | tf_op jit(solution)/shard_map/ppermute | solution.py:643
  38.2 8.9 %collective-permute-start.12 = (f32[2,1,512]{2,1,0:T(1,128)S(1)}, f32[2,1,512]{2,1,0:T(1,128)S(1)}, u32[]{:S(2)}, u32[]{:S(2)}) collective-permute-start(f32[2,1,512]{2,1,0:T(1,128)S(1)} %pad_maximum_fusion.3.refs_8_), channel_id=1, source_target_pairs={{0,32},{32,0},{64,96},{96,64},{1,33},{33,1},{65,97},{97,65},{2,34}... | collective-permute-start | bytes 12296 | tf_op jit(solution)/shard_map/ppermute | solution.py:643
  38.2 8.8 %collective-permute-start.15 = (bf16[2,528,128]{2,1,0:T(8,128)(2,1)S(1)}, bf16[2,528,128]{2,1,0:T(8,128)(2,1)S(1)}, u32[]{:S(2)}, u32[]{:S(2)}) collective-permute-start(bf16[2,528,128]{2,1,0:T(8,128)(2,1)S(1)} %pad_maximum_fusion.2), channel_id=1, source_target_pairs={{0,32},{32,0},{64,96},{96,64},{1,33},{33,1},{65,97},{97,65},{2,34}... | collective-permute-start | bytes 811016 | tf_op jit(solution)/shard_map/ppermute | solution.py:643
  47.3 19.8 %collective-permute-start.21 = (bf16[2,2,528,128]{3,2,1,0:T(8,128)(2,1)S(1)}, bf16[2,2,528,128]{3,2,1,0:T(8,128)(2,1)S(1)}, u32[]{:S(2)}, u32[]{:S(2)}) collective-permute-start(bf16[2,2,528,128]{3,2,1,0:T(8,128)(2,1)S(1)} %pad_maximum_fusion), channel_id=1, source_target_pairs={{0,96},{32,64},{64,32},{96,0},{1,97},{33,65},{65,33},{97,1},{2,98}... | collective-permute-start | bytes 1622024 | tf_op jit(solution)/shard_map/ppermute | solution.py:643
  48.8 9.5 %collective-permute-start.17 = (f32[2,1,512]{2,1,0:T(1,128)S(1)}, f32[2,1,512]{2,1,0:T(1,128)S(1)}, u32[]{:S(2)}, u32[]{:S(2)}) collective-permute-start(f32[2,1,512]{2,1,0:T(1,128)S(1)} %pad_maximum_fusion.5), channel_id=1, source_target_pairs={{0,2},{2,0},{1,3},{3,1},{4,6},{6,4},{5,7},{7,5},{8,10},{10,8},{9,1... | collective-permute-start | bytes 12296 | tf_op jit(solution)/shard_map/ppermute | solution.py:639
  58.3 5.6 %collective-permute-start.20 = (f32[1,2176]{1,0:T(1,128)S(1)}, f32[1,2176]{1,0:T(1,128)S(1)}, u32[]{:S(2)}, u32[]{:S(2)}) collective-permute-start(f32[1,2176]{1,0:T(1,128)S(1)} %get-tuple-element.251), channel_id=1, source_target_pairs={{0,8},{4,12},{8,0},{12,4},{1,9},{5,13},{9,1},{13,5},{2,10},{6,14},... | collective-permute-start | bytes 26120 | tf_op jit(solution)/shard_map/ppermute | solution.py:688
  72.2 5.5 %collective-permute-start.29 = (f32[1,8192]{1,0:T(1,128)S(1)}, f32[1,8192]{1,0:T(1,128)S(1)}, u32[]{:S(2)}, u32[]{:S(2)}) collective-permute-start(f32[1,8192]{1,0:T(1,128)S(1)} %add.133), channel_id=1, source_target_pairs={{0,2},{2,0},{16,18},{18,16},{1,3},{3,1},{17,19},{19,17},{4,6},{6,4... | collective-permute-start | bytes 98312 | tf_op jit(solution)/shard_map/ppermute | solution.py:688
  73.1 5.1 %collective-permute-start.28 = (f32[1,8192]{1,0:T(1,128)S(1)}, f32[1,8192]{1,0:T(1,128)S(1)}, u32[]{:S(2)}, u32[]{:S(2)}) collective-permute-start(f32[1,8192]{1,0:T(1,128)S(1)} %add.133), channel_id=1, source_target_pairs={{0,18},{2,16},{16,2},{18,0},{1,19},{3,17},{17,3},{19,1},{4,22},{6,... | collective-permute-start | bytes 98312 | tf_op jit(solution)/shard_map/ppermute | solution.py:688
  79.4 5.8 %collective-permute-start.32 = (f32[1,8192]{1,0:T(1,128)S(1)}, f32[1,8192]{1,0:T(1,128)S(1)}, u32[]{:S(2)}, u32[]{:S(2)}) collective-permute-start(f32[1,8192]{1,0:T(1,128)S(1)} %add_add_fusion.1), channel_id=1, source_target_pairs={{0,64},{32,96},{64,0},{96,32},{1,65},{33,97},{65,1},{97,33},{2,66}... | collective-permute-start | bytes 98312 | tf_op jit(solution)/shard_map/ppermute | solution.py:688
  89.9 10.1 %collective-permute-start.35 = (f32[1,2048]{1,0:T(1,128)S(1)}, f32[1,2048]{1,0:T(1,128)S(1)}, u32[]{:S(2)}, u32[]{:S(2)}) collective-permute-start(f32[1,2048]{1,0:T(1,128)S(1)} %col_step.2), channel_id=1, source_target_pairs={{0,8},{4,12},{8,0},{12,4},{1,9},{5,13},{9,1},{13,5},{2,10},{6,14},... | collective-permute-start | bytes 24584 | tf_op jit(solution)/shard_map/ppermute | solution.py:688
  91.9 8.1 %collective-permute-start.34 = (f32[1,2048]{1,0:T(1,128)S(1)}, f32[1,2048]{1,0:T(1,128)S(1)}, u32[]{:S(2)}, u32[]{:S(2)}) collective-permute-start(f32[1,2048]{1,0:T(1,128)S(1)} %col_step.2), channel_id=1, source_target_pairs={{0,12},{4,8},{8,4},{12,0},{1,13},{5,9},{9,5},{13,1},{2,14},{6,10},... | collective-permute-start | bytes 24584 | tf_op jit(solution)/shard_map/ppermute | solution.py:688
  92.5 7.5 %collective-permute-start.33 = (f32[1,2048]{1,0:T(1,128)S(1)}, f32[1,2048]{1,0:T(1,128)S(1)}, u32[]{:S(2)}, u32[]{:S(2)}) collective-permute-start(f32[1,2048]{1,0:T(1,128)S(1)} %col_step.2), channel_id=1, source_target_pairs={{0,4},{4,0},{8,12},{12,8},{1,5},{5,1},{9,13},{13,9},{2,6},{6,2},{1... | collective-permute-start | bytes 24584 | tf_op jit(solution)/shard_map/ppermute | solution.py:688
  103.8 10.1 %collective-permute-start.39 = (f32[1,4096]{1,0:T(1,128)S(1)}, f32[1,4096]{1,0:T(1,128)S(1)}, u32[]{:S(2)}, u32[]{:S(2)}) collective-permute-start(f32[1,4096]{1,0:T(1,128)S(1)} %add.143), channel_id=1, source_target_pairs={{0,2},{2,0},{16,18},{18,16},{1,3},{3,1},{17,19},{19,17},{4,6},{6,4... | collective-permute-start | bytes 49160 | tf_op jit(solution)/shard_map/ppermute | solution.py:688
  104.7 9.2 %collective-permute-start.38 = (f32[1,4096]{1,0:T(1,128)S(1)}, f32[1,4096]{1,0:T(1,128)S(1)}, u32[]{:S(2)}, u32[]{:S(2)}) collective-permute-start(f32[1,4096]{1,0:T(1,128)S(1)} %add.143), channel_id=1, source_target_pairs={{0,18},{2,16},{16,2},{18,0},{1,19},{3,17},{17,3},{19,1},{4,22},{6,... | collective-permute-start | bytes 49160 | tf_op jit(solution)/shard_map/ppermute | solution.py:688
  106.7 7.1 %collective-permute-start.37 = (f32[1,4096]{1,0:T(1,128)S(1)}, f32[1,4096]{1,0:T(1,128)S(1)}, u32[]{:S(2)}, u32[]{:S(2)}) collective-permute-start(f32[1,4096]{1,0:T(1,128)S(1)} %add.143), channel_id=1, source_target_pairs={{0,16},{2,18},{16,0},{18,2},{1,17},{3,19},{17,1},{19,3},{4,20},{6,... | collective-permute-start | bytes 49160 | tf_op jit(solution)/shard_map/ppermute | solution.py:688
  113.9 5.3 %collective-permute-start.42 = (f32[1,4096]{1,0:T(1,128)S(1)}, f32[1,4096]{1,0:T(1,128)S(1)}, u32[]{:S(2)}, u32[]{:S(2)}) collective-permute-start(f32[1,4096]{1,0:T(1,128)S(1)} %add_add_fusion.5), channel_id=1, source_target_pairs={{0,64},{32,96},{64,0},{96,32},{1,65},{33,97},{65,1},{97,33},{2,66}... | collective-permute-start | bytes 49160 | tf_op jit(solution)/shard_map/ppermute | solution.py:688
  124.0 5.2 %collective-permute-start.45 = (f32[1,2048]{1,0:T(1,128)S(1)}, f32[1,2048]{1,0:T(1,128)S(1)}, u32[]{:S(2)}, u32[]{:S(2)}) collective-permute-start(f32[1,2048]{1,0:T(1,128)S(1)} %col_step.3), channel_id=1, source_target_pairs={{0,8},{4,12},{8,0},{12,4},{1,9},{5,13},{9,1},{13,5},{2,10},{6,14},... | collective-permute-start | bytes 24584 | tf_op jit(solution)/shard_map/ppermute | solution.py:688
  135.8 7.7 %collective-permute-start.49 = (f32[1,4096]{1,0:T(1,128)S(1)}, f32[1,4096]{1,0:T(1,128)S(1)}, u32[]{:S(2)}, u32[]{:S(2)}) collective-permute-start(f32[1,4096]{1,0:T(1,128)S(1)} %add.153), channel_id=1, source_target_pairs={{0,2},{2,0},{16,18},{18,16},{1,3},{3,1},{17,19},{19,17},{4,6},{6,4... | collective-permute-start | bytes 49160 | tf_op jit(solution)/shard_map/ppermute | solution.py:688
  137.9 5.6 %collective-permute-start.48 = (f32[1,4096]{1,0:T(1,128)S(1)}, f32[1,4096]{1,0:T(1,128)S(1)}, u32[]{:S(2)}, u32[]{:S(2)}) collective-permute-start(f32[1,4096]{1,0:T(1,128)S(1)} %add.153), channel_id=1, source_target_pairs={{0,18},{2,16},{16,2},{18,0},{1,19},{3,17},{17,3},{19,1},{4,22},{6,... | collective-permute-start | bytes 49160 | tf_op jit(solution)/shard_map/ppermute | solution.py:688
  143.7 6.1 %collective-permute-start.52 = (f32[1,4096]{1,0:T(1,128)S(1)}, f32[1,4096]{1,0:T(1,128)S(1)}, u32[]{:S(2)}, u32[]{:S(2)}) collective-permute-start(f32[1,4096]{1,0:T(1,128)S(1)} %add_add_fusion.3), channel_id=1, source_target_pairs={{0,64},{32,96},{64,0},{96,32},{1,65},{33,97},{65,1},{97,33},{2,66}... | collective-permute-start | bytes 49160 | tf_op jit(solution)/shard_map/ppermute | solution.py:688
  153.4 5.4 %collective-permute-start.53 = (bf16[16,128,256]{2,1,0:T(8,128)(2,1)S(1)}, bf16[16,128,256]{2,1,0:T(8,128)(2,1)S(1)}, u32[]{:S(2)}, u32[]{:S(2)}) collective-permute-start(bf16[16,128,256]{2,1,0:T(8,128)(2,1)S(1)} %get-tuple-element.346), channel_id=1, source_target_pairs={{0,1},{1,0},{2,3},{3,2},{4,5},{5,4},{6,7},{7,6},{8,9},{9,8},{10,11... | collective-permute-start | bytes 3145736 | tf_op jit(solution)/shard_map/ppermute | solution.py:639
  160.1 21.7 %all-to-all-start = ((bf16[16,128,256]{2,1,0:T(8,128)(2,1)}), bf16[16,128,256]{2,1,0:T(8,128)(2,1)S(1)}, u32[]{:S(2)}, u32[]{:S(2)}) async-start(bf16[16,128,256]{2,1,0:T(8,128)(2,1)} %add_convert_fusion), calls=%async_computation | async-start | bytes 2097152 | tf_op jit(solution)/shard_map/all_to_all | solution.py:647
  165.3 10.8 %collective-permute-start.54 = (bf16[512,256]{1,0:T(8,128)(2,1)S(1)}, bf16[512,256]{1,0:T(8,128)(2,1)S(1)}, u32[]{:S(2)}, u32[]{:S(2)}) collective-permute-start(bf16[512,256]{1,0:T(8,128)(2,1)S(1)} %get-tuple-element.359), channel_id=1, source_target_pairs={{0,8},{4,12},{8,0},{12,4},{1,9},{5,13},{9,1},{13,5},{2,10},{6,14},... | collective-permute-start | bytes 786440 | tf_op jit(solution)/shard_map/ppermute | solution.py:643
  166.8 14.1 %collective-permute-start.55 = (bf16[512,256]{1,0:T(8,128)(2,1)S(1)}, bf16[512,256]{1,0:T(8,128)(2,1)S(1)}, u32[]{:S(2)}, u32[]{:S(2)}) collective-permute-start(bf16[512,256]{1,0:T(8,128)(2,1)S(1)} %get-tuple-element.360), channel_id=1, source_target_pairs={{0,12},{4,8},{8,4},{12,0},{1,13},{5,9},{9,5},{13,1},{2,14},{6,10},... | collective-permute-start | bytes 786440 | tf_op jit(solution)/shard_map/ppermute | solution.py:643
  167.5 13.4 %collective-permute-start.56 = (bf16[512,256]{1,0:T(8,128)(2,1)S(1)}, bf16[512,256]{1,0:T(8,128)(2,1)S(1)}, u32[]{:S(2)}, u32[]{:S(2)}) collective-permute-start(bf16[512,256]{1,0:T(8,128)(2,1)S(1)} %get-tuple-element.361), channel_id=1, source_target_pairs={{0,4},{4,0},{8,12},{12,8},{1,5},{5,1},{9,13},{13,9},{2,6},{6,2},{1... | collective-permute-start | bytes 786440 | tf_op jit(solution)/shard_map/ppermute | solution.py:643
  (27 other events, 91.3 us)
